TPU v7x, 32 devices: a whole 2x2x4 slice. The times are simulated.
32 devices in a mesh: section: 2 (over x), dp: 4 (over z), tensor: 4 (over y, core).
Axes of the slice: x: 2, y: 2, z: 4, core: 2. Of those that a mesh axis runs over, the one named last changes fastest.
Arguments:
- codes: bfloat16 [8, 256, 3, 1024], P('dp', 'tensor'), may hold values from -6 to 6
- cotangent: bfloat16 [8, 256, 3, 1024], P('dp', 'tensor'), may hold values from -6 to 6
- doc_lengths: int32 [8, 4], P('dp'), may hold values from 1 to 240, 256 in all within a row
- w_qkv: bfloat16 [2, 3, 1024, 1024], P('section', None, 'dp', 'tensor'), may hold values from -0.1875 to 0.1875
- w_out: bfloat16 [2, 1024, 1024], P('section', 'tensor', 'dp'), may hold values from -0.5 to 0.5
- w_up: bfloat16 [2, 1024, 4096], P('section', 'dp', 'tensor'), may hold values from -0.1875 to 0.1875
- w_down: bfloat16 [2, 4096, 1024], P('section', 'tensor', 'dp'), may hold values from -0.09375 to 0.09375
- gains: float32 [2, 2, 1024], P('section'), may hold values from 0.1 to 1.9
Outputs:
- results: bfloat16 [2, 8, 256, 3, 1024], P('section', 'dp', 'tensor')
- grad_qkv: float32 [2, 3, 1024, 1024], P('section', None, 'dp', 'tensor')
- grad_out: float32 [2, 1024, 1024], P('section', 'tensor', 'dp')
- grad_up: float32 [2, 1024, 4096], P('section', 'dp', 'tensor')
- grad_down: float32 [2, 4096, 1024], P('section', 'tensor', 'dp')
- grad_gains: float32 [2, 2, 1024], P('section')
Inputs may be any that keep to these rules, and one draw needn't show every extreme that they name: `doc_lengths`: each packed row of 256 frames is cut into 4 documents whose lengths sum to 256; the longest of each row has exactly 240 frames.
All inputs are finite; a program needn't handle non-finite values.
Results may differ from a plain program's by a relative error of at most 0.017.
Values may be sent and summed in bfloat16 or wider, within the bound.
No kernel may reach another device: no remote copies, remote signals or barrier semaphores. Data moves between devices by JAX's collectives and lax.ppermute only.
A program may use at most 128 MiB of HBM per device.

v0:
```python
import jax
import jax.numpy as jnp
from jax import lax
from jax.sharding import PartitionSpec as P

HEAD_DIM = 64


EPS = 1e-05
NEG = -1e30
SCALE = 0.125


def passed_along(value, axis, steps):
    count = lax.axis_size(axis)
    leading, last = (max(0, -steps), min(count, count - steps))
    return lax.ppermute(value, axis, [(source, source + steps) for source in range(leading, last)])


def normed(values, gain):
    inv_root = lax.rsqrt(jnp.mean(values * values, axis=-1, keepdims=True) + EPS)
    return (values * inv_root * gain).astype(jnp.bfloat16)


def norm_back(values, gain, grad):
    inv_root = lax.rsqrt(jnp.mean(values * values, axis=-1, keepdims=True) + EPS)
    unit_rows = values * inv_root
    scaled = grad * gain
    grad_values = inv_root * (
        scaled - unit_rows * jnp.mean(unit_rows * scaled, axis=-1, keepdims=True)
    )
    return (grad_values, jnp.sum(grad * unit_rows, axis=0))


def inner_prod(left, right):
    return lax.dot_general(
        left, right, (((0,), (0,)), ((), ())), preferred_element_type=jnp.float32
    )


def row_gather(values):
    return lax.all_gather(values, "tensor", axis=0, tiled=True)


def row_sum(left, right):
    return lax.psum_scatter(
        jnp.dot(left, right, preferred_element_type=jnp.float32),
        "tensor",
        scatter_dimension=0,
        tiled=True,
    )


def layout_specs(layout):
    if layout == "frames":
        return ("qhd,khd->hqk", "hqk,khd->qhd", "hqk,qhd->khd")
    return ("fqhd,fkhd->fhqk", "fhqk,fkhd->fqhd", "fhqk,fqhd->fkhd")


def split_qkv(projected, layout):
    row_count = projected.shape[0]
    head_count = projected.shape[1] // (3 * HEAD_DIM)
    lead = (row_count,) if layout == "frames" else (row_count // 3, 3)
    split_heads = projected.reshape(lead + (3, head_count, HEAD_DIM))
    return (split_heads[..., 0, :, :], split_heads[..., 1, :, :], split_heads[..., 2, :, :])


def attention_mask(layout, segment, row_count):
    if layout == "frames":
        position = lax.iota(jnp.int32, row_count)
        return ((position[:, None] >= position[None, :]) & (segment[:, None] == segment[None, :]))[
            None
        ]
    token_pos = lax.iota(jnp.int32, 3)
    return (token_pos[:, None] >= token_pos[None, :])[None, None]


def attend(projected, layout, segment):
    queries, key_rows, value_rows = split_qkv(projected, layout)
    specs = layout_specs(layout)
    allowed = attention_mask(layout, segment, projected.shape[0])
    scores = jnp.einsum(specs[0], queries, key_rows, preferred_element_type=jnp.float32) * SCALE
    scores = jnp.where(allowed, scores, NEG)
    row_max = jnp.max(scores, axis=-1, keepdims=True)
    expo_scores = jnp.exp(scores - row_max)
    row_total = jnp.sum(expo_scores, axis=-1, keepdims=True)
    attn_weights = (expo_scores / row_total).astype(jnp.bfloat16)
    mixed_heads = jnp.einsum(specs[1], attn_weights, value_rows, preferred_element_type=jnp.float32)
    log_total = (row_max + jnp.log(row_total))[..., 0]
    return (mixed_heads.reshape(projected.shape[0], -1).astype(jnp.bfloat16), log_total)


def attend_back(projected, grad_mixed, log_total, layout, segment):
    queries, key_rows, value_rows = split_qkv(projected, layout)
    specs = layout_specs(layout)
    allowed = attention_mask(layout, segment, projected.shape[0])
    scores = jnp.einsum(specs[0], queries, key_rows, preferred_element_type=jnp.float32) * SCALE
    scores = jnp.where(allowed, scores, NEG)
    attn_weights = jnp.exp(scores - log_total[..., None])
    grad_heads = grad_mixed.reshape(queries.shape)
    grad_weights = jnp.einsum(specs[0], grad_heads, value_rows, preferred_element_type=jnp.float32)
    centre = jnp.sum(attn_weights * grad_weights, axis=-1, keepdims=True)
    grad_scores = (SCALE * attn_weights * (grad_weights - centre)).astype(jnp.bfloat16)
    grad_queries = jnp.einsum(
        specs[1], grad_scores, key_rows, preferred_element_type=jnp.float32
    ).astype(jnp.bfloat16)
    grad_keys = jnp.einsum(
        specs[2], grad_scores, queries, preferred_element_type=jnp.float32
    ).astype(jnp.bfloat16)
    grad_values = jnp.einsum(
        specs[2], attn_weights.astype(jnp.bfloat16), grad_heads, preferred_element_type=jnp.float32
    ).astype(jnp.bfloat16)
    joined = jnp.stack([grad_queries, grad_keys, grad_values], axis=-3)
    return joined.reshape(projected.shape)


def block_forward(stream, weights, layout, segment):
    w_joined, w_out, w_up, w_down, gain_pair = weights
    normed_in = row_gather(normed(stream, gain_pair[0]))
    projected = jnp.dot(normed_in, w_joined, preferred_element_type=jnp.float32).astype(
        jnp.bfloat16
    )
    mixed_heads, log_total = attend(projected, layout, segment)
    hidden = stream + row_sum(mixed_heads, w_out)
    normed_mid = row_gather(normed(hidden, gain_pair[1]))
    pre_act = jnp.dot(normed_mid, w_up, preferred_element_type=jnp.float32)
    activated = jax.nn.gelu(pre_act).astype(jnp.bfloat16)
    block_out = hidden + row_sum(activated, w_down)
    return (
        block_out,
        (
            stream,
            normed_in,
            projected,
            mixed_heads,
            log_total,
            hidden,
            normed_mid,
            pre_act,
            activated,
        ),
    )


def block_backward(grad_y, state, weights, layout, segment):
    w_joined, w_out, w_up, w_down, gain_pair = weights
    stream, normed_in, projected, mixed_heads, log_total, hidden, normed_mid, pre_act, activated = (
        state
    )
    grad_all = row_gather(grad_y)
    grad_down = inner_prod(activated, grad_all)
    grad_act = jnp.dot(grad_all, w_down.T, preferred_element_type=jnp.float32)
    grad_pre = jax.vjp(jax.nn.gelu, pre_act)[1](grad_act)[0].astype(jnp.bfloat16)
    grad_up = inner_prod(normed_mid, grad_pre)
    grad_mid, gain_mid = norm_back(hidden, gain_pair[1], row_sum(grad_pre, w_up.T))
    grad_hidden = grad_y.astype(jnp.float32) + grad_mid
    branch_all = row_gather(grad_hidden.astype(jnp.bfloat16))
    grad_out_w = inner_prod(mixed_heads, branch_all)
    grad_mixed = jnp.dot(branch_all, w_out.T, preferred_element_type=jnp.float32).astype(
        jnp.bfloat16
    )
    grad_proj = attend_back(projected, grad_mixed, log_total, layout, segment)
    grad_joined = inner_prod(normed_in, grad_proj)
    grad_in, gain_in = norm_back(stream, gain_pair[0], row_sum(grad_proj, w_joined.T))
    model_width = grad_joined.shape[0]
    grad_qkv_w = grad_joined.reshape(model_width, 3, -1).transpose(1, 0, 2)
    return (
        grad_hidden + grad_in,
        (grad_qkv_w, grad_out_w, grad_up, grad_down),
        jnp.stack([gain_in, gain_mid]),
    )


def doc_segments(lengths, frame_count):
    ends = jnp.cumsum(lengths)
    position = lax.iota(jnp.int32, frame_count)
    return jnp.sum((position[:, None] >= ends[None, :]).astype(jnp.int32), axis=1)


def zero_grads(weights):
    w_joined, w_out, w_up, w_down, gain_pair = weights
    model_width = w_joined.shape[0]
    return (
        jnp.zeros((3, model_width, w_joined.shape[1] // 3), jnp.float32),
        jnp.zeros(w_out.shape, jnp.float32),
        jnp.zeros(w_up.shape, jnp.float32),
        jnp.zeros(w_down.shape, jnp.float32),
    )


def only(flag, tree):
    return jax.tree.map(lambda value: jnp.where(flag, value, jnp.zeros_like(value)), tree)


def reduce_sums(grads, gain_grad):
    shards = (
        lax.psum_scatter(
            grads[0].astype(jnp.bfloat16), "dp", scatter_dimension=1, tiled=True
        ).astype(jnp.float32),
        lax.psum_scatter(
            grads[1].astype(jnp.bfloat16), "dp", scatter_dimension=1, tiled=True
        ).astype(jnp.float32),
        lax.psum_scatter(
            grads[2].astype(jnp.bfloat16), "dp", scatter_dimension=0, tiled=True
        ).astype(jnp.float32),
        lax.psum_scatter(
            grads[3].astype(jnp.bfloat16), "dp", scatter_dimension=1, tiled=True
        ).astype(jnp.float32),
    )
    gain_total = lax.psum(gain_grad, ("dp", "tensor"))
    return (shards, gain_total)


def add_tree(left, right):
    return jax.tree.map(lambda one, other: one + other, left, right)


def block_weights(gathered, gain_rows, which):
    qkv_full = gathered[0][which]
    model_width = qkv_full.shape[1]
    return (
        qkv_full.transpose(1, 0, 2).reshape(model_width, 3 * qkv_full.shape[2]),
        gathered[1][which],
        gathered[2][which],
        gathered[3][which],
        gain_rows[which],
    )


def on_device(codes, cotangent, doc_lengths, w_qkv, w_out, w_up, w_down, gains):
    section_index = lax.axis_index("section")
    is_first = section_index == 0
    is_second = section_index == 1
    gathered = (
        lax.all_gather(w_qkv, "dp", axis=2, tiled=True),
        lax.all_gather(w_out, "dp", axis=2, tiled=True),
        lax.all_gather(w_up, "dp", axis=1, tiled=True),
        lax.all_gather(w_down, "dp", axis=2, tiled=True),
    )
    weights = block_weights(gathered, gains, 0)
    model_width = weights[0].shape[0]
    micro_count = codes.shape[0]
    own_frames = codes.shape[1]
    frame_count = own_frames * lax.axis_size("tensor")
    token_shape = codes.shape[1:]
    grad_totals = zero_grads(weights)
    gain_acc = jnp.zeros((2, model_width), jnp.float32)
    shard_totals = (
        jnp.zeros(w_qkv.shape[1:], jnp.float32),
        jnp.zeros(w_out.shape[1:], jnp.float32),
        jnp.zeros(w_up.shape[1:], jnp.float32),
        jnp.zeros(w_down.shape[1:], jnp.float32),
    )
    results = []
    for step in range(micro_count):
        segment = doc_segments(doc_lengths[step], frame_count)
        code_rows = codes[step].astype(jnp.float32)
        frame_in = jnp.sum(code_rows, axis=1)
        frame_out, saved = block_forward(frame_in, weights, "frames", segment)
        sent = only(is_first, frame_out.astype(jnp.bfloat16))
        arrived = passed_along(sent, "section", 1)
        local_in = (code_rows + arrived.astype(jnp.float32)[:, None, :]).reshape(-1, model_width)
        local_out, local_state = block_forward(local_in, weights, "codes", segment)
        grad_in, grads_local, gain_local = block_backward(
            cotangent[step].reshape(-1, model_width), local_state, weights, "codes", segment
        )
        grad_back, local_out, grads_local, gain_local = only(
            is_second,
            (
                grad_in.astype(jnp.bfloat16).reshape(token_shape),
                local_out.astype(jnp.bfloat16).reshape(token_shape),
                grads_local,
                gain_local,
            ),
        )
        returned = passed_along(grad_back, "section", -1)
        returned_f = returned.astype(jnp.float32)
        incoming = jnp.sum(returned_f, axis=1).astype(jnp.bfloat16)
        frame_grad, grads_frame, gain_frame = block_backward(
            incoming, saved, weights, "frames", segment
        )
        code_grad, grads_frame, gain_frame = only(
            is_first,
            ((returned_f + frame_grad[:, None, :]).astype(jnp.bfloat16), grads_frame, gain_frame),
        )
        results.append(code_grad + local_out)
        step_grads = add_tree(grads_local, grads_frame)
        step_gain = gain_local + gain_frame
        grad_totals = add_tree(grad_totals, step_grads)
        gain_acc = gain_acc + step_gain
    shard_totals, gain_totals = reduce_sums(grad_totals, gain_acc)
    return (
        jnp.stack(results)[None],
        shard_totals[0][None],
        shard_totals[1][None],
        shard_totals[2][None],
        shard_totals[3][None],
        gain_totals[None],
    )


def solution(mesh):
    placed = (
        P("dp", "tensor", None, None),
        P("dp", "tensor", None, None),
        P("dp", None),
        P("section", None, "dp", "tensor"),
        P("section", "tensor", "dp"),
        P("section", "dp", "tensor"),
        P("section", "tensor", "dp"),
        P("section", None, None),
    )
    return jax.shard_map(
        on_device,
        mesh=mesh,
        in_specs=placed,
        out_specs=(
            P("section", "dp", "tensor", None, None),
            P("section", None, "dp", "tensor"),
            P("section", "tensor", "dp"),
            P("section", "dp", "tensor"),
            P("section", "tensor", "dp"),
            P("section", None, None),
        ),
        check_vma=False,
    )
```

profile of v0, /device:TPU:0, one launch (start us, length us, event | category | flops | bytes accessed | tf_op | source)
XLA Modules:
  0.0 1172.3 jit_solution(5094853575616067468)
XLA Ops:
  20.6 23.1 %all_gather.62 = bf16[1,256,1024]{2,1,0:T(8,128)(2,1)S(1)} all-gather(bf16[1,256,256]{2,1,0:T(8,128)(2,1)S(1)} %copy-done.77), channel_id=1, replica_groups=mesh['section'=2,'dp'=4,'tensor'=4] {'dp'}, dimensions={2}, use_global_device_ids=true | all-gather | bytes 655360 | tf_op jit(solution)/shard_map/all_gather | solution.py:236
  44.4 16.2 %all-gather.12.cloned.1.call-done = bf16[1,3,1024,256]{2,3,1,0:T(8,128)(2,1)} async-done(((bf16[1,3,256,256]{2,3,1,0:T(8,128)(2,1)}), bf16[1,3,1024,256]{2,3,1,0:T(8,128)(2,1)}) %all-gather.12.cloned.1.call-update) | async-done | bytes 1572880 | tf_op jit(solution)/shard_map/all_gather | solution.py:235
  89.3 27.1 %reduce-scatter.21.cloned.1.call-done = f32[64,1024]{1,0:T(8,128)} async-done(((f32[256,1024]{1,0:T(8,128)}), f32[64,1024]{1,0:T(8,128)}) %reduce-scatter.21.cloned.1.call-update) | async-done | bytes 262160 | tf_op jit(solution)/shard_map/reduce_scatter | solution.py:46
  124.4 39.4 %all-gather.14.cloned.1.call-done = bf16[1,1024,1024]{2,1,0:T(8,128)(2,1)} async-done(((bf16[1,256,1024]{2,1,0:T(8,128)(2,1)}), bf16[1,1024,1024]{2,1,0:T(8,128)(2,1)}) %all-gather.14.cloned.1.call-update) | async-done | bytes 2097168 | tf_op jit(solution)/shard_map/all_gather | solution.py:237
  167.0 43.1 %all-gather.16.cloned.1.call-done = bf16[1,1024,1024]{2,1,0:T(8,128)(2,1)} async-done(((bf16[1,1024,256]{2,1,0:T(8,128)(2,1)}), bf16[1,1024,1024]{2,1,0:T(8,128)(2,1)}) %all-gather.16.cloned.1.call-update) | async-done | bytes 2097168 | tf_op jit(solution)/shard_map/all_gather | solution.py:238
  242.8 22.5 %reduce-scatter.23.cloned.1.call-done = f32[64,1024]{1,0:T(8,128)} async-done(((f32[256,1024]{1,0:T(8,128)}), f32[64,1024]{1,0:T(8,128)}) %reduce-scatter.23.cloned.1.call-update) | async-done | bytes 262160 | tf_op jit(solution)/shard_map/reduce_scatter | solution.py:46
  293.0 18.1 %all-gather.26.cloned.1.call-done = bf16[768,1024]{1,0:T(8,128)(2,1)} async-done(((bf16[192,1024]{1,0:T(8,128)(2,1)}), bf16[768,1024]{1,0:T(8,128)(2,1)}) %all-gather.26.cloned.1.call-update) | async-done | bytes 1572880 | tf_op jit(solution)/shard_map/all_gather | solution.py:42
  361.0 38.0 %reduce-scatter.25.cloned.1.call-done = f32[192,1024]{1,0:T(8,128)} async-done(((f32[768,1024]{1,0:T(8,128)}), f32[192,1024]{1,0:T(8,128)}) %reduce-scatter.25.cloned.1.call-update) | async-done | bytes 786448 | tf_op jit(solution)/shard_map/reduce_scatter | solution.py:46
  426.2 16.4 %all-gather.20.cloned.1.call-done = bf16[768,1024]{1,0:T(8,128)(2,1)} async-done(((bf16[192,1024]{1,0:T(8,128)(2,1)}), bf16[768,1024]{1,0:T(8,128)(2,1)}) %all-gather.20.cloned.1.call-update) | async-done | bytes 1572880 | tf_op jit(solution)/shard_map/all_gather | solution.py:42
  453.7 38.1 %reduce-scatter.27.cloned.1.call-done = f32[192,1024]{1,0:T(8,128)} async-done(((f32[768,1024]{1,0:T(8,128)}), f32[192,1024]{1,0:T(8,128)}) %reduce-scatter.27.cloned.1.call-update) | async-done | bytes 786448 | tf_op jit(solution)/shard_map/reduce_scatter | solution.py:46
  496.7 19.2 %all-gather.24.cloned.1.call-done = bf16[768,1024]{1,0:T(8,128)(2,1)} async-done(((bf16[192,1024]{1,0:T(8,128)(2,1)}), bf16[768,1024]{1,0:T(8,128)(2,1)}) %all-gather.24.cloned.1.call-update) | async-done | bytes 1572880 | tf_op jit(solution)/shard_map/all_gather | solution.py:42
  541.7 38.0 %reduce-scatter.41.cloned.1.call-done = f32[192,1024]{1,0:T(8,128)} async-done(((f32[768,1024]{1,0:T(8,128)}), f32[192,1024]{1,0:T(8,128)}) %reduce-scatter.41.cloned.1.call-update) | async-done | bytes 786448 | tf_op jit(solution)/shard_map/reduce_scatter | solution.py:46
  587.8 15.1 %all-gather.30.cloned.1.call-done = bf16[768,1024]{1,0:T(8,128)(2,1)} async-done(((bf16[192,1024]{1,0:T(8,128)(2,1)}), bf16[768,1024]{1,0:T(8,128)(2,1)}) %all-gather.30.cloned.1.call-update) | async-done | bytes 1572880 | tf_op jit(solution)/shard_map/all_gather | solution.py:42
  607.8 16.3 %all-gather.28.cloned.1.call-done = bf16[768,1024]{1,0:T(8,128)(2,1)} async-done(((bf16[192,1024]{1,0:T(8,128)(2,1)}), bf16[768,1024]{1,0:T(8,128)(2,1)}) %all-gather.28.cloned.1.call-update) | async-done | bytes 1572880 | tf_op jit(solution)/shard_map/all_gather | solution.py:42
  635.3 38.0 %reduce-scatter.43.cloned.1.call-done = f32[192,1024]{1,0:T(8,128)} async-done(((f32[768,1024]{1,0:T(8,128)}), f32[192,1024]{1,0:T(8,128)}) %reduce-scatter.43.cloned.1.call-update) | async-done | bytes 786448 | tf_op jit(solution)/shard_map/reduce_scatter | solution.py:46
  746.1 35.3 %reduce-scatter.45.cloned.1.call-done = f32[192,1024]{1,0:T(8,128)} async-done(((f32[768,1024]{1,0:T(8,128)}), f32[192,1024]{1,0:T(8,128)}) %reduce-scatter.45.cloned.1.call-update) | async-done | bytes 786448 | tf_op jit(solution)/shard_map/reduce_scatter | solution.py:46
  784.4 37.5 %reduce-scatter.35.cloned.1.call-done = f32[192,1024]{1,0:T(8,128)} async-done(((f32[768,1024]{1,0:T(8,128)}), f32[192,1024]{1,0:T(8,128)}) %reduce-scatter.35.cloned.1.call-update) | async-done | bytes 786448 | tf_op jit(solution)/shard_map/reduce_scatter | solution.py:46
  828.5 14.5 %collective-permute-done.1 = bf16[64,3,1024]{2,1,0:T(4,128)(2,1)S(1)} collective-permute-done((bf16[64,3,1024]{2,1,0:T(4,128)(2,1)}, bf16[64,3,1024]{2,1,0:T(4,128)(2,1)S(1)}, u32[]{:S(2)}, u32[]{:S(2)}) %collective-permute-start.1) | collective-permute-done | bytes 393248 | tf_op jit(solution)/shard_map/ppermute | solution.py:17
  863.1 17.8 %reduce-scatter.31.cloned.1.call-done = f32[64,1024]{1,0:T(8,128)} async-done(((f32[256,1024]{1,0:T(8,128)}), f32[64,1024]{1,0:T(8,128)}) %reduce-scatter.31.cloned.1.call-update) | async-done | bytes 262160 | tf_op jit(solution)/shard_map/reduce_scatter | solution.py:46
  896.5 24.8 %reduce-scatter.51.cloned.1.call-done = f32[192,1024]{1,0:T(8,128)} async-done(((f32[768,1024]{1,0:T(8,128)}), f32[192,1024]{1,0:T(8,128)}) %reduce-scatter.51.cloned.1.call-update) | async-done | bytes 786448 | tf_op jit(solution)/shard_map/reduce_scatter | solution.py:46
  1030.0 43.3 %reduce-scatter.57.cloned.1.call-done = bf16[256,1024]{1,0:T(8,128)(2,1)} async-done(((bf16[1024,1024]{1,0:T(8,128)(2,1)}), bf16[256,1024]{1,0:T(8,128)(2,1)}) %reduce-scatter.57.cloned.1.call-update) | async-done | bytes 524304 | tf_op jit(solution)/shard_map/reduce_scatter | solution.py:203
  1076.7 20.0 %reduce-scatter.55.cloned.1.call-done = bf16[256,256]{1,0:T(8,128)(2,1)} async-done(((bf16[256,1024]{1,0:T(8,128)(2,1)}), bf16[256,256]{1,0:T(8,128)(2,1)}) %reduce-scatter.55.cloned.1.call-update) | async-done | bytes 131088 | tf_op jit(solution)/shard_map/reduce_scatter | solution.py:200
  1098.3 24.2 %reduce-scatter.49.cloned.1.call-done = f32[64,1024]{1,0:T(8,128)} async-done(((f32[256,1024]{1,0:T(8,128)}), f32[64,1024]{1,0:T(8,128)}) %reduce-scatter.49.cloned.1.call-update) | async-done | bytes 262160 | tf_op jit(solution)/shard_map/reduce_scatter | solution.py:46
  1127.4 35.9 %psum.7 = f32[1,2,1024]{2,1,0:T(2,128)} all-reduce(f32[1,2,1024]{2,1,0:T(2,128)S(1)} %fusion.150), channel_id=1, replica_groups=mesh['section'=2,'dp'=4,'tensor'=4] {'dp','tensor'}, use_global_device_ids=true, to_apply=%region_64.65 | all-reduce | flops 2048 | bytes 16384 | tf_op jit(solution)/shard_map/psum | solution.py:210
  (543 shorter events, 494.0 us)
Async XLA Ops:
  9.2 78.9 %reduce-scatter.37.cloned.1.call-start = ((), (), s32[]{:S(2)}) async-start(), calls=%async_computation.35 | async-start | bytes 1310720 | tf_op jit(solution)/shard_map/reduce_scatter | solution.py:46
  78.8 84.9 %all-gather.14.cloned.1.call-start = ((), (), s32[]{:S(2)}) async-start(), calls=%async_computation.22 | async-start | bytes 2621440 | tf_op jit(solution)/shard_map/all_gather | solution.py:237
  79.4 130.8 %all-gather.16.cloned.1.call-start = ((), (), s32[]{:S(2)}) async-start(), calls=%async_computation.23 | async-start | bytes 2621440 | tf_op jit(solution)/shard_map/all_gather | solution.py:238
  80.0 157.2 %reduce-scatter.39.cloned.1.call-start = ((), (), s32[]{:S(2)}) async-start(), calls=%async_computation.36 | async-start | bytes 1310720 | tf_op jit(solution)/shard_map/reduce_scatter | solution.py:46
  225.6 85.5 %all-gather.26.cloned.1.call-start = ((), (), s32[]{:S(2)}) async-start(), calls=%async_computation.37 | async-start | bytes 1966080 | tf_op jit(solution)/shard_map/all_gather | solution.py:42
  292.9 106.2 %reduce-scatter.25.cloned.1.call-start = ((), (), s32[]{:S(2)}) async-start(), calls=%async_computation.26 | async-start | bytes 3932160 | tf_op jit(solution)/shard_map/reduce_scatter | solution.py:46
  406.9 84.9 %reduce-scatter.27.cloned.1.call-start = ((), (), s32[]{:S(2)}) async-start(), calls=%async_computation.29 | async-start | bytes 3932160 | tf_op jit(solution)/shard_map/reduce_scatter | solution.py:46
  453.7 62.2 %all-gather.24.cloned.1.call-start = ((), (), s32[]{:S(2)}) async-start(), calls=%async_computation.30 | async-start | bytes 1966080 | tf_op jit(solution)/shard_map/all_gather | solution.py:42
  496.1 83.7 %reduce-scatter.41.cloned.1.call-start = ((), (), s32[]{:S(2)}) async-start(), calls=%async_computation.38 | async-start | bytes 3932160 | tf_op jit(solution)/shard_map/reduce_scatter | solution.py:46
  541.6 61.3 %all-gather.30.cloned.1.call-start = ((), (), s32[]{:S(2)}) async-start(), calls=%async_computation.40 | async-start | bytes 1966080 | tf_op jit(solution)/shard_map/all_gather | solution.py:42
  587.3 86.0 %reduce-scatter.43.cloned.1.call-start = ((), (), s32[]{:S(2)}) async-start(), calls=%async_computation.41 | async-start | bytes 3932160 | tf_op jit(solution)/shard_map/reduce_scatter | solution.py:46
  635.3 68.1 %all-gather.32.cloned.1.call-start = ((), (), s32[]{:S(2)}) async-start(), calls=%async_computation.42 | async-start | bytes 1966080 | tf_op jit(solution)/shard_map/all_gather | solution.py:42
  678.1 68.0 %reduce-scatter.29.cloned.1.call-start = ((), (), s32[]{:S(2)}) async-start(), calls=%async_computation.31 | async-start | bytes 3932160 | tf_op jit(solution)/shard_map/reduce_scatter | solution.py:46
  702.7 78.8 %reduce-scatter.45.cloned.1.call-start = ((), (), s32[]{:S(2)}) async-start(), calls=%async_computation.43 | async-start | bytes 3932160 | tf_op jit(solution)/shard_map/reduce_scatter | solution.py:46
  739.2 82.8 %reduce-scatter.35.cloned.1.call-start = ((), (), s32[]{:S(2)}) async-start(), calls=%async_computation.34 | async-start | bytes 3932160 | tf_op jit(solution)/shard_map/reduce_scatter | solution.py:46
  746.1 134.8 %reduce-scatter.31.cloned.1.call-start = ((), (), s32[]{:S(2)}) async-start(), calls=%async_computation.32 | async-start | bytes 1310720 | tf_op jit(solution)/shard_map/reduce_scatter | solution.py:46
  856.0 65.2 %reduce-scatter.51.cloned.1.call-start = ((), (), s32[]{:S(2)}) async-start(), calls=%async_computation.46 | async-start | bytes 3932160 | tf_op jit(solution)/shard_map/reduce_scatter | solution.py:46
  862.4 121.8 %reduce-scatter.33.cloned.1.call-start = ((), (), s32[]{:S(2)}) async-start(), calls=%async_computation.33 | async-start | bytes 1310720 | tf_op jit(solution)/shard_map/reduce_scatter | solution.py:46
  895.3 90.2 %reduce-scatter.47.cloned.1.call-start = ((), (), s32[]{:S(2)}) async-start(), calls=%async_computation.44 | async-start | bytes 1310720 | tf_op jit(solution)/shard_map/reduce_scatter | solution.py:46
  956.6 71.3 %reduce-scatter.59.cloned.1.call-start = ((), (), s32[]{:S(2)}) async-start(), calls=%async_computation.50 | async-start | bytes 2621440 | tf_op jit(solution)/shard_map/reduce_scatter | solution.py:206
  967.9 105.4 %reduce-scatter.57.cloned.1.call-start = ((), (), s32[]{:S(2)}) async-start(), calls=%async_computation.49 | async-start | bytes 2621440 | tf_op jit(solution)/shard_map/reduce_scatter | solution.py:203
  977.9 118.8 %reduce-scatter.55.cloned.1.call-start = ((), (), s32[]{:S(2)}) async-start(), calls=%async_computation.48 | async-start | bytes 655360 | tf_op jit(solution)/shard_map/reduce_scatter | solution.py:200
  999.8 122.7 %reduce-scatter.49.cloned.1.call-start = ((), (), s32[]{:S(2)}) async-start(), calls=%async_computation.45 | async-start | bytes 1310720 | tf_op jit(solution)/shard_map/reduce_scatter | solution.py:46
  1004.3 159.0 %reduce-scatter.53.cloned.1.call-start = ((), (), s32[]{:S(2)}) async-start(), calls=%async_computation.47 | async-start | bytes 1966080 | tf_op jit(solution)/shard_map/reduce_scatter | solution.py:197
  (135 other events, 2598.0 us)
Sparse Core Ops, SparseCore 0:
  10.2 50.4 all-gather.11
  66.5 21.5 reduce-scatter.36
  91.4 24.8 reduce-scatter.20
  117.8 45.9 all-gather.13
  165.2 44.9 all-gather.15
  214.0 23.1 reduce-scatter.38
  240.4 24.8 reduce-scatter.22
  361.1 37.9 reduce-scatter.24
  453.8 37.9 reduce-scatter.26
  496.2 19.6 all-gather.23
  541.7 37.9 reduce-scatter.40
  635.4 37.9 reduce-scatter.42
  702.8 37.9 reduce-scatter.28
  743.5 37.9 reduce-scatter.44
  784.0 37.8 reduce-scatter.34
  856.2 24.6 reduce-scatter.30
  883.2 38.0 reduce-scatter.50
  924.0 26.8 reduce-scatter.32
  956.8 24.8 reduce-scatter.46
  983.9 43.9 reduce-scatter.58
  1030.2 43.0 reduce-scatter.56
  1075.7 20.9 reduce-scatter.54
  1099.2 23.2 reduce-scatter.48
  1124.8 35.8 reduce-scatter.52
  (7 shorter events, 136.3 us)
where the time goes:
time: 1180 us; the launch traced here: 1170 us
  waiting for transfers between devices  663 us (56%)
  matrix products  175 us (15%)
  blocking collectives  118 us (10%)
  local copies, waits for them, and re-layouts  114 us (10%)
  other arithmetic  72.7 us (6%)
  between operations  16.4 us (1%)
  starting transfers between devices  13.6 us (1%)
    reduce_scatter x16, waiting for transfers between devices, row_sum(): lax.psum_scatter(jnp.dot(left, right, preferred_element_type=jnp.float32)...  361 us
    all_gather x8, waiting for transfers between devices, row_gather(): return lax.all_gather(values, 'tensor', axis=0, tiled=True)  103 us
    all_gather x8, blocking collectives, row_gather(): return lax.all_gather(values, 'tensor', axis=0, tiled=True)  58.7 us
    dot_general x16, matrix products, row_sum(): jnp.dot(left, right, preferred_element_type=jnp.float32)  49.4 us
    reduce_scatter x1, waiting for transfers between devices, reduce_sums(): lax.psum_scatter(grads[2].astype(jnp.bfloat16), 'dp', scatter_dimension=0...  43.3 us
    all_gather x1, waiting for transfers between devices, on_device(): lax.all_gather(w_down, 'dp', axis=2, tiled=True)  43.1 us
    all_gather x1, waiting for transfers between devices, on_device(): lax.all_gather(w_up, 'dp', axis=1, tiled=True)  39.4 us
    dot_general x16, matrix products, inner_prod(): lax.dot_general(left, right, (((0,), (0,)), ((), ())), preferred_element_...  38.4 us
  transfers between devices with their start and end apart: 35, of which 28 were waited for; matrix products, arithmetic and copies ran while one was open for 20% of the time, Pallas kernels for 0%

commit v1 on v0

v1 whole, which is shorter than its diff:
```python
import functools

import jax
import jax.numpy as jnp
from jax import lax
from jax.experimental import pallas as pl
from jax.experimental.pallas import tpu as pltpu
from jax.sharding import PartitionSpec as P

HEAD_DIM = 64
BLK = 256
HEADS = BLK // HEAD_DIM
EPS = 1e-05
NEG = -1e30
SCALE = 0.125
F32 = jnp.float32
BF16 = jnp.bfloat16
VMEM = 48 * 1024 * 1024


def mm(left, right):
    return jnp.dot(left, right, preferred_element_type=F32)


def mm_t(left, right):
    return lax.dot_general(left, right, (((1,), (1,)), ((), ())), preferred_element_type=F32)


def inner(left, right):
    return lax.dot_general(left, right, (((0,), (0,)), ((), ())), preferred_element_type=F32)


def unit_of(values):
    inv_root = lax.rsqrt(jnp.mean(values * values, axis=-1, keepdims=True) + EPS)
    return values * inv_root, inv_root


def normed(values, gain):
    return (unit_of(values)[0] * gain).astype(BF16)


def norm_back(values, gain, grad):
    unit_rows, inv_root = unit_of(values)
    scaled = grad * gain
    back = inv_root * (scaled - unit_rows * jnp.mean(unit_rows * scaled, axis=-1, keepdims=True))
    return back, jnp.sum(grad * unit_rows, axis=0, keepdims=True)


def gelu_pair(pre):
    square = pre * pre
    th = jnp.tanh(0.7978845608028654 * pre * (1.0 + 0.044715 * square))
    half = 0.5 + 0.5 * th
    act = pre * half
    slope = half + act * (1.0 - th) * (0.7978845608028654 + 3 * 0.044715 * 0.7978845608028654 * square)
    return act, slope


def cols(value, index):
    return value[:, index * BLK : (index + 1) * BLK]


def head_masks(shape):
    lane = lax.broadcasted_iota(jnp.int32, shape, 1) // HEAD_DIM
    return [lane == h for h in range(HEADS)]


def spread(value, masks):
    zero = jnp.zeros_like(value)
    return jnp.concatenate([jnp.where(m, value, zero) for m in masks], axis=0)


def gathered(value, masks):
    n = value.shape[0] // HEADS
    out = jnp.where(masks[0], value[:n], 0.0)
    for h in range(1, HEADS):
        out = jnp.where(masks[h], value[h * n : (h + 1) * n], out)
    return out


def head_weights(q4, k, bias):
    s = mm_t(q4, k) * SCALE + jnp.concatenate([bias] * HEADS, axis=0)
    e = jnp.exp(s - jnp.max(s, axis=-1, keepdims=True))
    return e / jnp.sum(e, axis=-1, keepdims=True)


def frames_in_body(order, s_ref, wq_ref, wo_ref, gain_ref, bias_ref, nin_ref, proj_ref, mixed_ref, hid_ref, nmid_ref, held):
    g = pl.program_id(0)
    R, N = bias_ref.shape[:2]

    @pl.when(g == 0)
    def _():
        s = s_ref[...]
        nin_ref[...] = normed(s, gain_ref[0:1])
        hid_ref[...] = s

    for which in range(3):
        acc = mm(nin_ref[:, :BLK], wq_ref[0, 0, which])
        for z in range(1, wq_ref.shape[0]):
            acc += mm(nin_ref[:, z * BLK : (z + 1) * BLK], wq_ref[z, 0, which])
        proj_ref[0, which] = acc.astype(BF16)
    masks = head_masks((N, BLK))
    for r in range(R):
        rows = pl.ds(r * N, N)
        p = head_weights(spread(proj_ref[0, 0, rows], masks), proj_ref[0, 1, rows], bias_ref[r])
        held[rows] = gathered(mm(p.astype(BF16), proj_ref[0, 2, rows]), masks).astype(BF16)
    for z in range(wo_ref.shape[0]):
        hid_ref[:, z * BLK : (z + 1) * BLK] += mm(held[...], wo_ref[z, 0, 0])

    @pl.when(g == 0)
    def _():
        mixed_ref[...] = held[...]

    @pl.when(g == pl.num_programs(0) - 1)
    def _():
        nmid_ref[...] = normed(hid_ref[...], gain_ref[1:2])


def whole(shape):
    return pl.BlockSpec(shape, lambda g, order: (0,) * len(shape))


def call(body, order, inputs, in_specs, outs, out_specs, grid, scratch=(), flops=0, moved=0):
    return pl.pallas_call(
        body,
        out_shape=outs,
        grid_spec=pltpu.PrefetchScalarGridSpec(
            num_scalar_prefetch=1,
            grid=(grid,),
            in_specs=in_specs,
            out_specs=out_specs,
            scratch_shapes=scratch,
        ),
        compiler_params=pltpu.CompilerParams(
            dimension_semantics=("arbitrary",), vmem_limit_bytes=VMEM
        ),
        cost_estimate=pl.CostEstimate(flops=flops, bytes_accessed=moved, transcendentals=0),
    )(order, *inputs)


def struct(shape, dtype):
    return jax.ShapeDtypeStruct(shape, dtype)


def qkv_spec(nz):
    return pl.BlockSpec((nz, 1, 3, BLK, BLK), lambda g, order: (0, order[g], 0, 0, 0))


def out_spec(nz):
    return pl.BlockSpec((nz, 1, 1, BLK, BLK), lambda g, order: (0, order[g], 3, 0, 0))


def mlp_spec(nz, first, per):
    return pl.BlockSpec(
        (nz, 1, 1, BLK, BLK), lambda g, order: (0, order[g // per], first + g % per, 0, 0)
    )


def frames_in(order, s, W, gain, bias):
    rows, D = s.shape
    nz, T = W.shape[:2]
    return call(
        frames_in_body,
        order,
        (s, W, W, gain, bias),
        [whole(s.shape), qkv_spec(nz), out_spec(nz), whole(gain.shape), whole(bias.shape)],
        (
            struct((rows, D), BF16),
            struct((T, 3, rows, BLK), BF16),
            struct((rows, BLK), BF16),
            struct((rows, D), F32),
            struct((rows, D), BF16),
        ),
        (
            whole((rows, D)),
            pl.BlockSpec((1, 3, rows, BLK), lambda g, order: (g, 0, 0, 0)),
            whole((rows, BLK)),
            whole((rows, D)),
            whole((rows, D)),
        ),
        T,
        (pltpu.VMEM((rows, BLK), BF16),),
        flops=2 * rows * D * 4 * D,
        moved=8 * D * D + rows * D * 16,
    )


def own_rows(ref, R, own):
    n = ref.shape[0] // R
    return jnp.concatenate([ref[r * n : r * n + own] for r in range(R)], axis=0)


def frames_mlp_body(R, own, order, nmid_ref, hid_ref, wu_ref, wd_ref, act_ref, slope_ref, out_ref, acc):
    g = pl.program_id(0)
    nz = wu_ref.shape[0]

    @pl.when(g == 0)
    def _():
        acc[...] = own_rows(hid_ref, R, own)

    pre = mm(nmid_ref[:, :BLK], wu_ref[0, 0, 0])
    for z in range(1, nz):
        pre += mm(nmid_ref[:, z * BLK : (z + 1) * BLK], wu_ref[z, 0, 0])
    act, slope = gelu_pair(pre)
    slope_ref[0] = slope.astype(BF16)
    act = act.astype(BF16)

    @pl.when(g < 4)
    def _():
        act_ref[0] = act

    n = act.shape[0] // R
    mine = jnp.concatenate([act[r * n : r * n + own] for r in range(R)], axis=0)
    for z in range(nz):
        acc[:, z * BLK : (z + 1) * BLK] += mm(mine, wd_ref[z, 0, 0])

    @pl.when(g == pl.num_programs(0) - 1)
    def _():
        out_ref[...] = acc[...].astype(BF16)


def frames_mlp(order, nmid, hid, W, R, own):
    rows, D = hid.shape
    nz, T = W.shape[:2]
    per = 4
    return call(
        functools.partial(frames_mlp_body, R, own),
        order,
        (nmid, hid, W, W),
        [whole(nmid.shape), whole(hid.shape), mlp_spec(nz, 4, per), mlp_spec(nz, 8, per)],
        (
            struct((per, rows, BLK), BF16),
            struct((T * per, rows, BLK), BF16),
            struct((R * own, D), BF16),
        ),
        (
            pl.BlockSpec((1, rows, BLK), lambda g, order: (jnp.minimum(g, per - 1), 0, 0)),
            pl.BlockSpec((1, rows, BLK), lambda g, order: (g, 0, 0)),
            whole((R * own, D)),
        ),
        T * per,
        (pltpu.VMEM((R * own, D), F32),),
        flops=2 * (rows + R * own) * D * 4 * D,
        moved=16 * D * D + rows * D * 14,
    )


def frames_mlp_back_body(R, own, order, gy_ref, hid_ref, slope_ref, wu_ref, wd_ref, gain_ref, gpre_ref, ghid_ref, branch_ref, gg_ref, acc):
    g = pl.program_id(0)
    nz = wu_ref.shape[0]
    gact = mm_t(gy_ref[:, :BLK], wd_ref[0, 0, 0])
    for z in range(1, nz):
        gact += mm_t(gy_ref[:, z * BLK : (z + 1) * BLK], wd_ref[z, 0, 0])
    gpre = (gact * slope_ref[0].astype(F32)).astype(BF16)

    @pl.when(g < 4)
    def _():
        gpre_ref[0] = gpre

    for z in range(nz):
        part = mm_t(gpre, wu_ref[z, 0, 0])
        at = slice(z * BLK, (z + 1) * BLK)

        @pl.when(g == 0)
        def _():
            acc[:, at] = part

        @pl.when(g > 0)
        def _():
            acc[:, at] += part

    @pl.when(g == pl.num_programs(0) - 1)
    def _():
        back, _ = norm_back(hid_ref[...], gain_ref[1:2], acc[...])
        ghid = gy_ref[...].astype(F32) + back
        branch_ref[...] = ghid.astype(BF16)
        acc_own = own_rows(acc, R, own)
        hid_own = own_rows(hid_ref, R, own)
        back_own, gg = norm_back(hid_own, gain_ref[1:2], acc_own)
        gg_ref[...] = gg
        ghid_ref[...] = own_rows(gy_ref, R, own).astype(F32) + back_own


def frames_mlp_back(order, gy, hid, slope, W, gain, R, own):
    rows, D = hid.shape
    nz, T = W.shape[:2]
    per = 4
    return call(
        functools.partial(frames_mlp_back_body, R, own),
        order,
        (gy, hid, slope, W, W, gain),
        [
            whole(gy.shape),
            whole(hid.shape),
            pl.BlockSpec((1, rows, BLK), lambda g, order: (g, 0, 0)),
            mlp_spec(nz, 4, per),
            mlp_spec(nz, 8, per),
            whole(gain.shape),
        ],
        (
            struct((per, rows, BLK), BF16),
            struct((R * own, D), F32),
            struct((rows, D), BF16),
            struct((1, D), F32),
        ),
        (
            pl.BlockSpec((1, rows, BLK), lambda g, order: (jnp.minimum(g, per - 1), 0, 0)),
            whole((R * own, D)),
            whole((rows, D)),
            whole((1, D)),
        ),
        T * per,
        (pltpu.VMEM((rows, D), F32),),
        flops=4 * rows * D * 4 * D,
        moved=16 * D * D + rows * D * 14,
    )


def frames_back_body(own, order, branch_ref, proj_ref, wq_ref, wo_ref, bias_ref, s_ref, ghid_ref, glocal_ref, gain_ref, gproj_ref, grad_ref, gg_ref, held, acc):
    g = pl.program_id(0)
    R, N = bias_ref.shape[:2]
    nz = wq_ref.shape[0]
    gmix = mm_t(branch_ref[:, :BLK], wo_ref[0, 0, 0])
    for z in range(1, nz):
        gmix += mm_t(branch_ref[:, z * BLK : (z + 1) * BLK], wo_ref[z, 0, 0])
    gmix = gmix.astype(BF16)
    masks = head_masks((N, BLK))
    for r in range(R):
        rows = pl.ds(r * N, N)
        q, k, v = (proj_ref[0, i, rows] for i in range(3))
        q4 = spread(q, masks)
        p = head_weights(q4, k, bias_ref[r])
        gm4 = spread(gmix[r * N : (r + 1) * N], masks)
        ga = mm_t(gm4, v)
        gs = (SCALE * p * (ga - jnp.sum(p * ga, axis=-1, keepdims=True))).astype(BF16)
        held[0, rows] = gathered(mm(gs, k), masks).astype(BF16)
        held[1, rows] = inner(gs, q4).astype(BF16)
        held[2, rows] = inner(p.astype(BF16), gm4).astype(BF16)

    @pl.when(g == 0)
    def _():
        gproj_ref[...] = held[...]
        acc[...] = jnp.zeros_like(acc)

    for which in range(3):
        mine = jnp.concatenate([held[which, r * N : r * N + own] for r in range(R)], axis=0)
        for z in range(nz):
            acc[:, z * BLK : (z + 1) * BLK] += mm_t(mine, wq_ref[z, 0, which])

    @pl.when(g == pl.num_programs(0) - 1)
    def _():
        back, gg = norm_back(own_rows(s_ref, R, own), gain_ref[0:1], acc[...])
        gg_ref[...] = gg
        frame = ghid_ref[...] + back
        for c in range(glocal_ref.shape[0]):
            grad_ref[c] = (glocal_ref[c].astype(F32) + frame).astype(BF16)


def frames_back(order, branch, proj, W, bias, s, ghid, glocal, gain, own):
    rows, D = branch.shape
    nz, T = W.shape[:2]
    R = bias.shape[0]
    return call(
        functools.partial(frames_back_body, own),
        order,
        (branch, proj, W, W, bias, s, ghid, glocal, gain),
        [
            whole(branch.shape),
            pl.BlockSpec((1, 3, rows, BLK), lambda g, order: (g, 0, 0, 0)),
            qkv_spec(nz),
            out_spec(nz),
            whole(bias.shape),
            whole(s.shape),
            whole(ghid.shape),
            whole(glocal.shape),
            whole(gain.shape),
        ],
        (struct((3, rows, BLK), BF16), struct(glocal.shape, BF16), struct((1, D), F32)),
        (whole((3, rows, BLK)), whole(glocal.shape), whole((1, D))),
        T,
        (pltpu.VMEM((3, rows, BLK), BF16), pltpu.VMEM((R * own, D), F32)),
        flops=2 * rows * D * 4 * D,
        moved=8 * D * D + rows * D * 16,
    )


def head_sum(prods):
    row = lax.broadcasted_iota(jnp.int32, (BLK, BLK), 0) // HEAD_DIM
    col = lax.broadcasted_iota(jnp.int32, (BLK, BLK), 1) // HEAD_DIM
    ones = jnp.where(row == col, 1.0, 0.0).astype(BF16)
    high = prods.astype(BF16)
    low = (prods - high.astype(F32)).astype(BF16)
    return mm(high, ones) + mm(low, ones)


def token_pairs(count):
    return [(a, b) for a in range(count) for b in range(a + 1)]


def token_weights(q, k, count):
    pairs = token_pairs(count)
    m = q[0].shape[0]
    s = head_sum(jnp.concatenate([q[a] * k[b] for a, b in pairs], axis=0)) * SCALE
    s = {pair: s[i * m : (i + 1) * m] for i, pair in enumerate(pairs)}
    out = {}
    for a in range(count):
        top = s[a, 0]
        for b in range(1, a + 1):
            top = jnp.maximum(top, s[a, b])
        e = [jnp.exp(s[a, b] - top) for b in range(a + 1)]
        total = e[0]
        for b in range(1, a + 1):
            total = total + e[b]
        for b in range(a + 1):
            out[a, b] = e[b] / total
    return out


def split_tokens(value, count):
    m = value.shape[0] // count
    return [value[i * m : (i + 1) * m].astype(F32) for i in range(count)]


def codes_in_body(order, codes_ref, sent_ref, wq_ref, wo_ref, gain_ref, nin_ref, proj_ref, keep_ref, send_ref, hid_ref, nmid_ref):
    g = pl.program_id(0)
    C, m, _ = codes_ref.shape
    nz = wq_ref.shape[0]

    @pl.when(g == 0)
    def _():
        for c in range(C):
            s = codes_ref[c].astype(F32) + sent_ref[...].astype(F32)
            rows = pl.ds(c * m, m)
            nin_ref[rows] = normed(s, gain_ref[0:1])
            hid_ref[rows] = s

    part = []
    for which in range(3):
        acc = mm(nin_ref[:, :BLK], wq_ref[0, 0, which])
        for z in range(1, nz):
            acc += mm(nin_ref[:, z * BLK : (z + 1) * BLK], wq_ref[z, 0, which])
        acc = acc.astype(BF16)
        proj_ref[0, which] = acc
        part.append(split_tokens(acc, C))
    q, k, v = part
    p = token_weights(q, k, C)
    mixed = []
    for a in range(C):
        total = p[a, 0].astype(BF16).astype(F32) * v[0]
        for b in range(1, a + 1):
            total += p[a, b].astype(BF16).astype(F32) * v[b]
        mixed.append(total)
    mixed = jnp.concatenate(mixed, axis=0).astype(BF16)

    @pl.when(g < 2)
    def _():
        keep_ref[0] = mixed

    @pl.when(g >= 2)
    def _():
        send_ref[0] = mixed

    for z in range(nz):
        hid_ref[:, z * BLK : (z + 1) * BLK] += mm(mixed, wo_ref[z, 0, 0])

    @pl.when(g == pl.num_programs(0) - 1)
    def _():
        nmid_ref[...] = normed(hid_ref[...], gain_ref[1:2])


def kept(shape, half):
    return pl.BlockSpec(
        (1,) + shape, lambda g, order: (jnp.minimum(g, half - 1),) + (0,) * len(shape)
    )


def given(shape, half):
    return pl.BlockSpec(
        (1,) + shape, lambda g, order: (jnp.maximum(g - half, 0),) + (0,) * len(shape)
    )


def codes_in(order, codes, sent, W, gain):
    C, m, D = codes.shape
    rows = C * m
    nz, T = W.shape[:2]
    return call(
        codes_in_body,
        order,
        (codes, sent, W, W, gain),
        [whole(codes.shape), whole(sent.shape), qkv_spec(nz), out_spec(nz), whole(gain.shape)],
        (
            struct((rows, D), BF16),
            struct((T, 3, rows, BLK), BF16),
            struct((T // 2, rows, BLK), BF16),
            struct((T // 2, rows, BLK), BF16),
            struct((rows, D), F32),
            struct((rows, D), BF16),
        ),
        (
            whole((rows, D)),
            pl.BlockSpec((1, 3, rows, BLK), lambda g, order: (g, 0, 0, 0)),
            kept((rows, BLK), 2),
            given((rows, BLK), 2),
            whole((rows, D)),
            whole((rows, D)),
        ),
        T,
        flops=2 * rows * D * 4 * D,
        moved=8 * D * D + rows * D * 16,
    )


def codes_gact_body(order, cot_ref, wd_ref, gact_ref):
    gact = mm_t(cot_ref[:, :BLK], wd_ref[0, 0, 0])
    for z in range(1, wd_ref.shape[0]):
        gact += mm_t(cot_ref[:, z * BLK : (z + 1) * BLK], wd_ref[z, 0, 0])
    gact_ref[0] = gact.astype(BF16)


def codes_gact(order, cot, W):
    rows, D = cot.shape
    nz, T = W.shape[:2]
    per = 4
    return call(
        codes_gact_body,
        order,
        (cot, W),
        [whole(cot.shape), mlp_spec(nz, 8, per)],
        struct((T * per, rows, BLK), BF16),
        pl.BlockSpec((1, rows, BLK), lambda g, order: (g, 0, 0)),
        T * per,
        flops=2 * rows * D * 4 * D,
        moved=8 * D * D + rows * D * 10,
    )


def codes_mlp_body(order, nmid_ref, hid_ref, cot_ref, gact_ref, wu_ref, gain_ref, akeep_ref, asend_ref, gkeep_ref, gsend_ref, ghid_ref, branch_ref, gg_ref, acc):
    g = pl.program_id(0)
    half = pl.num_programs(0) // 2
    nz = wu_ref.shape[0]
    pre = mm(nmid_ref[:, :BLK], wu_ref[0, 0, 0])
    for z in range(1, nz):
        pre += mm(nmid_ref[:, z * BLK : (z + 1) * BLK], wu_ref[z, 0, 0])
    act, slope = gelu_pair(pre)
    act = act.astype(BF16)
    gpre = (gact_ref[0].astype(F32) * slope).astype(BF16)

    @pl.when(g < half)
    def _():
        akeep_ref[0] = act
        gkeep_ref[0] = gpre

    @pl.when(g >= half)
    def _():
        asend_ref[0] = act
        gsend_ref[0] = gpre

    for z in range(nz):
        part = mm_t(gpre, wu_ref[z, 0, 0])
        at = slice(z * BLK, (z + 1) * BLK)

        @pl.when(g == 0)
        def _():
            acc[:, at] = part

        @pl.when(g > 0)
        def _():
            acc[:, at] += part

    @pl.when(g == pl.num_programs(0) - 1)
    def _():
        back, gg = norm_back(hid_ref[...], gain_ref[1:2], acc[...])
        gg_ref[...] = gg
        ghid = cot_ref[...].astype(F32) + back
        ghid_ref[...] = ghid
        branch_ref[...] = ghid.astype(BF16)


def codes_mlp(order, nmid, hid, cot, gact, W, gain):
    rows, D = hid.shape
    nz, T = W.shape[:2]
    per = 4
    half = T * per // 2
    blocks = struct((half, rows, BLK), BF16)
    return call(
        codes_mlp_body,
        order,
        (nmid, hid, cot, gact, W, gain),
        [
            whole(nmid.shape),
            whole(hid.shape),
            whole(cot.shape),
            pl.BlockSpec((1, rows, BLK), lambda g, order: (g, 0, 0)),
            mlp_spec(nz, 4, per),
            whole(gain.shape),
        ],
        (
            blocks,
            blocks,
            blocks,
            blocks,
            struct((rows, D), F32),
            struct((rows, D), BF16),
            struct((1, D), F32),
        ),
        (
            kept((rows, BLK), half),
            given((rows, BLK), half),
            kept((rows, BLK), half),
            given((rows, BLK), half),
            whole((rows, D)),
            whole((rows, D)),
            whole((1, D)),
        ),
        T * per,
        (pltpu.VMEM((rows, D), F32),),
        flops=4 * rows * D * 4 * D,
        moved=8 * D * D + rows * D * 30,
    )


def codes_back_body(order, branch_ref, proj_ref, wq_ref, wo_ref, codes_ref, sent_ref, ghid_ref, gain_ref, keep_ref, send_ref, glocal_ref, gsent_ref, gg_ref, acc):
    g = pl.program_id(0)
    C, m, _ = codes_ref.shape
    nz = wq_ref.shape[0]
    gmix = mm_t(branch_ref[:, :BLK], wo_ref[0, 0, 0])
    for z in range(1, nz):
        gmix += mm_t(branch_ref[:, z * BLK : (z + 1) * BLK], wo_ref[z, 0, 0])
    gm = split_tokens(gmix.astype(BF16), C)
    q, k, v = (split_tokens(proj_ref[0, i], C) for i in range(3))
    p = token_weights(q, k, C)
    pairs = token_pairs(C)
    ga = head_sum(jnp.concatenate([gm[a] * v[b] for a, b in pairs], axis=0))
    ga = {pair: ga[i * m : (i + 1) * m] for i, pair in enumerate(pairs)}
    gq, gk, gv = [], [None] * C, [None] * C

    def add(left, right):
        return right if left is None else left + right

    for a in range(C):
        centre = p[a, 0] * ga[a, 0]
        for b in range(1, a + 1):
            centre += p[a, b] * ga[a, b]
        total = None
        for b in range(a + 1):
            gs = (SCALE * p[a, b] * (ga[a, b] - centre)).astype(BF16).astype(F32)
            total = add(total, gs * k[b])
            gk[b] = add(gk[b], gs * q[a])
            gv[b] = add(gv[b], p[a, b].astype(BF16).astype(F32) * gm[a])
        gq.append(total)
    joined = [jnp.concatenate(part, axis=0).astype(BF16) for part in (gq, gk, gv)]

    @pl.when(g < 2)
    def _():
        for which in range(3):
            keep_ref[0, which] = joined[which]

    @pl.when(g >= 2)
    def _():
        for which in range(3):
            send_ref[0, which] = joined[which]

    for z in range(nz):
        part = mm_t(joined[0], wq_ref[z, 0, 0])
        for which in range(1, 3):
            part += mm_t(joined[which], wq_ref[z, 0, which])
        at = slice(z * BLK, (z + 1) * BLK)

        @pl.when(g == 0)
        def _():
            acc[:, at] = part

        @pl.when(g > 0)
        def _():
            acc[:, at] += part

    @pl.when(g == pl.num_programs(0) - 1)
    def _():
        total = None
        gains = None
        for c in range(C):
            rows = slice(c * m, (c + 1) * m)
            s = codes_ref[c].astype(F32) + sent_ref[...].astype(F32)
            back, gg = norm_back(s, gain_ref[0:1], acc[rows])
            gains = add(gains, gg)
            local = (ghid_ref[rows] + back).astype(BF16)
            glocal_ref[c] = local
            total = add(total, local.astype(F32))
        gsent_ref[...] = total.astype(BF16)
        gg_ref[...] = gains


def codes_back(order, branch, proj, W, codes, sent, ghid, gain):
    rows, D = branch.shape
    C, m, _ = codes.shape
    nz, T = W.shape[:2]
    blocks = struct((T // 2, 3, rows, BLK), BF16)
    return call(
        codes_back_body,
        order,
        (branch, proj, W, W, codes, sent, ghid, gain),
        [
            whole(branch.shape),
            pl.BlockSpec((1, 3, rows, BLK), lambda g, order: (g, 0, 0, 0)),
            qkv_spec(nz),
            out_spec(nz),
            whole(codes.shape),
            whole(sent.shape),
            whole(ghid.shape),
            whole(gain.shape),
        ],
        (blocks, blocks, struct(codes.shape, BF16), struct((m, D), BF16), struct((1, D), F32)),
        (
            kept((3, rows, BLK), 2),
            given((3, rows, BLK), 2),
            whole(codes.shape),
            whole((m, D)),
            whole((1, D)),
        ),
        T,
        (pltpu.VMEM((rows, D), F32),),
        flops=2 * rows * D * 4 * D,
        moved=8 * D * D + rows * D * 20,
    )


def codes_out_body(order, hid_ref, keep_ref, send_ref, wd_ref, out_ref, acc):
    g = pl.program_id(0)
    half = pl.num_programs(0) // 2
    C, m, _ = out_ref.shape

    @pl.when(g == 0)
    def _():
        acc[...] = hid_ref[...]

    act = jnp.where(g < half, keep_ref[0], send_ref[0])
    for z in range(wd_ref.shape[0]):
        acc[:, z * BLK : (z + 1) * BLK] += mm(act, wd_ref[z, 0, 0])

    @pl.when(g == pl.num_programs(0) - 1)
    def _():
        for c in range(C):
            out_ref[c] = acc[c * m : (c + 1) * m].astype(BF16)


def codes_out(order, hid, keep, send, W, C):
    rows, D = hid.shape
    nz, T = W.shape[:2]
    per = 4
    half = T * per // 2
    m = rows // C
    return call(
        codes_out_body,
        order,
        (hid, keep, send, W),
        [whole(hid.shape), kept((rows, BLK), half), given((rows, BLK), half), mlp_spec(nz, 8, per)],
        struct((C, m, D), BF16),
        whole((C, m, D)),
        T * per,
        (pltpu.VMEM((rows, D), F32),),
        flops=2 * rows * D * 4 * D,
        moved=8 * D * D + rows * D * 14,
    )


def pair_rows(wide, narrow):
    return inner(wide, narrow)


def put(ref, value, by_rows):
    for z in range(ref.shape[0]):
        at = slice(z * BLK, (z + 1) * BLK)
        ref[z, 0] = (value[at] if by_rows else value[:, at]).astype(BF16)


def got(ref, by_rows):
    parts = [ref[z, 0].astype(F32) for z in range(ref.shape[0])]
    return jnp.concatenate(parts, axis=0 if by_rows else 1)


def far_body(split, flag, wide_a, wide_b, row_a, col_a, swide_a, swide_b, row_b, col_b, out_ref):
    g = pl.program_id(0)

    @pl.when((flag[0] == 0) & (g < split))
    def _():
        put(out_ref, inner(wide_a[...], row_a[0]) + inner(swide_a[...], row_b[0]), True)

    @pl.when((flag[0] == 0) & (g >= split))
    def _():
        put(out_ref, inner(col_a[0], wide_b[...]) + inner(col_b[0], swide_b[...]), False)


def last_body(split, flag, w0a, w0b, row_0, col_0, wide_a, wide_b, row_a, col_a, swide_a, swide_b, row_b, col_b, got_ref, out_ref):
    g = pl.program_id(0)

    @pl.when((flag[0] == 1) & (g < split))
    def _():
        put(out_ref, inner(w0a[...], row_0[0]), True)

    @pl.when((flag[0] == 1) & (g >= split))
    def _():
        put(out_ref, inner(col_0[0], w0b[...]), False)

    @pl.when((flag[0] == 0) & (g < split))
    def _():
        total = inner(wide_a[...], row_a[0]) + inner(swide_a[...], row_b[0])
        put(out_ref, total + got(got_ref, True), True)

    @pl.when((flag[0] == 0) & (g >= split))
    def _():
        total = inner(col_a[0], wide_b[...]) + inner(col_b[0], swide_b[...])
        put(out_ref, total + got(got_ref, False), False)


def part_specs(split, count, base, rows):
    row = pl.BlockSpec((1, rows, BLK), lambda g, f: (base * split + jnp.minimum(g, split - 1), 0, 0))
    ncol = count - split
    col = pl.BlockSpec((1, rows, BLK), lambda g, f: (base * ncol + jnp.maximum(g - split, 0), 0, 0))
    return [row, col]


def grads_far(flag, own, sib, split, count, nz):
    rows, D = own[0].shape
    specs = [whole(own[0].shape), whole(own[1].shape)] + part_specs(split, count, 1, rows)
    return call(
        functools.partial(far_body, split),
        flag,
        own + sib,
        specs + specs,
        struct((nz, count, BLK, BLK), BF16),
        pl.BlockSpec((nz, 1, BLK, BLK), lambda g, f: (0, g, 0, 0)),
        count,
        flops=4 * rows * D * BLK * count,
        moved=rows * D * 16,
    )


def grads_last(flag, first, own, sib, received, split, count, nz):
    rows0 = first[0].shape[0]
    rows, D = own[0].shape
    first_specs = [whole(first[0].shape), whole(first[1].shape)] + part_specs(split, count, 0, rows0)
    specs = [whole(own[0].shape), whole(own[1].shape)] + part_specs(split, count, 0, rows)
    block = pl.BlockSpec((nz, 1, BLK, BLK), lambda g, f: (0, g, 0, 0))
    return call(
        functools.partial(last_body, split),
        flag,
        first + own + sib + (received,),
        first_specs + specs + specs + [block],
        struct((nz, count, BLK, BLK), BF16),
        block,
        count,
        flops=4 * rows * D * BLK * count,
        moved=rows * D * 24,
    )


def swap(value, axis, bit):
    count = lax.axis_size(axis)
    return lax.ppermute(value, axis, [(i, i ^ bit) for i in range(count)])


def swap_in(value, section, bit):
    count = lax.axis_size("tensor")
    pairs = [(section * count + i, section * count + (i ^ bit)) for i in range(count)]
    return lax.ppermute(value, ("section", "tensor"), pairs)


def gather_weights(w_qkv, w_out, w_up, w_down):
    depth = w_qkv.shape[1]
    shards = lax.axis_size("dp")
    slices = lax.axis_size("tensor")
    both = ("dp", "tensor")
    if depth == BLK:
        up_blocks = w_up.reshape(BLK, -1, BLK).transpose(1, 0, 2)
        flat = jnp.concatenate(
            [w_qkv, w_out[None], up_blocks, w_down.reshape(-1, BLK, BLK)], axis=0
        )
        out = lax.all_gather(flat, both)
        return out.reshape(shards, slices, *flat.shape)
    per = BLK // depth
    nz = shards // per

    def by_rows(value):
        out = lax.all_gather(value, both).reshape(nz, per, slices, value.shape[0], depth, BLK)
        return out.transpose(0, 2, 3, 1, 4, 5).reshape(nz, slices, -1, BLK, BLK)

    def by_cols(value):
        out = lax.all_gather(value, both)
        out = out.reshape(nz, per, slices, value.shape[0] // BLK, BLK, depth)
        return out.transpose(0, 2, 3, 4, 1, 5).reshape(nz, slices, -1, BLK, BLK)

    up_blocks = w_up.reshape(depth, -1, BLK).transpose(1, 0, 2)
    return jnp.concatenate(
        [by_rows(w_qkv), by_cols(w_out), by_rows(up_blocks), by_cols(w_down)], axis=2
    )


def scatter_blocks(parts, split):
    shards = lax.axis_size("dp")
    nz, count = parts.shape[:2]
    per = shards // nz
    if per == 1:
        out = lax.psum_scatter(parts, "dp", scatter_dimension=0, tiled=False)
        return out[:split], out[split:]
    depth = BLK // per
    rows = parts[:, :split].reshape(nz, split, per, depth, BLK)
    rows = rows.transpose(0, 2, 1, 3, 4).reshape(shards, -1, BLK)
    columns = parts[:, split:].reshape(nz, count - split, BLK, per, depth)
    columns = columns.transpose(0, 3, 1, 2, 4).reshape(shards, -1, BLK)
    out = lax.psum_scatter(
        jnp.concatenate([rows, columns], axis=1), "dp", scatter_dimension=0, tiled=False
    )
    cut = split * depth
    return out[:cut].reshape(split, depth, BLK), out[cut:].reshape(-1, BLK, depth)


def on_device(codes, cotangent, doc_lengths, w_qkv, w_out, w_up, w_down, gains):
    is_first = lax.axis_index("section") == 0
    flag = is_first.astype(jnp.int32).reshape(1)
    t = lax.axis_index("tensor")
    T = lax.axis_size("tensor")
    R, F, C, D = codes.shape
    M = R * F
    N = T * F
    gain = gains[0]
    W = gather_weights(w_qkv[0], w_out[0], w_up[0], w_down[0])
    nz = W.shape[0]
    order = t ^ jnp.array([0, 2, 1, 3], jnp.int32)
    codes_t = codes.transpose(2, 0, 1, 3).reshape(C, M, D)
    cot = cotangent.transpose(2, 0, 1, 3).reshape(C * M, D)

    frame_own = jnp.sum(codes_t.astype(F32), axis=0).reshape(R, F, D)
    far = swap(frame_own, "tensor", 2)
    near = swap(jnp.stack([frame_own, far]), "tensor", 1)
    s0 = jnp.stack([frame_own, near[0], far, near[1]], axis=1).reshape(R * N, D)
    place = t ^ lax.iota(jnp.int32, T)
    pos = (place[:, None] * F + lax.iota(jnp.int32, F)[None]).reshape(N)
    ends = jnp.cumsum(doc_lengths, axis=1)
    seg = jnp.sum((pos[None, :, None] >= ends[:, None, :]).astype(jnp.int32), axis=2)
    allowed = (pos[:, None] >= pos[None, :])[None] & (seg[:, :, None] == seg[:, None, :])
    bias = jnp.where(allowed, 0.0, NEG).astype(F32)

    n_in0, proj0, mixed0, hid0, n_mid0 = frames_in(order, s0, W, gain, bias)
    act0, slope0, out0 = frames_mlp(order, n_mid0, hid0, W, R, F)
    sent = lax.ppermute(out0, "section", [(0, 1)])

    gact1 = codes_gact(order, cot, W)
    n_in1, proj1, mixed1, mixed1_s, hid1, n_mid1 = codes_in(order, codes_t, sent, W, gain)
    act1, act1_s, gpre1, gpre1_s, ghid1, branch1, gg_mid1 = codes_mlp(
        order, n_mid1, hid1, cot, gact1, W, gain
    )
    gproj1, gproj1_s, glocal, gsent, gg_in1 = codes_back(
        order, branch1, proj1, W, codes_t, sent, ghid1, gain
    )

    gsent = lax.ppermute(gsent, "section", [(1, 0)])
    glocal = lax.ppermute(glocal, "section", [(1, 0)])
    gfar = swap_in(gsent, 0, 2)
    gnear = swap_in(jnp.stack([gsent, gfar]), 0, 1)
    gy0 = (
        jnp.stack([gsent, gnear[0], gfar, gnear[1]], axis=0)
        .reshape(T, R, F, D)
        .transpose(1, 0, 2, 3)
        .reshape(R * N, D)
    )

    def exchange(value):
        return swap_in(value, 1, 1)

    out1 = codes_out(order, hid1, act1, act1_s, W, C)
    per = act1.shape[0] // 2
    mlp_own = (n_mid1, cot, gpre1, act1)
    mlp_sib = (exchange(n_mid1), exchange(cot), exchange(gpre1_s), exchange(act1_s))
    mlp_got = swap_in(grads_far(flag, mlp_own, mlp_sib, per, 2 * per, nz), 1, 2)
    att_own = (n_in1, branch1, gproj1.reshape(-1, C * M, BLK), mixed1)
    att_sib = (
        exchange(n_in1),
        exchange(branch1),
        exchange(gproj1_s).reshape(-1, C * M, BLK),
        exchange(mixed1_s),
    )
    att_got = swap_in(grads_far(flag, att_own, att_sib, 3, 4, nz), 1, 2)

    gpre0, ghid0, branch0, gg_mid0 = frames_mlp_back(order, gy0, hid0, slope0, W, gain, R, F)
    mlp_total = grads_last(
        flag, (n_mid0, gy0, gpre0, act0), mlp_own, mlp_sib, mlp_got, per, 2 * per, nz
    )
    up_part, down_part = scatter_blocks(mlp_total, per)
    gproj0, code_grad, gg_in0 = frames_back(
        order, branch0, proj0, W, bias, s0, ghid0, glocal, gain, F
    )
    att_total = grads_last(
        flag, (n_in0, branch0, gproj0, mixed0[None]), att_own, att_sib, att_got, 3, 4, nz
    )
    qkv_part, out_part = scatter_blocks(att_total, 3)

    gain_part = jnp.where(
        is_first,
        jnp.concatenate([gg_in0, gg_mid0], axis=0),
        jnp.concatenate([gg_in1, gg_mid1], axis=0),
    )
    grad_gains = lax.psum(gain_part, ("dp", "tensor"))
    result = jnp.where(is_first, code_grad, out1).reshape(C, R, F, D).transpose(1, 2, 0, 3)
    depth = w_up.shape[1]
    return (
        result[None],
        qkv_part.astype(F32)[None],
        out_part.reshape(-1, depth).astype(F32)[None],
        up_part.transpose(1, 0, 2).reshape(depth, -1).astype(F32)[None],
        down_part.reshape(-1, depth).astype(F32)[None],
        grad_gains[None],
    )


def solution(mesh):
    placed = (
        P("dp", "tensor", None, None),
        P("dp", "tensor", None, None),
        P("dp", None),
        P("section", None, "dp", "tensor"),
        P("section", "tensor", "dp"),
        P("section", "dp", "tensor"),
        P("section", "tensor", "dp"),
        P("section", None, None),
    )
    return jax.shard_map(
        on_device,
        mesh=mesh,
        in_specs=placed,
        out_specs=(
            P("section", "dp", "tensor", None, None),
            P("section", None, "dp", "tensor"),
            P("section", "tensor", "dp"),
            P("section", "dp", "tensor"),
            P("section", "tensor", "dp"),
            P("section", None, None),
        ),
        check_vma=False,
    )
```

time: 1180 us -> 571 us (0.48)
  waiting for transfers between devices: 663 us -> 231 us
  Pallas kernels: 0 us -> 212 us
  matrix products: 175 us -> 0 us
  blocking collectives: 118 us -> 36.6 us
  local copies, waits for them, and re-layouts: 114 us -> 33.8 us
  other arithmetic: 72.7 us -> 11.5 us
  starting transfers between devices: 13.6 us -> 28.8 us
    reduce_scatter x20 -> x2, waiting for transfers between devices: 430 us -> 93.4 us  [scatter_blocks(): out = lax.psum_scatter(parts, 'dp', scatter_dimension=0, tiled=False)]
    pallas_call x0 -> x13, Pallas kernels: none -> 212 us  [call(): pl.pallas_call(body, out_shape=outs, grid_spec=pltpu.PrefetchScalarGridSp...]
    dot_general x72 -> x0, matrix products: 175 us -> none  [the longest x16 49.4 us: row_sum(): jnp.dot(left, right, preferred_element_type=jnp.float32)]
    all_gather x11 -> x1, waiting for transfers between devices: 202 us -> 106 us  [gather_weights(): out = lax.all_gather(flat, both)]
    all_gather x9 -> x0, blocking collectives: 81.8 us -> none  [the longest x8 58.7 us: row_gather(): return lax.all_gather(values, 'tensor', axis=0, tiled=True)]
    convert_element_type x16 -> x1, local copies, waits for them, and re-layouts: 26.4 us -> 0.33 us  [on_device(): up_part.transpose(1, 0, 2).reshape(depth, -1).astype(F32)[None]]
    reduce_sum x23 -> x2, other arithmetic: 23.8 us -> 0.22 us  [the longest x1 0.13 us: on_device(): frame_own = jnp.sum(codes_t.astype(F32), axis=0).reshape(R, F, D)]
    reshape x6 -> x1, local copies, waits for them, and re-layouts: 23.7 us -> 0.96 us  [on_device(): jnp.where(is_first, code_grad, out1).reshape(C, R, F, D)]
  transfers between devices with their start and end apart: 35 -> 20, of which waited for: 28 -> 6; matrix products, arithmetic and copies ran while one was open for 20% -> 2% of each run, Pallas kernels for 0% -> 19%
where the time goes in v1:
time: 571 us; the launch traced here: 568 us
  waiting for transfers between devices  231 us (40%)
  Pallas kernels  212 us (37%)
  blocking collectives  36.6 us (6%)
  local copies, waits for them, and re-layouts  33.8 us (6%)
  starting transfers between devices  28.8 us (5%)
  between operations  14.4 us (3%)
  other arithmetic  11.5 us (2%)
    pallas_call x13, Pallas kernels, call(): pl.pallas_call(body, out_shape=outs, grid_spec=pltpu.PrefetchScalarGridSp...  212 us
    all_gather x1, waiting for transfers between devices, gather_weights(): out = lax.all_gather(flat, both)  106 us
    reduce_scatter x2, waiting for transfers between devices, scatter_blocks(): out = lax.psum_scatter(parts, 'dp', scatter_dimension=0, tiled=False)  93.4 us
    psum x1, blocking collectives, on_device(): grad_gains = lax.psum(gain_part, ('dp', 'tensor'))  36.6 us
    unnamed x108, local copies, waits for them, and re-layouts  26 us
    ppermute x2, waiting for transfers between devices, swap(): return lax.ppermute(value, axis, [(i, i ^ bit) for i in range(count)])  19.4 us
    ppermute x12, starting transfers between devices, swap_in(): return lax.ppermute(value, ('section', 'tensor'), pairs)  18.8 us
  transfers between devices with their start and end apart: 20, of which 6 were waited for; matrix products, arithmetic and copies ran while one was open for 2% of the time, Pallas kernels for 19%

profile of v1, /device:TPU:0, one launch (start us, length us, event | category | flops | bytes accessed | tf_op | source)
XLA Modules:
  0.0 568.5 jit_solution(17826984577565473712)
XLA Ops:
  13.1 3.0 collective-permute-start
  16.2 18.5 %collective-permute-done = f32[2,64,1024]{2,1,0:T(8,128)S(1)} collective-permute-done((f32[2,64,1024]{2,1,0:T(8,128)S(1)}, f32[2,64,1024]{2,1,0:T(8,128)S(1)}, u32[]{:S(2)}, u32[]{:S(2)}) %collective-permute-start) | collective-permute-done | bytes 524320 | tf_op jit(solution)/shard_map/ppermute | solution.py:859
  41.5 106.3 %all-gather.3.cloned.1.call-done = bf16[192,256,256]{2,1,0:T(8,128)(2,1)} async-done(((bf16[12,256,256]{2,1,0:T(8,128)(2,1)}), bf16[192,256,256]{2,1,0:T(8,128)(2,1)}) %all-gather.3.cloned.1.call-update) | async-done | bytes 25165840 | tf_op jit(solution)/shard_map/all_gather | solution.py:878
  147.9 14.1 %shard_map.136 = (bf16[512,1024]{1,0:T(8,128)(2,1)S(1)}, bf16[4,3,512,256]{3,2,1,0:T(8,128)(2,1)}, bf16[512,256]{1,0:T(8,128)(2,1)S(1)}, f32[512,1024]{1,0:T(8,128)S(1)}, bf16[512,1024]{1,0:T(8,128)(2,1)S(1)}) custom-call(s32[4]{0:T(128)S(1)} %broadcast_xor_fusion.order, f32[512,1024]{1,0:T(8,128)} %bitcast.105, bf16[4,4,12,256,256]{4,3,2,1,0:T(8,128)(2,1)} %bitcast.90, ...), custom_call_target="tpu_custom_call" | custom-call | flops 4294967296 | bytes 16777216 | tf_op jit(solution)/shard_map/pallas_call | solution.py:123
  162.0 21.4 %shard_map.137 = (bf16[4,512,256]{2,1,0:T(8,128)(2,1)S(1)}, bf16[16,512,256]{2,1,0:T(8,128)(2,1)}, bf16[128,1024]{1,0:T(8,128)(2,1)S(1)}) custom-call(s32[4]{0:T(128)S(1)} %broadcast_xor_fusion.order, bf16[512,1024]{1,0:T(8,128)(2,1)S(1)} %get-tuple-element.39.nmid_ref.w0a, f32[512,1024]{1,0:T(8,128)S(1)} %get-tuple-element.40.hid_ref, ...), custom_call_target="tpu_custom_call" | custom-call | flops 5368709120 | bytes 24117248 | tf_op jit(solution)/shard_map/pallas_call | solution.py:123
  184.5 3.8 collective-permute-start.2
  188.3 13.0 %shard_map.139.gact_ref = bf16[16,384,256]{2,1,0:T(8,128)(2,1)S(1)} custom-call(s32[4]{0:T(128)S(1)} %broadcast_xor_fusion.order, bf16[384,1024]{1,0:T(8,128)(2,1)S(1)} %bitcast.72, bf16[4,4,12,256,256]{4,3,2,1,0:T(8,128)(2,1)} %bitcast.94), custom_call_target="tpu_custom_call" | custom-call | flops 3221225472 | bytes 12320768 | tf_op jit(solution)/shard_map/pallas_call | solution.py:123
  203.0 10.1 %shard_map.138 = (bf16[384,1024]{1,0:T(8,128)(2,1)S(1)}, bf16[4,3,384,256]{3,2,1,0:T(8,128)(2,1)}, bf16[2,384,256]{2,1,0:T(8,128)(2,1)S(1)}, bf16[2,384,256]{2,1...) custom-call(s32[4]{0:T(128)S(1)} %broadcast_xor_fusion.order, ...), custom_call_target="tpu_custom_call" | custom-call | flops 3221225472 | bytes 14680064 | tf_op jit(solution)/shard_map/pallas_call | solution.py:123
  215.1 38.2 %shard_map.140 = (bf16[8,384,256]{2,1,0:T(8,128)(2,1)S(1)}, bf16[8,384,256]{2,1,0:T(8,128)(2,1)}, bf16[8,384,256]{2,1,0:T(8,128)(2,1)}, bf16[8,384,256]{2,1,0:T(...) custom-call(s32[4]{0:T(128)S(1)} %broadcast_xor_fusion.order, ...), custom_call_target="tpu_custom_call" | custom-call | flops 6442450944 | bytes 20185088 | tf_op jit(solution)/shard_map/pallas_call | solution.py:123
  254.4 18.6 %shard_map.141 = (bf16[2,3,384,256]{3,2,1,0:T(8,128)(2,1)S(1)}, bf16[2,3,384,256]{3,2,1,0:T(8,128)(2,1)}, bf16[3,128,1024]{2,1,0:T(8,128)(2,1)S(1)}, bf16[128,1024]{1,0:T(8,128)(2,1)S(1)}, f32[1,1024]{1,0:T(1,128)S(1)}) custom-call(s32[4]{0:T(128)S(1)} %broadcast_xor_fusion.order, bf16[384,1024]{1,0:T(8,128)(2,1)S(1)} %get-tuple-element.44.branch_ref.wide_b, ...), custom_call_target="tpu_custom_call" | custom-call | flops 3221225472 | bytes 16252928 | tf_op jit(solution)/shard_map/pallas_call | solution.py:123
  279.3 7.3 %collective-permute-done.3 = bf16[128,1024]{1,0:T(8,128)(2,1)S(1)} collective-permute-done((bf16[128,1024]{1,0:T(8,128)(2,1)S(1)}, bf16[128,1024]{1,0:T(8,128)(2,1)S(1)}, u32[]{:S(2)}, u32[]{:S(2)}) %collective-permute-start.3) | collective-permute-done | bytes 262176 | tf_op jit(solution)/shard_map/ppermute | solution.py:956
  286.7 3.7 collective-permute-start.4
  291.1 4.9 collective-permute-done.4
  312.0 3.1 shard_map.145
  320.6 40.1 %shard_map.142 = (bf16[4,512,256]{2,1,0:T(8,128)(2,1)S(1)}, f32[128,1024]{1,0:T(8,128)S(1)}, bf16[512,1024]{1,0:T(8,128)(2,1)S(1)}, f32[1,1024]{1,0:T(1,128)S(1)}) custom-call(s32[4]{0:T(128)S(1)} %broadcast_xor_fusion.order, bf16[512,1024]{1,0:T(8,128)(2,1)S(1)} %bitcast.77, f32[512,1024]{1,0:T(8,128)S(1)} %copy-done.4, ...), custom_call_target="tpu_custom_call" | custom-call | flops 8589934592 | bytes 24117248 | tf_op jit(solution)/shard_map/pallas_call | solution.py:123
  360.8 7.7 %shard_map.147 = bf16[4,8,256,256]{3,2,1,0:T(8,128)(2,1)} custom-call(s32[1]{0:T(128)} %bitcast.35.flag, bf16[384,1024]{1,0:T(8,128)(2,1)S(1)} %get-tuple-element.42.nmid_ref.wide_a, bf16[384,1024]{1,0:T(8,128)(2,1)S(1)} %bitcast.75, bf16[8,384,256]{2,1,0:T(8,128)(2,1)S(1)} %copy-done.7, bf16[8,384,256]{2,1,0:T(8,128)(2,1)} %copy-done, ...), custom_call_target="tpu_custom_call" | custom-call | flops 3221225472 | bytes 6291456 | tf_op jit(solution)/shard_map/pallas_call | solution.py:123
  368.5 2.6 collective-permute-start.16
  371.2 16.8 %shard_map.143 = (bf16[3,512,256]{2,1,0:T(8,128)(2,1)S(1)}, bf16[3,128,1024]{2,1,0:T(8,128)(2,1)S(1)}, f32[1,1024]{1,0:T(1,128)S(1)}) custom-call(s32[4]{0:T(128)S(1)} %broadcast_xor_fusion.order, bf16[512,1024]{1,0:T(8,128)(2,1)S(1)} %get-tuple-element.49.branch_ref.w0b, bf16[4,3,512,256]{3,2,1,0:T(8,128)(2,1)} %get-tuple-element.50.proj_ref, ...), custom_call_target="tpu_custom_call" | custom-call | flops 4294967296 | bytes 16777216 | tf_op jit(solution)/shard_map/pallas_call | solution.py:123
  390.2 5.5 shard_map.146
  398.1 9.8 %shard_map.148 = bf16[4,8,256,256]{3,2,1,0:T(8,128)(2,1)} custom-call(s32[1]{0:T(128)} %bitcast.35.flag, bf16[512,1024]{1,0:T(8,128)(2,1)S(1)} %copy-done.14, bf16[512,1024]{1,0:T(8,128)(2,1)S(1)} %bitcast.78, bf16[4,512,256]{2,1,0:T(8,128)(2,1)} %copy-done.33, bf16[4,512,256]{2,1,0:T(8,128)(2,1)} %copy-done.32, ...), custom_call_target="tpu_custom_call" | custom-call | flops 3221225472 | bytes 9437184 | tf_op jit(solution)/shard_map/pallas_call | solution.py:123
  409.8 13.4 %shard_map.144 = bf16[3,128,1024]{2,1,0:T(8,128)(2,1)S(1)} custom-call(s32[4]{0:T(128)S(1)} %broadcast_xor_fusion.order, f32[384,1024]{1,0:T(8,128)S(1)} %copy-done.6, bf16[8,384,256]{2,1,0:T(8,128)(2,1)S(1)} %copy-done.1, bf16[8,384,256]{2,1,0:T(8,128)(2,1)} %get-tuple-element.55.send_ref, bf16[4,4,12,256,256]{4,3,2,1,0:T(8,128)(2,1)} %bitcast.104), custom_call_target="tpu_custom_call" | custom-call | flops 3221225472 | bytes 13893632 | tf_op jit(solution)/shard_map/pallas_call | solution.py:123
  424.4 36.6 %psum.7 = f32[1,2,1024]{2,1,0:T(2,128)} all-reduce(f32[1,2,1024]{2,1,0:T(2,128)S(1)} %fusion.1), channel_id=1, replica_groups=mesh['section'=2,'dp'=4,'tensor'=4] {'dp','tensor'}, use_global_device_ids=true, to_apply=%region_5.6 | all-reduce | flops 2048 | bytes 16384 | tf_op jit(solution)/shard_map/psum | solution.py:1002
  462.6 1.9 slice_convert_fusion
  464.5 93.4 %reduce-scatter.5.cloned.1.call-done = bf16[1,8,256,256]{3,2,1,0:T(8,128)(2,1)} async-done(((bf16[4,8,256,256]{3,2,1,0:T(8,128)(2,1)}), bf16[1,8,256,256]{3,2,1,0:T(8,128)(2,1)}) %reduce-scatter.5.cloned.1.call-update) | async-done | bytes 1048592 | tf_op jit(solution)/shard_map/reduce_scatter | solution.py:903
  (169 shorter events, 60.1 us)
Async XLA Ops:
  7.2 140.7 %all-gather.3.cloned.1.call-start = ((), (), s32[]{:S(2)}) async-start(), calls=%async_computation.4 | async-start | bytes 26738688 | tf_op jit(solution)/shard_map/all_gather | solution.py:878
  11.9 449.1 %reduce-scatter.3.cloned.1.call-start = ((), (), s32[]{:S(2)}) async-start(), calls=%async_computation.2 | async-start | bytes 2621440 | tf_op jit(solution)/shard_map/reduce_scatter | solution.py:903
  13.1 21.5 %collective-permute-start = (f32[2,64,1024]{2,1,0:T(8,128)S(1)}, f32[2,64,1024]{2,1,0:T(8,128)S(1)}, u32[]{:S(2)}, u32[]{:S(2)}) collective-permute-start(f32[2,64,1024]{2,1,0:T(8,128)S(1)} %convert_reduce_fusion), channel_id=1, source_target_pairs={{0,2},{1,3},{2,0},{3,1},{4,6},{5,7},{6,4},{7,5},{8,10},{9,11},{10,... | collective-permute-start | bytes 1572872 | tf_op jit(solution)/shard_map/ppermute | solution.py:859
  35.7 3.0 collective-permute-start.1
  37.7 110.2 %copy-start.8 = (f32[2,256,256]{2,1,0:T(8,128)}, f32[2,256,256]{2,1,0:T(8,128)S(1)}, u32[]{:S(2)}) copy-start(f32[2,256,256]{2,1,0:T(8,128)S(1)} %and_select_fusion.bias_ref) | copy-start | bytes 1572868
  40.0 107.9 %copy-start.38 = (f32[1,2,1024]{2,1,0:T(2,128)S(1)}, f32[1,2,1024]{2,1,0:T(2,128)}, u32[]{:S(2)}) copy-start(f32[1,2,1024]{2,1,0:T(2,128)} %param.16) | copy-start | bytes 24580
  184.5 18.6 %collective-permute-start.2 = (bf16[128,1024]{1,0:T(8,128)(2,1)S(1)}, bf16[128,1024]{1,0:T(8,128)(2,1)S(1)}, u32[]{:S(2)}, u32[]{:S(2)}) collective-permute-start(bf16[128,1024]{1,0:T(8,128)(2,1)S(1)} %get-tuple-element.41), channel_id=1, source_target_pairs={{0,16},{1,17},{2,18},{3,19},{4,20},{5,21},{6,22},{7,23},{8,24},{9,... | collective-permute-start | bytes 786440 | tf_op jit(solution)/shard_map/ppermute | solution.py:945
  215.1 63.6 %copy-start.17 = (bf16[384,1024]{1,0:T(8,128)(2,1)}, bf16[384,1024]{1,0:T(8,128)(2,1)S(1)}, u32[]{:S(2)}) copy-start(bf16[384,1024]{1,0:T(8,128)(2,1)S(1)} %get-tuple-element.59.wide_a) | copy-start | bytes 2359300
  274.9 31.6 %collective-permute-start.9 = (bf16[2,3,384,256]{3,2,1,0:T(8,128)(2,1)}, bf16[2,3,384,256]{3,2,1,0:T(8,128)(2,1)}, u32[]{:S(2)}, u32[]{:S(2)}) collective-permute-start(bf16[2,3,384,256]{3,2,1,0:T(8,128)(2,1)} %get-tuple-element.62), channel_id=1, source_target_pairs={{16,17},{17,16},{18,19},{19,18},{20,21},{21,20},{22,23},{23,22},{2... | collective-permute-start | bytes 3538952 | tf_op jit(solution)/shard_map/ppermute | solution.py:865
  276.6 10.1 %collective-permute-start.3 = (bf16[128,1024]{1,0:T(8,128)(2,1)S(1)}, bf16[128,1024]{1,0:T(8,128)(2,1)S(1)}, u32[]{:S(2)}, u32[]{:S(2)}) collective-permute-start(bf16[128,1024]{1,0:T(8,128)(2,1)S(1)} %get-tuple-element.47), channel_id=1, source_target_pairs={{16,0},{17,1},{18,2},{19,3},{20,4},{21,5},{22,6},{23,7},{24,8},{25... | collective-permute-start | bytes 786440 | tf_op jit(solution)/shard_map/ppermute | solution.py:956
  277.9 23.2 %collective-permute-start.8 = (bf16[384,1024]{1,0:T(8,128)(2,1)S(1)}, bf16[384,1024]{1,0:T(8,128)(2,1)S(1)}, u32[]{:S(2)}, u32[]{:S(2)}) collective-permute-start(bf16[384,1024]{1,0:T(8,128)(2,1)S(1)} %get-tuple-element.44.branch_ref.wide_b), channel_id=1, source_target_pairs={{16,17},{17,16},{18,19},{19,18},{20,21},{21,20},{22,23},{23,22},{2... | collective-permute-start | bytes 2359304 | tf_op jit(solution)/shard_map/ppermute | solution.py:865
  278.6 25.2 %collective-permute-start.7 = (bf16[384,1024]{1,0:T(8,128)(2,1)S(1)}, bf16[384,1024]{1,0:T(8,128)(2,1)S(1)}, u32[]{:S(2)}, u32[]{:S(2)}) collective-permute-start(bf16[384,1024]{1,0:T(8,128)(2,1)S(1)} %get-tuple-element.59.wide_a), channel_id=1, source_target_pairs={{16,17},{17,16},{18,19},{19,18},{20,21},{21,20},{22,23},{23,22},{2... | collective-permute-start | bytes 2359304 | tf_op jit(solution)/shard_map/ppermute | solution.py:865
  286.7 9.3 %collective-permute-start.4 = (bf16[128,1024]{1,0:T(8,128)(2,1)S(1)}, bf16[128,1024]{1,0:T(8,128)(2,1)S(1)}, u32[]{:S(2)}, u32[]{:S(2)}) collective-permute-start(bf16[128,1024]{1,0:T(8,128)(2,1)S(1)} %collective-permute-done.3), channel_id=1, source_target_pairs={{0,2},{1,3},{2,0},{3,1},{4,6},{5,7},{6,4},{7,5},{8,10},{9,11},{10,... | collective-permute-start | bytes 786440 | tf_op jit(solution)/shard_map/ppermute | solution.py:865
  290.4 8.4 %collective-permute-start.10 = (bf16[2,384,256]{2,1,0:T(8,128)(2,1)S(1)}, bf16[2,384,256]{2,1,0:T(8,128)(2,1)S(1)}, u32[]{:S(2)}, u32[]{:S(2)}) collective-permute-start(bf16[2,384,256]{2,1,0:T(8,128)(2,1)S(1)} %get-tuple-element.63), channel_id=1, source_target_pairs={{16,17},{17,16},{18,19},{19,18},{20,21},{21,20},{22,23},{23,22},{2... | collective-permute-start | bytes 1179656 | tf_op jit(solution)/shard_map/ppermute | solution.py:865
  296.8 19.3 %collective-permute-start.5 = (bf16[2,128,1024]{2,1,0:T(8,128)(2,1)}, bf16[2,128,1024]{2,1,0:T(8,128)(2,1)}, u32[]{:S(2)}, u32[]{:S(2)}) collective-permute-start(bf16[2,128,1024]{2,1,0:T(8,128)(2,1)} %pad_maximum_fusion.4), channel_id=1, source_target_pairs={{0,1},{1,0},{2,3},{3,2},{4,5},{5,4},{6,7},{7,6},{8,9},{9,8},{10,11... | collective-permute-start | bytes 1572872 | tf_op jit(solution)/shard_map/ppermute | solution.py:865
  299.5 19.5 %collective-permute-start.13 = (bf16[384,1024]{1,0:T(8,128)(2,1)S(1)}, bf16[384,1024]{1,0:T(8,128)(2,1)}, u32[]{:S(2)}, u32[]{:S(2)}) collective-permute-start(bf16[384,1024]{1,0:T(8,128)(2,1)S(1)} %bitcast.74), channel_id=1, source_target_pairs={{16,17},{17,16},{18,19},{19,18},{20,21},{21,20},{22,23},{23,22},{2... | collective-permute-start | bytes 2359304 | tf_op jit(solution)/shard_map/ppermute | solution.py:865
  302.0 58.8 %collective-permute-start.14 = (bf16[8,384,256]{2,1,0:T(8,128)(2,1)}, bf16[8,384,256]{2,1,0:T(8,128)(2,1)}, u32[]{:S(2)}, u32[]{:S(2)}) collective-permute-start(bf16[8,384,256]{2,1,0:T(8,128)(2,1)} %get-tuple-element.67), channel_id=1, source_target_pairs={{16,17},{17,16},{18,19},{19,18},{20,21},{21,20},{22,23},{23,22},{2... | collective-permute-start | bytes 4718600 | tf_op jit(solution)/shard_map/ppermute | solution.py:865
  304.7 56.0 %collective-permute-start.15 = (bf16[8,384,256]{2,1,0:T(8,128)(2,1)}, bf16[8,384,256]{2,1,0:T(8,128)(2,1)}, u32[]{:S(2)}, u32[]{:S(2)}) collective-permute-start(bf16[8,384,256]{2,1,0:T(8,128)(2,1)} %get-tuple-element.55.send_ref), channel_id=1, source_target_pairs={{16,17},{17,16},{18,19},{19,18},{20,21},{21,20},{22,23},{23,22},{2... | collective-permute-start | bytes 4718600 | tf_op jit(solution)/shard_map/ppermute | solution.py:865
  315.2 73.7 %collective-permute-start.11 = (bf16[4,4,256,256]{3,2,1,0:T(8,128)(2,1)}, bf16[4,4,256,256]{3,2,1,0:T(8,128)(2,1)S(1)}, u32[]{:S(2)}, u32[]{:S(2)}) collective-permute-start(bf16[4,4,256,256]{3,2,1,0:T(8,128)(2,1)} %shard_map.145), channel_id=1, source_target_pairs={{16,18},{17,19},{18,16},{19,17},{20,22},{21,23},{22,20},{23,21},{2... | collective-permute-start | bytes 6291464 | tf_op jit(solution)/shard_map/ppermute | solution.py:865
  316.1 44.6 %collective-permute-start.12 = (bf16[384,1024]{1,0:T(8,128)(2,1)S(1)}, bf16[384,1024]{1,0:T(8,128)(2,1)S(1)}, u32[]{:S(2)}, u32[]{:S(2)}) collective-permute-start(bf16[384,1024]{1,0:T(8,128)(2,1)S(1)} %get-tuple-element.42.nmid_ref.wide_a), channel_id=1, source_target_pairs={{16,17},{17,16},{18,19},{19,18},{20,21},{21,20},{22,23},{23,22},{2... | collective-permute-start | bytes 2359304 | tf_op jit(solution)/shard_map/ppermute | solution.py:865
  319.0 52.1 %collective-permute-start.6 = (bf16[3,128,1024]{2,1,0:T(8,128)(2,1)S(1)}, bf16[3,128,1024]{2,1,0:T(8,128)(2,1)S(1)}, u32[]{:S(2)}, u32[]{:S(2)}) collective-permute-start(bf16[3,128,1024]{2,1,0:T(8,128)(2,1)S(1)} %copy-done.42), channel_id=1, source_target_pairs={{16,0},{17,1},{18,2},{19,3},{20,4},{21,5},{22,6},{23,7},{24,8},{25... | collective-permute-start | bytes 2359304 | tf_op jit(solution)/shard_map/ppermute | solution.py:957
  320.5 40.2 %copy-start.7 = (bf16[8,384,256]{2,1,0:T(8,128)(2,1)S(1)}, bf16[8,384,256]{2,1,0:T(8,128)(2,1)}, u32[]{:S(2)}) copy-start(bf16[8,384,256]{2,1,0:T(8,128)(2,1)} %get-tuple-element.66.row_a) | copy-start | bytes 4718596
  368.5 27.6 %collective-permute-start.16 = (bf16[4,8,256,256]{3,2,1,0:T(8,128)(2,1)}, bf16[4,8,256,256]{3,2,1,0:T(8,128)(2,1)}, u32[]{:S(2)}, u32[]{:S(2)}) collective-permute-start(bf16[4,8,256,256]{3,2,1,0:T(8,128)(2,1)} %shard_map.147), channel_id=1, source_target_pairs={{16,18},{17,19},{18,16},{19,17},{20,22},{21,23},{22,20},{23,21},{2... | collective-permute-start | bytes 12582920 | tf_op jit(solution)/shard_map/ppermute | solution.py:865
  395.7 162.2 %reduce-scatter.5.cloned.1.call-start = ((), (), s32[]{:S(2)}) async-start(), calls=%async_computation.3 | async-start | bytes 5242880 | tf_op jit(solution)/shard_map/reduce_scatter | solution.py:903
  (48 other events, 380.9 us)
Sparse Core Ops, SparseCore 0:
  12.0 135.8 all-gather.2
  395.9 50.3 reduce-scatter.2
  448.7 109.1 reduce-scatter.4

commit v2 on v1

v2 whole, which is shorter than its diff:
```python
import functools

import jax
import jax.numpy as jnp
from jax import lax
from jax.experimental import pallas as pl
from jax.experimental.pallas import tpu as pltpu
from jax.sharding import PartitionSpec as P

HEAD_DIM = 64
BLK = 256
HEADS = BLK // HEAD_DIM
EPS = 1e-05
NEG = -1e30
SCALE = 0.125
F32 = jnp.float32
BF16 = jnp.bfloat16
VMEM = 60 * 1024 * 1024
ACTIVE = 4
COST = 8


def mm(left, right):
    return jnp.dot(left, right, preferred_element_type=F32)


def mm_t(left, right):
    return lax.dot_general(left, right, (((1,), (1,)), ((), ())), preferred_element_type=F32)


def inner(left, right):
    return lax.dot_general(left, right, (((0,), (0,)), ((), ())), preferred_element_type=F32)


def unit_of(values):
    inv_root = lax.rsqrt(jnp.mean(values * values, axis=-1, keepdims=True) + EPS)
    return values * inv_root, inv_root


def normed(values, gain):
    return (unit_of(values)[0] * gain).astype(BF16)


def norm_back(values, gain, grad):
    unit_rows, inv_root = unit_of(values)
    scaled = grad * gain
    back = inv_root * (scaled - unit_rows * jnp.mean(unit_rows * scaled, axis=-1, keepdims=True))
    return back, jnp.sum(grad * unit_rows, axis=0, keepdims=True)


def gelu_pair(pre):
    square = pre * pre
    th = jnp.tanh(0.7978845608028654 * pre * (1.0 + 0.044715 * square))
    half = 0.5 + 0.5 * th
    act = pre * half
    slope = half + act * (1.0 - th) * (0.7978845608028654 + 3 * 0.044715 * 0.7978845608028654 * square)
    return act, slope


def head_masks(shape):
    lane = lax.broadcasted_iota(jnp.int32, shape, 1) // HEAD_DIM
    return [lane == h for h in range(HEADS)]


def spread(value, masks):
    zero = jnp.zeros_like(value)
    return jnp.concatenate([jnp.where(m, value, zero) for m in masks], axis=0)


def gathered(value, masks):
    n = value.shape[0] // HEADS
    out = jnp.where(masks[0], value[:n], 0.0)
    for h in range(1, HEADS):
        out = jnp.where(masks[h], value[h * n : (h + 1) * n], out)
    return out


def head_weights(q4, k, bias):
    s = mm_t(q4, k) * SCALE + jnp.concatenate([bias] * HEADS, axis=0)
    e = jnp.exp(s - jnp.max(s, axis=-1, keepdims=True))
    return e / jnp.sum(e, axis=-1, keepdims=True)


def whole(shape):
    return pl.BlockSpec(shape, lambda g, order: (0,) * len(shape))


def struct(shape, dtype):
    return jax.ShapeDtypeStruct(shape, dtype)


def call(body, order, inputs, in_specs, outs, out_specs, grid, scratch=(), flops=0, moved=0):
    def run(flags, *refs):
        if flags.shape[0] <= ACTIVE:
            return body(flags, *refs)

        @pl.when(flags[ACTIVE] == 1)
        def _():
            body(flags, *refs)

    return pl.pallas_call(
        run,
        out_shape=outs,
        grid_spec=pltpu.PrefetchScalarGridSpec(
            num_scalar_prefetch=1,
            grid=(grid,),
            in_specs=in_specs,
            out_specs=out_specs,
            scratch_shapes=scratch,
        ),
        compiler_params=pltpu.CompilerParams(
            dimension_semantics=("arbitrary",), vmem_limit_bytes=VMEM
        ),
        cost_estimate=pl.CostEstimate(
            flops=flops // COST, bytes_accessed=moved // COST, transcendentals=0
        ),
    )(order, *inputs)


def weight_spec(W, third):
    nz = W.shape[0]

    def at(g, order):
        step, which = third(g)
        return (0, order[step] * order[ACTIVE], which * order[ACTIVE], 0, 0)

    return pl.BlockSpec((nz, 1, 4, BLK, BLK), at)


def clip(g, low, high):
    return jnp.minimum(jnp.maximum(g, low), high)


def deep(ref, index):
    return ref[:, 0, index].reshape(-1, BLK)


def store_out(g, first, held, sems, outs):
    for i, out in enumerate(outs):

        @pl.when(g == first + i)
        def _():
            pltpu.make_async_copy(held.at[i], out, sems.at[i]).start()


def stored(held, sems, outs):
    for i, out in enumerate(outs):
        pltpu.make_async_copy(held.at[i], out, sems.at[i]).wait()


HBM_REF = pl.BlockSpec(memory_space=pl.ANY)


def pick(ref, r, R, F):
    return jnp.concatenate(
        [ref[pl.ds(at, F)] for at in range(r * F, ref.shape[0], R * F)], axis=0
    )


def place(ref, r, R, F, value):
    for i, at in enumerate(range(r * F, ref.shape[0], R * F)):
        ref[pl.ds(at, F)] = value[i * F : (i + 1) * F]


def frames_fwd_body(own, order, s_ref, wa_ref, wb_ref, gain_ref, bias_ref, nin_ref, proj_ref, mixed_ref, hid_ref, nmid_ref, act_ref, slope_ref, out_ref, held, acc, acts, sems):
    g = pl.program_id(0)
    T = pl.num_programs(0) // 2
    R, N = bias_ref.shape[:2]
    nz = wa_ref.shape[0]

    @pl.when(g == 0)
    def _():
        s = s_ref[...]
        nin_ref[...] = normed(s, gain_ref[0:1])
        hid_ref[...] = s

    @pl.when(g < T)
    def _():
        for which in range(3):
            proj_ref[0, which] = mm(nin_ref[...], deep(wa_ref, which)).astype(BF16)
        masks = head_masks((N, BLK))
        for r in range(R):
            q, k, v = (pick(proj_ref.at[0, i], r, R, own) for i in range(3))
            p = head_weights(spread(q, masks), k, bias_ref[r])
            place(held, r, R, own, gathered(mm(p.astype(BF16), v), masks).astype(BF16))
        for z in range(nz):
            hid_ref[:, z * BLK : (z + 1) * BLK] += mm(held[...], wa_ref[z, 0, 3])

    @pl.when(g == 0)
    def _():
        mixed_ref[...] = held[...]

    @pl.when(g == T)
    def _():
        nmid_ref[...] = normed(hid_ref[...], gain_ref[1:2])
        acc[...] = hid_ref[: R * own]

    @pl.when(g >= T)
    def _():
        mine = []
        for j in range(4):
            act, slope = gelu_pair(mm(nmid_ref[...], deep(wa_ref, j)))
            slope_ref[0, j] = slope.astype(BF16)
            act = act.astype(BF16)
            acts[jnp.minimum(g - T, 1), j] = act
            mine.append(act[: R * own])
        mine = jnp.concatenate(mine, axis=1)
        for z in range(nz):
            acc[:, z * BLK : (z + 1) * BLK] += mm(mine, wb_ref[z, 0].reshape(-1, BLK))

    store_out(g, T, acts, sems, [act_ref])

    @pl.when(g == 2 * T - 1)
    def _():
        out_ref[...] = acc[...].astype(BF16)
        stored(acts, sems, [act_ref])


def frames_fwd(order, s, W, gain, bias, own):
    rows, D = s.shape
    T = W.shape[1]
    R = bias.shape[0]
    return call(
        functools.partial(frames_fwd_body, own),
        order,
        (s, W, W, gain, bias),
        [
            whole(s.shape),
            weight_spec(W, lambda g: (g % T, g // T)),
            weight_spec(W, lambda g: (jnp.maximum(g - T, 0), 2)),
            whole(gain.shape),
            whole(bias.shape),
        ],
        (
            struct((rows, D), BF16),
            struct((T, 3, rows, BLK), BF16),
            struct((rows, BLK), BF16),
            struct((rows, D), F32),
            struct((rows, D), BF16),
            struct((4, rows, BLK), BF16),
            struct((T, 4, rows, BLK), BF16),
            struct((R * own, D), BF16),
        ),
        (
            whole((rows, D)),
            pl.BlockSpec((1, 3, rows, BLK), lambda g, order: (jnp.minimum(g, T - 1) * order[ACTIVE], 0, 0, 0)),
            whole((rows, BLK)),
            whole((rows, D)),
            whole((rows, D)),
            HBM_REF,
            pl.BlockSpec((1, 4, rows, BLK), lambda g, order: (jnp.maximum(g - T, 0) * order[ACTIVE], 0, 0, 0)),
            whole((R * own, D)),
        ),
        2 * T,
        (
            pltpu.VMEM((rows, BLK), BF16),
            pltpu.VMEM((R * own, D), F32),
            pltpu.VMEM((2, 4, rows, BLK), BF16),
            pltpu.SemaphoreType.DMA((1,)),
        ),
        flops=2 * rows * D * 10 * D,
        moved=24 * D * D + rows * D * 30,
    )


def frames_bwd_body(own, order, gy_ref, hid_ref, slope_ref, wa_ref, wb_ref, gain_ref, proj_ref, bias_ref, s_ref, gpre_ref, branch_ref, gproj_ref, frame_ref, gg_ref, held, acc, acc_in, ghid, pres, gmix, sems):
    g = pl.program_id(0)
    T = pl.num_programs(0) // 2
    R, N = bias_ref.shape[:2]
    nz = wa_ref.shape[0]

    @pl.when(g < T)
    def _():
        part = None
        for j in range(4):
            lanes = jnp.concatenate([wb_ref[z, 0, j] for z in range(nz)], axis=1)
            gpre = (mm_t(gy_ref[...], lanes) * slope_ref[0, j].astype(F32)).astype(BF16)

            pres[jnp.minimum(g, 1), j] = gpre
            piece = mm_t(gpre, deep(wa_ref, j))
            part = piece if part is None else part + piece
        acc[...] = part + jnp.where(g == 0, 0.0, acc[...])

    store_out(g, 0, pres, sems, [gpre_ref])

    @pl.when(g == T - 1)
    def _():
        back, _ = norm_back(hid_ref[...], gain_ref[1:2], acc[...])
        branch_ref[...] = (gy_ref[...].astype(F32) + back).astype(BF16)
        back_own, gg = norm_back(hid_ref[: R * own], gain_ref[1:2], acc[: R * own])
        gg_ref[1:2] = gg
        ghid[...] = gy_ref[: R * own].astype(F32) + back_own

    @pl.when(g >= T)
    def _():
        lanes = jnp.concatenate([wa_ref[z, 0, 3] for z in range(nz)], axis=1)
        gmix[...] = mm_t(branch_ref[...], lanes).astype(BF16)
        masks = head_masks((N, BLK))
        for r in range(R):
            q, k, v = (pick(proj_ref.at[0, i], r, R, own) for i in range(3))
            q4 = spread(q, masks)
            p = head_weights(q4, k, bias_ref[r])
            gm4 = spread(pick(gmix, r, R, own), masks)
            ga = mm_t(gm4, v)
            gs = (SCALE * p * (ga - jnp.sum(p * ga, axis=-1, keepdims=True))).astype(BF16)
            place(held.at[0], r, R, own, gathered(mm(gs, k), masks).astype(BF16))
            place(held.at[1], r, R, own, inner(gs, q4).astype(BF16))
            place(held.at[2], r, R, own, inner(p.astype(BF16), gm4).astype(BF16))

        @pl.when(g == T)
        def _():
            gproj_ref[...] = held[...]

        part = None
        for which in range(3):
            piece = mm_t(held[which, : R * own], deep(wa_ref, which))
            part = piece if part is None else part + piece
        acc_in[...] = part + jnp.where(g == T, 0.0, acc_in[...])

    @pl.when(g == 2 * T - 1)
    def _():
        back, gg = norm_back(s_ref[: R * own], gain_ref[0:1], acc_in[...])
        gg_ref[0:1] = gg
        frame_ref[...] = ghid[...] + back
        stored(pres, sems, [gpre_ref])


def frames_bwd(order, gy, hid, slope, W, gain, proj, bias, s, own):
    rows, D = hid.shape
    T = W.shape[1]
    R = bias.shape[0]
    return call(
        functools.partial(frames_bwd_body, own),
        order,
        (gy, hid, slope, W, W, gain, proj, bias, s),
        [
            whole(gy.shape),
            whole(hid.shape),
            pl.BlockSpec((1, 4, rows, BLK), lambda g, order: (jnp.minimum(g, T - 1) * order[ACTIVE], 0, 0, 0)),
            weight_spec(W, lambda g: (g % T, 1 - g // T)),
            weight_spec(W, lambda g: (jnp.minimum(g, T - 1), 2)),
            whole(gain.shape),
            pl.BlockSpec((1, 3, rows, BLK), lambda g, order: (jnp.maximum(g - T, 0) * order[ACTIVE], 0, 0, 0)),
            whole(bias.shape),
            whole(s.shape),
        ],
        (
            struct((4, rows, BLK), BF16),
            struct((rows, D), BF16),
            struct((3, rows, BLK), BF16),
            struct((R * own, D), F32),
            struct((2, D), F32),
        ),
        (
            HBM_REF,
            whole((rows, D)),
            whole((3, rows, BLK)),
            whole((R * own, D)),
            whole((2, D)),
        ),
        2 * T,
        (
            pltpu.VMEM((3, rows, BLK), BF16),
            pltpu.VMEM((rows, D), F32),
            pltpu.VMEM((R * own, D), F32),
            pltpu.VMEM((R * own, D), F32),
            pltpu.VMEM((2, 4, rows, BLK), BF16),
            pltpu.VMEM((rows, BLK), BF16),
            pltpu.SemaphoreType.DMA((1,)),
        ),
        flops=2 * rows * D * 14 * D,
        moved=24 * D * D + rows * D * 30,
    )


def head_sum(prods):
    row = lax.broadcasted_iota(jnp.int32, (BLK, BLK), 0) // HEAD_DIM
    col = lax.broadcasted_iota(jnp.int32, (BLK, BLK), 1) // HEAD_DIM
    ones = jnp.where(row == col, 1.0, 0.0).astype(BF16)
    high = prods.astype(BF16)
    low = (prods - high.astype(F32)).astype(BF16)
    return mm(high, ones) + mm(low, ones)


def token_pairs(count):
    return [(a, b) for a in range(1, count) for b in range(a + 1)]


def pair_sums(left, right, count):
    pairs = token_pairs(count)
    m = left[0].shape[0]
    sums = head_sum(jnp.concatenate([left[a] * right[b] for a, b in pairs], axis=0))
    return {pair: sums[i * m : (i + 1) * m] for i, pair in enumerate(pairs)}


def token_weights(q, k, count):
    s = pair_sums(q, k, count)
    out = {}
    for a in range(1, count):
        top = s[a, 0]
        for b in range(1, a + 1):
            top = jnp.maximum(top, s[a, b])
        e = [jnp.exp((s[a, b] - top) * SCALE) for b in range(a + 1)]
        total = e[0]
        for b in range(1, a + 1):
            total = total + e[b]
        share = 1.0 / total
        for b in range(a + 1):
            out[a, b] = e[b] * share
    return out


def rounded(value):
    return value.astype(BF16).astype(F32)


def split_tokens(value, count):
    m = value.shape[0] // count
    return [value[i * m : (i + 1) * m].astype(F32) for i in range(count)]


def codes_fwd_body(order, codes_ref, sent_ref, cot_ref, gact_ref, w_ref, gain_ref, proj_ref, hid_ref, ghid_ref, gg_ref, own_ref, far_ref, other_ref, bundle_ref, nin, nmid, branch, acc, acts, pres, mixes, sems):
    g = pl.program_id(0)
    T = pl.num_programs(0) // 2
    C, m, _ = codes_ref.shape
    nz = w_ref.shape[0]
    four = lambda ref, at: ref.at[pl.ds(at, 4)]
    to_a = [four(own_ref, 0), far_ref, four(bundle_ref, 0), other_ref]
    to_p = [four(own_ref, 4), four(own_ref, 8), four(bundle_ref, 4), four(bundle_ref, 8)]
    to_m = [own_ref.at[12], own_ref.at[13], bundle_ref.at[24], bundle_ref.at[25]]
    wides = [(nin, 12), (nmid, 16), (branch, 20)]

    def move(i):
        wide, at = wides[i]
        return pltpu.make_async_copy(wide, four(bundle_ref, at), sems.at[3, i])

    @pl.when(g == 0)
    def _():
        for c in range(C):
            s = codes_ref[c].astype(F32) + sent_ref[...].astype(F32)
            rows = pl.ds(c * m, m)
            hid_ref[rows] = s
            s = normed(s, gain_ref[0:1])
            for z in range(nz):
                nin[z, rows] = s[:, z * BLK : (z + 1) * BLK]
        move(0).start()

    @pl.when(g < T)
    def _():
        part = []
        wide = jnp.concatenate([nin[z] for z in range(nz)], axis=1)
        for which in range(3):
            block = mm(wide, deep(w_ref, which)).astype(BF16)
            proj_ref[0, which] = block
            part.append(split_tokens(block, C))
        q, k, v = part
        p = token_weights(q, k, C)
        mixed = [v[0]]
        for a in range(1, C):
            total = rounded(p[a, 0]) * v[0]
            for b in range(1, a + 1):
                total += rounded(p[a, b]) * v[b]
            mixed.append(total)
        mixed = jnp.concatenate(mixed, axis=0).astype(BF16)
        mixes[g] = mixed
        for z in range(nz):
            hid_ref[:, z * BLK : (z + 1) * BLK] += mm(mixed, w_ref[z, 0, 3])

    @pl.when(g == T)
    def _():
        s = normed(hid_ref[...], gain_ref[1:2])
        for z in range(nz):
            nmid[z] = s[:, z * BLK : (z + 1) * BLK]
        move(1).start()

    @pl.when(g >= T)
    def _():
        part = None
        wide = jnp.concatenate([nmid[z] for z in range(nz)], axis=1)
        for j in range(4):
            act, slope = gelu_pair(mm(wide, deep(w_ref, j)))
            gpre = (gact_ref[0, j].astype(F32) * slope).astype(BF16)
            acts[g - T, j] = act.astype(BF16)
            pres[g - T, j] = gpre
            piece = mm_t(gpre, deep(w_ref, j))
            part = piece if part is None else part + piece
        acc[...] = part + jnp.where(g == T, 0.0, acc[...])

    store_out(g, 0, mixes, sems.at[0], to_m)
    store_out(g, T, acts, sems.at[1], to_a)
    store_out(g, T, pres, sems.at[2], to_p)

    @pl.when(g == 2 * T - 1)
    def _():
        back, gg = norm_back(hid_ref[...], gain_ref[1:2], acc[...])
        gg_ref[...] = gg
        ghid = cot_ref[...].astype(F32) + back
        ghid_ref[...] = ghid
        for z in range(nz):
            branch[z] = ghid[:, z * BLK : (z + 1) * BLK].astype(BF16)
        move(2).start()
        stored(mixes, sems.at[0], to_m)
        stored(acts, sems.at[1], to_a)
        stored(pres, sems.at[2], to_p)
        for i in range(3):
            move(i).wait()


OWN_BLOCKS, BUNDLE = 14, 26


def kept(shape, first, half):
    return pl.BlockSpec(
        (1,) + shape, lambda g, order: (clip(g - first, 0, half - 1) * order[ACTIVE],) + (0,) * len(shape)
    )


def codes_fwd(order, codes, sent, cot, gact, W, gain):
    C, m, D = codes.shape
    rows = C * m
    nz, T = W.shape[:2]
    act = struct((4, rows, BLK), BF16)
    wide = pltpu.VMEM((nz, rows, BLK), BF16)
    return call(
        codes_fwd_body,
        order,
        (codes, sent, cot, gact, W, gain),
        [
            whole(codes.shape),
            whole(sent.shape),
            whole(cot.shape),
            kept((4, rows, BLK), T, T),
            weight_spec(W, lambda g: (g % T, g // T)),
            whole(gain.shape),
        ],
        (
            struct((T, 3, rows, BLK), BF16),
            struct((rows, D), F32),
            struct((rows, D), F32),
            struct((1, D), F32),
            struct((OWN_BLOCKS, rows, BLK), BF16),
            act,
            act,
            struct((BUNDLE, rows, BLK), BF16),
        ),
        (
            kept((3, rows, BLK), 0, T),
            whole((rows, D)),
            whole((rows, D)),
            whole((1, D)),
            *[HBM_REF] * 4,
        ),
        2 * T,
        (
            wide,
            wide,
            wide,
            pltpu.VMEM((rows, D), F32),
            pltpu.VMEM((T, 4, rows, BLK), BF16),
            pltpu.VMEM((T, 4, rows, BLK), BF16),
            pltpu.VMEM((T, rows, BLK), BF16),
            pltpu.SemaphoreType.DMA((4, T)),
        ),
        flops=2 * rows * D * 12 * D,
        moved=16 * D * D + rows * D * 40,
    )


def codes_gact_body(order, cot_ref, wd_ref, gact_ref):
    for j in range(4):
        lanes = jnp.concatenate([wd_ref[z, 0, j] for z in range(wd_ref.shape[0])], axis=1)
        gact_ref[0, j] = mm_t(cot_ref[...], lanes).astype(BF16)


def codes_gact(order, cot, W):
    rows, D = cot.shape
    T = W.shape[1]
    return call(
        codes_gact_body,
        order,
        (cot, W),
        [whole(cot.shape), weight_spec(W, lambda g: (g, 2))],
        struct((T, 4, rows, BLK), BF16),
        pl.BlockSpec((1, 4, rows, BLK), lambda g, order: (g * order[ACTIVE], 0, 0, 0)),
        T,
        flops=2 * rows * D * 4 * D,
        moved=8 * D * D + rows * D * 10,
    )


def codes_back_body(order, proj_ref, w_ref, codes_ref, sent_ref, ghid_ref, gain_ref, keep_ref, send_ref, glocal_ref, gsent_ref, gg_ref, acc, held, branch, sems):
    g = pl.program_id(0)
    C, m, _ = codes_ref.shape
    T = pl.num_programs(0)

    @pl.when(g == 0)
    def _():
        branch[...] = ghid_ref[...].astype(BF16)

    nz = w_ref.shape[0]
    lanes = jnp.concatenate([w_ref[z, 0, 3] for z in range(nz)], axis=1)
    gmix = mm_t(branch[...], lanes)
    gm = split_tokens(gmix.astype(BF16), C)
    q, k, v = (split_tokens(proj_ref[0, i], C) for i in range(3))
    p = token_weights(q, k, C)
    ga = pair_sums(gm, v, C)

    def add(left, right):
        return right if left is None else left + right

    gq, gk, gv = [jnp.zeros_like(q[0])], [None] * C, [gm[0]] + [None] * (C - 1)
    for a in range(1, C):
        centre = p[a, 0] * ga[a, 0]
        for b in range(1, a + 1):
            centre += p[a, b] * ga[a, b]
        total = None
        for b in range(a + 1):
            gs = rounded(SCALE * p[a, b] * (ga[a, b] - centre))
            total = add(total, gs * k[b])
            gk[b] = add(gk[b], gs * q[a])
            gv[b] = add(gv[b], rounded(p[a, b]) * gm[a])
        gq.append(total)
    joined = [jnp.concatenate(part, axis=0).astype(BF16) for part in (gq, gk, gv)]

    for which in range(3):
        held[g, which] = joined[which]
    part = None
    for which in range(3):
        part = add(part, mm_t(joined[which], deep(w_ref, which)))
    acc[...] = part + jnp.where(g == 0, 0.0, acc[...])
    outs = [keep_ref.at[0], keep_ref.at[1], send_ref.at[0], send_ref.at[1]]
    store_out(g, 0, held, sems, outs)

    @pl.when(g == T - 1)
    def _():
        total = None
        gains = None
        for c in range(C):
            rows = slice(c * m, (c + 1) * m)
            s = codes_ref[c].astype(F32) + sent_ref[...].astype(F32)
            back, gg = norm_back(s, gain_ref[0:1], acc[rows])
            gains = add(gains, gg)
            local = (ghid_ref[rows] + back).astype(BF16)
            glocal_ref[c] = local
            total = add(total, local.astype(F32))
        gsent_ref[...] = total.astype(BF16)
        gg_ref[...] = gains
        stored(held, sems, outs)


def codes_back(order, proj, W, codes, sent, ghid, gain):
    rows, D = ghid.shape
    C, m, _ = codes.shape
    T = W.shape[1]
    half = T // 2
    blocks = struct((half, 3, rows, BLK), BF16)
    return call(
        codes_back_body,
        order,
        (proj, W, codes, sent, ghid, gain),
        [
            pl.BlockSpec((1, 3, rows, BLK), lambda g, order: (g * order[ACTIVE], 0, 0, 0)),
            weight_spec(W, lambda g: (g, 0)),
            whole(codes.shape),
            whole(sent.shape),
            whole(ghid.shape),
            whole(gain.shape),
        ],
        (blocks, blocks, struct(codes.shape, BF16), struct((m, D), BF16), struct((1, D), F32)),
        (
            HBM_REF,
            HBM_REF,
            whole(codes.shape),
            whole((m, D)),
            whole((1, D)),
        ),
        T,
        (
            pltpu.VMEM((rows, D), F32),
            pltpu.VMEM((T, 3, rows, BLK), BF16),
            pltpu.VMEM((rows, D), BF16),
            pltpu.SemaphoreType.DMA((T,)),
        ),
        flops=2 * rows * D * 4 * D,
        moved=8 * D * D + rows * D * 20,
    )


def codes_out_body(order, hid_ref, a0_ref, a1_ref, a2_ref, a3_ref, wd_ref, out_ref, acc):
    g = pl.program_id(0)
    T = pl.num_programs(0)
    C, m, _ = out_ref.shape

    @pl.when(g == 0)
    def _():
        acc[...] = hid_ref[...]

    for i, act_ref in enumerate((a0_ref, a1_ref, a2_ref, a3_ref)):

        @pl.when(g == i)
        def _():
            act = jnp.concatenate([act_ref[j] for j in range(4)], axis=1)
            for z in range(wd_ref.shape[0]):
                acc[:, z * BLK : (z + 1) * BLK] += mm(act, wd_ref[z, 0].reshape(-1, BLK))

    @pl.when(g == T - 1)
    def _():
        for c in range(C):
            out_ref[c] = acc[c * m : (c + 1) * m].astype(BF16)


def codes_out(order, hid, acts, W, C):
    rows, D = hid.shape
    T = W.shape[1]
    m = rows // C
    return call(
        codes_out_body,
        order,
        (hid, *acts, W),
        [
            whole(hid.shape),
            *[pl.BlockSpec((4, rows, BLK), lambda g, order: (0, 0, 0))] * 4,
            weight_spec(W, lambda g: (g, 2)),
        ],
        struct((C, m, D), BF16),
        whole((C, m, D)),
        T,
        (pltpu.VMEM((rows, D), F32),),
        flops=2 * rows * D * 4 * D,
        moved=8 * D * D + rows * D * 14,
    )


def put(ref, value, by_rows):
    for z in range(ref.shape[0]):
        at = slice(z * BLK, (z + 1) * BLK)
        ref[z, 0] = (value[at] if by_rows else value[:, at]).astype(BF16)


def got(ref, by_rows):
    parts = [ref[z, 0].astype(F32) for z in range(ref.shape[0])]
    return jnp.concatenate(parts, axis=0 if by_rows else 1)


def grads_body(parts, has_got, flag, *refs):
    g = pl.program_id(0)
    slots = sum(part[0] and max(part[3], part[4]) for part in parts)
    out_ref = refs[len(refs) - 1 - slots]
    turned = refs[len(refs) - slots :]
    got_ref = refs[len(refs) - 2 - slots]
    at = 0
    for by_rows, begin, end, ones, zeros in parts:
        for value, count in ((1, ones), (0, zeros)):
            pairs = [(refs[at + 2 * i], refs[at + 2 * i + 1]) for i in range(count)]
            at += 2 * count
            if not count:
                continue

            def full(wide):
                if len(wide.shape) == 3:
                    return jnp.concatenate([wide[z] for z in range(wide.shape[0])], axis=1)
                return wide[...]

            if by_rows:

                @pl.when((flag[0] == value) & (g == begin))
                def _():
                    for (wide, _), turn in zip(pairs, turned):
                        turn[:, : wide.shape[-2]] = full(wide).T

            @pl.when((flag[0] == value) & (g >= begin) & (g < end))
            def _():
                total = None
                for i, (wide, narrow) in enumerate(pairs):
                    if by_rows:
                        piece = mm(turned[i][:, : wide.shape[-2]], narrow[0])
                    else:
                        piece = inner(narrow[0], full(wide))
                    total = piece if total is None else total + piece
                if has_got and value == 0:
                    total = total + got(got_ref, by_rows)
                put(out_ref, total, by_rows)


def grads(flag, nz, parts, received=None):
    inputs, specs, plan = [], [], []
    begin = flops = moved = 0
    for by_rows, count, ones, zeros in parts:
        for wide, narrow, base, *more in ones + zeros:
            if isinstance(wide, tuple):
                wide, at = wide
                rows = wide.shape[1]
                specs.append(
                    pl.BlockSpec((nz, rows, BLK), lambda g, f, a=at // nz: (a, 0, 0))
                )
            else:
                rows = wide.shape[0]
                specs.append(whole(wide.shape))
            specs.append(
                pl.BlockSpec(
                    (1, rows, BLK),
                    lambda g, f, s=begin, b=base, c=count, m=sum(more): (
                        b + clip(g - s, 0, c - 1),
                        m,
                        0,
                    ),
                )
            )
            inputs += [wide, narrow]
            flops += rows * nz * BLK * BLK * count
            moved += 4 * rows * nz * BLK
        plan.append((by_rows, begin, begin + count, len(ones), len(zeros)))
        begin += count
    turns = []
    for by_rows, _, ones, zeros in parts:
        if by_rows:
            rows = [[p[1].shape[1] for p in side] for side in (ones, zeros)]
            for i in range(max(len(side) for side in rows)):
                longest = max(side[i] for side in rows if len(side) > i)
                turns.append(pltpu.VMEM((nz * BLK, longest), BF16))
    block = pl.BlockSpec((nz, 1, BLK, BLK), lambda g, f: (0, g, 0, 0))
    if received is not None:
        inputs.append(received)
        specs.append(block)
    return call(
        functools.partial(grads_body, plan, received is not None),
        flag,
        inputs,
        specs,
        struct((nz, begin, BLK, BLK), BF16),
        block,
        begin,
        turns,
        flops=2 * flops,
        moved=moved + nz * begin * BLK * BLK * 4,
    )


def swap(value, axis, bit):
    count = lax.axis_size(axis)
    return lax.ppermute(value, axis, [(i, i ^ bit) for i in range(count)])


def swap_in(value, section, bit):
    count = lax.axis_size("tensor")
    pairs = [(section * count + i, section * count + (i ^ bit)) for i in range(count)]
    return lax.ppermute(value, ("section", "tensor"), pairs)


def together(*values):
    return lax.optimization_barrier(values)


def after(value, *others):
    return together(value, *others)[0]


def gather_weights(w_qkv, w_out, w_up, w_down):
    depth = w_qkv.shape[1]
    shards = lax.axis_size("dp")
    slices = lax.axis_size("tensor")
    both = ("dp", "tensor")
    if depth == BLK:
        up_blocks = [w_up[None, :, i : i + BLK] for i in range(0, w_up.shape[1], BLK)]
        flat = jnp.concatenate(
            [w_qkv, w_out[None], *up_blocks, w_down.reshape(-1, BLK, BLK)], axis=0
        )
        out = lax.all_gather(flat, both)
        return out.reshape(shards, slices, *flat.shape)
    per = BLK // depth
    nz = shards // per

    def by_rows(value):
        out = lax.all_gather(value, both).reshape(nz, per, slices, value.shape[0], depth, BLK)
        return out.transpose(0, 2, 3, 1, 4, 5).reshape(nz, slices, -1, BLK, BLK)

    def by_cols(value):
        out = lax.all_gather(value, both)
        out = out.reshape(nz, per, slices, value.shape[0] // BLK, BLK, depth)
        return out.transpose(0, 2, 3, 4, 1, 5).reshape(nz, slices, -1, BLK, BLK)

    up_blocks = w_up.reshape(depth, -1, BLK).transpose(1, 0, 2)
    return jnp.concatenate(
        [by_rows(w_qkv), by_cols(w_out), by_rows(up_blocks), by_cols(w_down)], axis=2
    )


def scatter_blocks(parts, split):
    shards = lax.axis_size("dp")
    nz, count = parts.shape[:2]
    per = shards // nz
    if per == 1:
        out = lax.psum_scatter(parts, "dp", scatter_dimension=0, tiled=False)
        return out[:split], out[split:]
    depth = BLK // per
    rows = parts[:, :split].reshape(nz, split, per, depth, BLK)
    rows = rows.transpose(0, 2, 1, 3, 4).reshape(shards, -1, BLK)
    columns = parts[:, split:].reshape(nz, count - split, BLK, per, depth)
    columns = columns.transpose(0, 3, 1, 2, 4).reshape(shards, -1, BLK)
    out = lax.psum_scatter(
        jnp.concatenate([rows, columns], axis=1), "dp", scatter_dimension=0, tiled=False
    )
    cut = split * depth
    return out[:cut].reshape(split, depth, BLK), out[cut:].reshape(-1, BLK, depth)


def on_device(codes, cotangent, doc_lengths, w_qkv, w_out, w_up, w_down, gains):
    is_first = lax.axis_index("section") == 0
    flag = is_first.astype(jnp.int32).reshape(1)
    t = lax.axis_index("tensor")
    T = lax.axis_size("tensor")
    R, F, C, D = codes.shape
    M = R * F
    N = T * F
    gain = gains[0]
    W = gather_weights(w_qkv[0], w_out[0], w_up[0], w_down[0])
    nz = W.shape[0]
    slices = t ^ jnp.array([0, 2, 1, 3], jnp.int32)
    order0 = jnp.concatenate([slices, flag])
    order1 = jnp.concatenate([slices, 1 - flag])
    codes_t = codes.transpose(2, 0, 1, 3).reshape(C, M, D)
    cot = cotangent.transpose(2, 0, 1, 3).reshape(C * M, D)

    frame_own = jnp.sum(codes_t.astype(F32), axis=0)
    far = swap(frame_own, "tensor", 2)
    s0 = jnp.concatenate(
        [frame_own, swap(frame_own, "tensor", 1), far, swap(far, "tensor", 1)], axis=0
    )
    spot = t ^ lax.iota(jnp.int32, T)
    pos = (spot[:, None] * F + lax.iota(jnp.int32, F)[None]).reshape(N)
    ends = jnp.cumsum(doc_lengths, axis=1)
    seg = jnp.sum((pos[None, :, None] >= ends[:, None, :]).astype(jnp.int32), axis=2)
    allowed = (pos[:, None] >= pos[None, :])[None] & (seg[:, :, None] == seg[:, None, :])
    bias = jnp.where(allowed, 0.0, NEG).astype(F32)

    n_in0, proj0, mixed0, hid0, n_mid0, act0, slope0, out0 = frames_fwd(order0, s0, W, gain, bias, F)
    sent = lax.ppermute(out0, "section", [(0, 1)])

    def swap1(value, bit):
        return swap_in(value, 1, bit)

    gact1 = codes_gact(order1, cot, W)
    late = after(cot, s0)
    cot_y = swap1(late, 2)
    cot_s, cot_d = swap1(late, 1), swap1(cot_y, 1)
    sent = after(sent, cot_s, cot_d)
    proj1, hid1, ghid1, gg_mid1, own1, act_far, act_other, bundle = codes_fwd(
        order1, codes_t, sent, cot, gact1, W, gain
    )
    act_y = swap1(act_far, 2)
    act_o = swap1(act_other, 1)
    bundle_s = swap1(bundle, 1)
    gproj1, gproj1_s, glocal, gsent, gg_in1 = codes_back(
        order1, proj1, W, codes_t, sent, ghid1, gain
    )

    gproj1, gproj1_s, glocal, gsent, gg_in1, act_y, act_o, bundle_s = together(
        gproj1, gproj1_s, glocal, gsent, gg_in1, act_y, act_o, bundle_s
    )

    gsent = lax.ppermute(gsent, "section", [(1, 0)])
    act_d = swap1(act_o, 2)
    out1 = codes_out(order1, hid1, [own1, act_far, bundle, act_other], W, C)
    gsent, out1 = together(gsent, out1)
    gfar = swap_in(gsent, 0, 2)

    M1 = C * M
    gproj1 = gproj1.reshape(-1, M1, BLK)
    bundle_s = after(bundle_s, gsent)
    gproj1_s = swap1(after(gproj1_s, gsent), 1).reshape(-1, M1, BLK)
    up_far = grads(
        flag, nz, [(True, 4, [], [((bundle, 16), own1, 8), ((bundle_s, 16), bundle_s, 8)])]
    )
    up_got = swap1(up_far, 2)
    att_far = grads(
        flag,
        nz,
        [
            (True, 3, [], [((bundle, 12), gproj1, 3), ((bundle_s, 12), gproj1_s, 3)]),
            (False, 1, [], [((bundle, 20), own1, 13), ((bundle_s, 20), bundle_s, 25)]),
        ],
    )
    gfar, up_far, att_far = together(gfar, up_far, att_far)
    att_got = swap1(att_far, 2)
    glocal = lax.ppermute(after(glocal, gfar), "section", [(1, 0)])
    gy0 = jnp.concatenate(
        [gsent, swap_in(gsent, 0, 1), gfar, swap_in(gfar, 0, 1)], axis=0
    )

    down_total = grads(
        flag,
        nz,
        [
            (
                False,
                4,
                [(gy0, act0, 0)],
                [(cot, own1, 0), (cot_s, bundle_s, 0), (cot_y, act_y, 0), (cot_d, act_d, 0)],
            )
        ],
    )
    down_part = scatter_blocks(down_total, 0)[1]

    gpre0, branch0, gproj0, frame, gg0 = frames_bwd(
        order0, gy0, hid0, slope0, W, gain, proj0, bias, s0, F
    )
    up_total = grads(
        flag,
        nz,
        [
            (
                True,
                4,
                [(n_mid0, gpre0, 0)],
                [((bundle, 16), own1, 4), ((bundle_s, 16), bundle_s, 4)],
            )
        ],
        up_got,
    )
    up_part = scatter_blocks(up_total, 4)[0]
    gproj0 = after(gproj0, up_total, glocal)
    att_total = grads(
        flag,
        nz,
        [
            (
                True,
                3,
                [(n_in0, gproj0, 0)],
                [((bundle, 12), gproj1, 0), ((bundle_s, 12), gproj1_s, 0)],
            ),
            (
                False,
                1,
                [(branch0, mixed0[None], 0)],
                [((bundle, 20), own1, 12), ((bundle_s, 20), bundle_s, 24)],
            ),
        ],
        att_got,
    )
    qkv_part, out_part = scatter_blocks(att_total, 3)
    gain_part = jnp.where(is_first, gg0, jnp.concatenate([gg_in1, gg_mid1], axis=0))
    grad_gains = lax.psum(after(gain_part, att_total), ("dp", "tensor"))

    code_grad = (glocal.astype(F32) + frame[None]).astype(BF16)
    result = jnp.where(is_first, code_grad, out1).reshape(C, R, F, D).transpose(1, 2, 0, 3)
    depth = w_up.shape[1]
    return (
        result[None],
        qkv_part.astype(F32)[None],
        out_part.reshape(-1, depth).astype(F32)[None],
        up_part.transpose(1, 0, 2).reshape(depth, -1).astype(F32)[None],
        down_part.reshape(-1, depth).astype(F32)[None],
        grad_gains[None],
    )


def solution(mesh):
    placed = (
        P("dp", "tensor", None, None),
        P("dp", "tensor", None, None),
        P("dp", None),
        P("section", None, "dp", "tensor"),
        P("section", "tensor", "dp"),
        P("section", "dp", "tensor"),
        P("section", "tensor", "dp"),
        P("section", None, None),
    )
    return jax.shard_map(
        on_device,
        mesh=mesh,
        in_specs=placed,
        out_specs=(
            P("section", "dp", "tensor", None, None),
            P("section", None, "dp", "tensor"),
            P("section", "tensor", "dp"),
            P("section", "dp", "tensor"),
            P("section", "tensor", "dp"),
            P("section", None, None),
        ),
        check_vma=False,
    )
```

time: 571 us -> 453 us (0.79)
  Pallas kernels: 212 us -> 108 us
  local copies, waits for them, and re-layouts: 33.8 us -> 17.5 us
  waiting for transfers between devices: 231 us -> 241 us
    pallas_call x13 -> x11, Pallas kernels: 212 us -> 108 us  [call(): pl.pallas_call(run, out_shape=outs, grid_spec=pltpu.PrefetchScalarGridSpe...]
    reduce_scatter x2 -> x3, waiting for transfers between devices: 93.4 us -> 31.4 us  [scatter_blocks(): out = lax.psum_scatter(parts, 'dp', scatter_dimension=0, tiled=False)]
    ppermute x1, waiting for transfers between devices: 0.01 us -> 41.8 us  [on_device(): glocal = lax.ppermute(after(glocal, gfar), 'section', [(1, 0)])]
    ppermute x1, waiting for transfers between devices: 7.32 us -> 40.4 us  [on_device(): gsent = lax.ppermute(gsent, 'section', [(1, 0)])]
    unnamed x108 -> x58, local copies, waits for them, and re-layouts: 26 us -> 15.1 us
    ppermute x12 -> x13, starting transfers between devices: 18.8 us -> 20.2 us  [swap_in(): return lax.ppermute(value, ('section', 'tensor'), pairs)]
    ppermute x2 -> x3, waiting for transfers between devices: 19.4 us -> 19.2 us  [swap(): return lax.ppermute(value, axis, [(i, i ^ bit) for i in range(count)])]
  transfers between devices with their start and end apart: 20 -> 23, of which waited for: 6 -> 8; matrix products, arithmetic and copies ran while one was open for 2% -> 2% of each run, Pallas kernels for 19% -> 21%
where the time goes in v2:
time: 453 us; the launch traced here: 451 us
  waiting for transfers between devices  241 us (53%)
  Pallas kernels  108 us (24%)
  blocking collectives  32.5 us (7%)
  starting transfers between devices  27.5 us (6%)
  local copies, waits for them, and re-layouts  17.5 us (4%)
  between operations  14.3 us (3%)
  other arithmetic  10.8 us (2%)
    pallas_call x11, Pallas kernels, call(): pl.pallas_call(run, out_shape=outs, grid_spec=pltpu.PrefetchScalarGridSpe...  108 us
    all_gather x1, waiting for transfers between devices, gather_weights(): out = lax.all_gather(flat, both)  105 us
    ppermute x1, waiting for transfers between devices, on_device(): glocal = lax.ppermute(after(glocal, gfar), 'section', [(1, 0)])  41.8 us
    ppermute x1, waiting for transfers between devices, on_device(): gsent = lax.ppermute(gsent, 'section', [(1, 0)])  40.4 us
    psum x1, blocking collectives, on_device(): grad_gains = lax.psum(after(gain_part, att_total), ('dp', 'tensor'))  32.5 us
    reduce_scatter x3, waiting for transfers between devices, scatter_blocks(): out = lax.psum_scatter(parts, 'dp', scatter_dimension=0, tiled=False)  31.4 us
    ppermute x13, starting transfers between devices, swap_in(): return lax.ppermute(value, ('section', 'tensor'), pairs)  20.2 us
    ppermute x3, waiting for transfers between devices, swap(): return lax.ppermute(value, axis, [(i, i ^ bit) for i in range(count)])  19.2 us
  transfers between devices with their start and end apart: 23, of which 8 were waited for; matrix products, arithmetic and copies ran while one was open for 2% of the time, Pallas kernels for 21%

profile of v2, /device:TPU:0, one launch (start us, length us, event | category | flops | bytes accessed | tf_op | source)
XLA Modules:
  0.0 451.5 jit_solution(16089164890542348273)
XLA Ops:
  12.7 3.0 collective-permute-start.1
  15.7 17.4 %collective-permute-done.1 = f32[128,1024]{1,0:T(8,128)S(1)} collective-permute-done((f32[128,1024]{1,0:T(8,128)S(1)}, f32[128,1024]{1,0:T(8,128)S(1)}, u32[]{:S(2)}, u32[]{:S(2)}) %collective-permute-start.1) | collective-permute-done | bytes 524320 | tf_op jit(solution)/shard_map/ppermute | solution.py:841
  42.6 104.8 %all-gather.3.cloned.1.call-done = bf16[192,256,256]{2,1,0:T(8,128)(2,1)} async-done(((bf16[12,256,256]{2,1,0:T(8,128)(2,1)}), bf16[192,256,256]{2,1,0:T(8,128)(2,1)}) %all-gather.3.cloned.1.call-update) | async-done | bytes 25165840 | tf_op jit(solution)/shard_map/all_gather | solution.py:868
  147.4 27.6 %shard_map.136 = (bf16[512,1024]{1,0:T(8,128)(2,1)}, bf16[4,3,512,256]{3,2,1,0:T(8,128)(2,1)}, bf16[512,256]{1,0:T(8,128)(2,1)}, f32[512,1024]{1,0:T(8,128)}, bf...) custom-call(s32[5]{0:T(128)} %get-tuple-element.114.flags, ...), custom_call_target="tpu_custom_call" | custom-call | flops 1342177280 | bytes 5111808 | tf_op jit(solution)/shard_map/pallas_call | solution.py:101
  177.4 3.3 shard_map.137.refs_3_
  180.7 2.1 collective-permute-done.3.refs_1_.refs_3_
  183.5 5.1 %shard_map.138 = (bf16[4,3,384,256]{3,2,1,0:T(8,128)(2,1)}, f32[384,1024]{1,0:T(8,128)}, f32[384,1024]{1,0:T(8,128)}, f32[1,1024]{1,0:T(1,128)}, bf16[14,384,256...) custom-call(s32[5]{0:T(128)} %get-tuple-element.115.flags, ...), custom_call_target="tpu_custom_call" | custom-call | flops 1207959552 | bytes 4063232 | tf_op jit(solution)/shard_map/pallas_call | solution.py:101
  188.6 2.9 collective-permute-start.9
  193.0 4.3 shard_map.139
  198.6 4.6 %shard_map.140 = bf16[3,128,1024]{2,1,0:T(8,128)(2,1)} custom-call(s32[5]{0:T(128)} %get-tuple-element.115.flags, f32[384,1024]{1,0:T(8,128)} %get-tuple-element.66.refs_0_, bf16[14,384,256]{2,1,0:T(8,128)(2,1)} %get-tuple-element.67.refs_1_.refs_5_.refs_3_.refs_9_, bf16[4,384,256]{2,1,0:T(8,128)(2,1)} %get-tuple-element.61.refs_2_, ...), custom_call_target="tpu_custom_call" | custom-call | flops 402653184 | bytes 1736704 | tf_op jit(solution)/shard_map/pallas_call | solution.py:101
  203.2 40.4 %collective-permute-done.10 = bf16[128,1024]{1,0:T(8,128)(2,1)S(1)} collective-permute-done((bf16[128,1024]{1,0:T(8,128)(2,1)}, bf16[128,1024]{1,0:T(8,128)(2,1)S(1)}, u32[]{:S(2)}, u32[]{:S(2)}) %collective-permute-start.10) | collective-permute-done | bytes 262176 | tf_op jit(solution)/shard_map/ppermute | solution.py:961
  245.1 3.4 collective-permute-start.11
  250.5 4.3 shard_map.141
  255.8 4.7 %shard_map.142 = bf16[4,4,256,256]{3,2,1,0:T(8,128)(2,1)} custom-call(s32[1]{0:T(128)} %bitcast.flags, bf16[26,384,256]{2,1,0:T(8,128)(2,1)} %get-tuple-element.63.refs_3_.refs_0_.refs_4_.refs_2_.refs_8_, bf16[6,384,256]{2,1,0:T(8,128)(2,1)} %bitcast.68, ...), custom_call_target="tpu_custom_call" | custom-call | flops 201326592 | bytes 1310720 | tf_op jit(solution)/shard_map/pallas_call | solution.py:101
  260.5 2.4 collective-permute-start.15
  265.3 6.6 %shard_map.146 = bf16[4,4,256,256]{3,2,1,0:T(8,128)(2,1)} custom-call(s32[1]{0:T(128)} %bitcast.flags, bf16[512,1024]{1,0:T(8,128)(2,1)} %copy-done.1, bf16[4,512,256]{2,1,0:T(8,128)(2,1)} %get-tuple-element.89.refs_1_, bf16[384,1024]{1,0:T(8,128)(2,1)} %bitcast.65, bf16[14,384,256]{2,1,0:T(8,128)(2,1)} %get-tuple-element.67.refs_1_.refs_5_.refs_3_.refs_9_, ...), custom_call_target="tpu_custom_call" | custom-call | flops 536870912 | bytes 1572864 | tf_op jit(solution)/shard_map/pallas_call | solution.py:101
  273.4 2.0 collective-permute-start.16
  275.4 33.8 %shard_map.143 = (bf16[4,512,256]{2,1,0:T(8,128)(2,1)}, bf16[512,1024]{1,0:T(8,128)(2,1)}, bf16[3,512,256]{2,1,0:T(8,128)(2,1)}, f32[128,1024]{1,0:T(8,128)}, f32[2,1024]{1,0:T(2,128)}) custom-call(s32[5]{0:T(128)} %get-tuple-element.114.flags, bf16[512,1024]{1,0:T(8,128)(2,1)} %copy-done.1, f32[512,1024]{1,0:T(8,128)} %get-tuple-element.76.refs_1_, ...), custom_call_target="tpu_custom_call" | custom-call | flops 1879048192 | bytes 5111808 | tf_op jit(solution)/shard_map/pallas_call | solution.py:101
  309.2 6.5 %shard_map.144 = bf16[4,4,256,256]{3,2,1,0:T(8,128)(2,1)} custom-call(s32[1]{0:T(128)} %bitcast.flags, bf16[512,1024]{1,0:T(8,128)(2,1)} %get-tuple-element.83.refs_0_, bf16[4,512,256]{2,1,0:T(8,128)(2,1)} %get-tuple-element.84.refs_1_, bf16[26,384,256]{2,1,0:T(8,128)(2,1)} %get-tuple-element.63.refs_3_.refs_0_.refs_4_.refs_2_.refs_8_, ...), custom_call_target="tpu_custom_call" | custom-call | flops 335544320 | bytes 1179648 | tf_op jit(solution)/shard_map/pallas_call | solution.py:101
  319.4 41.8 %collective-permute-done.13 = bf16[3,128,1024]{2,1,0:T(8,128)(2,1)S(1)} collective-permute-done((bf16[3,128,1024]{2,1,0:T(8,128)(2,1)}, bf16[3,128,1024]{2,1,0:T(8,128)(2,1)S(1)}, u32[]{:S(2)}, u32[]{:S(2)}) %collective-permute-start.13) | collective-permute-done | bytes 786464 | tf_op jit(solution)/shard_map/ppermute | solution.py:985
  362.6 7.4 %shard_map.145 = bf16[4,4,256,256]{3,2,1,0:T(8,128)(2,1)} custom-call(s32[1]{0:T(128)} %bitcast.flags, bf16[512,1024]{1,0:T(8,128)(2,1)} %get-tuple-element.81.refs_0_, bf16[3,512,256]{2,1,0:T(8,128)(2,1)} %get-tuple-element.85.refs_1_, bf16[26,384,256]{2,1,0:T(8,128)(2,1)} %get-tuple-element.63.refs_3_.refs_0_.refs_4_.refs_2_.refs_8_, ...), custom_call_target="tpu_custom_call" | custom-call | flops 335544320 | bytes 1835008 | tf_op jit(solution)/shard_map/pallas_call | solution.py:101
  372.6 32.5 %psum.7 = f32[1,2,1024]{2,1,0:T(2,128)} all-reduce(f32[1,2,1024]{2,1,0:T(2,128)S(1)} %bitcast.90), channel_id=1, replica_groups=mesh['section'=2,'dp'=4,'tensor'=4] {'dp','tensor'}, use_global_device_ids=true, to_apply=%region_6.7 | all-reduce | flops 2048 | bytes 16384 | tf_op jit(solution)/shard_map/psum | solution.py:1043
  405.1 2.1 bitcast_convert_fusion
  409.9 31.4 %reduce-scatter.4.cloned.1.call-done = bf16[1,4,256,256]{3,2,1,0:T(8,128)(2,1)} async-done(((bf16[4,4,256,256]{3,2,1,0:T(8,128)(2,1)}), bf16[1,4,256,256]{3,2,1,0:T(8,128)(2,1)}) %reduce-scatter.4.cloned.1.call-update) | async-done | bytes 524304 | tf_op jit(solution)/shard_map/reduce_scatter | solution.py:893
  (118 shorter events, 42.8 us)
Async XLA Ops:
  7.2 140.2 %all-gather.3.cloned.1.call-start = ((), (), s32[]{:S(2)}) async-start(), calls=%async_computation.6 | async-start | bytes 26738688 | tf_op jit(solution)/shard_map/all_gather | solution.py:868
  12.5 392.6 %reduce-scatter.8.cloned.1.call-start = ((), (), s32[]{:S(2)}) async-start(), calls=%async_computation.5 | async-start | bytes 2621440 | tf_op jit(solution)/shard_map/reduce_scatter | solution.py:893
  12.7 20.4 %collective-permute-start.1 = (f32[128,1024]{1,0:T(8,128)S(1)}, f32[128,1024]{1,0:T(8,128)S(1)}, u32[]{:S(2)}, u32[]{:S(2)}) collective-permute-start(f32[128,1024]{1,0:T(8,128)S(1)} %bitcast.75), channel_id=1, source_target_pairs={{0,2},{1,3},{2,0},{3,1},{4,6},{5,7},{6,4},{7,5},{8,10},{9,11},{10,... | collective-permute-start | bytes 1572872 | tf_op jit(solution)/shard_map/ppermute | solution.py:841
  15.7 17.5 %collective-permute-start = (f32[128,1024]{1,0:T(8,128)S(1)}, f32[128,1024]{1,0:T(8,128)S(1)}, u32[]{:S(2)}, u32[]{:S(2)}) collective-permute-start(f32[128,1024]{1,0:T(8,128)S(1)} %bitcast.76), channel_id=1, source_target_pairs={{0,1},{1,0},{2,3},{3,2},{4,5},{5,4},{6,7},{7,6},{8,9},{9,8},{10,11... | collective-permute-start | bytes 1572872 | tf_op jit(solution)/shard_map/ppermute | solution.py:841
  33.1 1.9 collective-permute-start.2
  36.6 2.6 collective-permute-start.5
  37.6 143.1 %collective-permute-start.4 = (bf16[384,1024]{1,0:T(8,128)(2,1)S(1)}, bf16[384,1024]{1,0:T(8,128)(2,1)}, u32[]{:S(2)}, u32[]{:S(2)}) collective-permute-start(bf16[384,1024]{1,0:T(8,128)(2,1)S(1)} %bitcast.62), channel_id=1, source_target_pairs={{16,17},{17,16},{18,19},{19,18},{20,21},{21,20},{22,23},{23,22},{2... | collective-permute-start | bytes 2359304 | tf_op jit(solution)/shard_map/ppermute | solution.py:847
  39.2 135.8 %copy-start.10 = (bf16[384,1024]{1,0:T(8,128)(2,1)}, bf16[384,1024]{1,0:T(8,128)(2,1)S(1)}, u32[]{:S(2)}) copy-start(bf16[384,1024]{1,0:T(8,128)(2,1)S(1)} %collective-permute-done.5.refs_6_) | copy-start | bytes 2359300
  39.2 141.5 %collective-permute-start.6 = (bf16[384,1024]{1,0:T(8,128)(2,1)S(1)}, bf16[384,1024]{1,0:T(8,128)(2,1)}, u32[]{:S(2)}, u32[]{:S(2)}) collective-permute-start(bf16[384,1024]{1,0:T(8,128)(2,1)S(1)} %collective-permute-done.5.refs_6_), channel_id=1, source_target_pairs={{16,17},{17,16},{18,19},{19,18},{20,21},{21,20},{22,23},{23,22},{2... | collective-permute-start | bytes 2359304 | tf_op jit(solution)/shard_map/ppermute | solution.py:847
  175.0 7.9 %collective-permute-start.3 = (bf16[128,1024]{1,0:T(8,128)(2,1)}, bf16[128,1024]{1,0:T(8,128)(2,1)S(1)}, u32[]{:S(2)}, u32[]{:S(2)}) collective-permute-start(bf16[128,1024]{1,0:T(8,128)(2,1)} %get-tuple-element.51), channel_id=1, source_target_pairs={{0,16},{1,17},{2,18},{3,19},{4,20},{5,21},{6,22},{7,23},{8,24},{9,... | collective-permute-start | bytes 786440 | tf_op jit(solution)/shard_map/ppermute | solution.py:937
  188.6 8.7 %collective-permute-start.9 = (bf16[26,384,256]{2,1,0:T(8,128)(2,1)}, bf16[26,384,256]{2,1,0:T(8,128)(2,1)}, u32[]{:S(2)}, u32[]{:S(2)}) collective-permute-start(bf16[26,384,256]{2,1,0:T(8,128)(2,1)} %get-tuple-element.63.refs_3_.refs_0_.refs_4_.refs_2_.refs_8_), channel_id=1, source_target_pairs={{16,17},{17,16},{18,19},{19,18},{20,21},{21,20},{22,23},{23,22},{2... | collective-permute-start | bytes 15335432 | tf_op jit(solution)/shard_map/ppermute | solution.py:847
  191.5 5.7 %collective-permute-start.7 = (bf16[4,384,256]{2,1,0:T(8,128)(2,1)}, bf16[4,384,256]{2,1,0:T(8,128)(2,1)S(1)}, u32[]{:S(2)}, u32[]{:S(2)}) collective-permute-start(bf16[4,384,256]{2,1,0:T(8,128)(2,1)} %get-tuple-element.61.refs_2_), channel_id=1, source_target_pairs={{16,18},{17,19},{18,16},{19,17},{20,22},{21,23},{22,20},{23,21},{2... | collective-permute-start | bytes 2359304 | tf_op jit(solution)/shard_map/ppermute | solution.py:847
  192.2 5.0 %collective-permute-start.8 = (bf16[4,384,256]{2,1,0:T(8,128)(2,1)}, bf16[4,384,256]{2,1,0:T(8,128)(2,1)S(1)}, u32[]{:S(2)}, u32[]{:S(2)}) collective-permute-start(bf16[4,384,256]{2,1,0:T(8,128)(2,1)} %get-tuple-element.62.refs_4_), channel_id=1, source_target_pairs={{16,17},{17,16},{18,19},{19,18},{20,21},{21,20},{22,23},{23,22},{2... | collective-permute-start | bytes 2359304 | tf_op jit(solution)/shard_map/ppermute | solution.py:847
  197.3 46.3 %collective-permute-start.10 = (bf16[128,1024]{1,0:T(8,128)(2,1)}, bf16[128,1024]{1,0:T(8,128)(2,1)S(1)}, u32[]{:S(2)}, u32[]{:S(2)}) collective-permute-start(bf16[128,1024]{1,0:T(8,128)(2,1)} %get-tuple-element.65), channel_id=1, source_target_pairs={{16,0},{17,1},{18,2},{19,3},{20,4},{21,5},{22,6},{23,7},{24,8},{25... | collective-permute-start | bytes 786440 | tf_op jit(solution)/shard_map/ppermute | solution.py:961
  243.6 11.1 %collective-permute-start.12 = (bf16[2,3,384,256]{3,2,1,0:T(8,128)(2,1)S(1)}, bf16[2,3,384,256]{3,2,1,0:T(8,128)(2,1)S(1)}, u32[]{:S(2)}, u32[]{:S(2)}) collective-permute-start(bf16[2,3,384,256]{3,2,1,0:T(8,128)(2,1)S(1)} %copy-done.22), channel_id=1, source_target_pairs={{16,17},{17,16},{18,19},{19,18},{20,21},{21,20},{22,23},{23,22},{2... | collective-permute-start | bytes 3538952 | tf_op jit(solution)/shard_map/ppermute | solution.py:847
  244.4 19.7 %collective-permute-start.18 = (bf16[4,384,256]{2,1,0:T(8,128)(2,1)}, bf16[4,384,256]{2,1,0:T(8,128)(2,1)S(1)}, u32[]{:S(2)}, u32[]{:S(2)}) collective-permute-start(bf16[4,384,256]{2,1,0:T(8,128)(2,1)} %copy-done.23), channel_id=1, source_target_pairs={{16,18},{17,19},{18,16},{19,17},{20,22},{21,23},{22,20},{23,21},{2... | collective-permute-start | bytes 2359304 | tf_op jit(solution)/shard_map/ppermute | solution.py:847
  245.1 15.4 %collective-permute-start.11 = (bf16[128,1024]{1,0:T(8,128)(2,1)S(1)}, bf16[128,1024]{1,0:T(8,128)(2,1)S(1)}, u32[]{:S(2)}, u32[]{:S(2)}) collective-permute-start(bf16[128,1024]{1,0:T(8,128)(2,1)S(1)} %collective-permute-done.10), channel_id=1, source_target_pairs={{0,2},{1,3},{2,0},{3,1},{4,6},{5,7},{6,4},{7,5},{8,10},{9,11},{10,... | collective-permute-start | bytes 786440 | tf_op jit(solution)/shard_map/ppermute | solution.py:847
  248.5 14.4 %collective-permute-start.14 = (bf16[128,1024]{1,0:T(8,128)(2,1)S(1)}, bf16[128,1024]{1,0:T(8,128)(2,1)S(1)}, u32[]{:S(2)}, u32[]{:S(2)}) collective-permute-start(bf16[128,1024]{1,0:T(8,128)(2,1)S(1)} %collective-permute-done.10), channel_id=1, source_target_pairs={{0,1},{1,0},{2,3},{3,2},{4,5},{5,4},{6,7},{7,6},{8,9},{9,8},{10,11... | collective-permute-start | bytes 786440 | tf_op jit(solution)/shard_map/ppermute | solution.py:847
  260.5 3.6 collective-permute-start.15
  271.9 135.3 %reduce-scatter.6.cloned.1.call-start = ((), (), s32[]{:S(2)}) async-start(), calls=%async_computation.4 | async-start | bytes 2621440 | tf_op jit(solution)/shard_map/reduce_scatter | solution.py:893
  273.4 35.8 %collective-permute-start.16 = (bf16[4,4,256,256]{3,2,1,0:T(8,128)(2,1)S(1)}, bf16[4,4,256,256]{3,2,1,0:T(8,128)(2,1)}, u32[]{:S(2)}, u32[]{:S(2)}) collective-permute-start(bf16[4,4,256,256]{3,2,1,0:T(8,128)(2,1)S(1)} %copy-done.7), channel_id=1, source_target_pairs={{16,18},{17,19},{18,16},{19,17},{20,22},{21,23},{22,20},{23,21},{2... | collective-permute-start | bytes 6291464 | tf_op jit(solution)/shard_map/ppermute | solution.py:847
  315.7 125.6 %reduce-scatter.4.cloned.1.call-start = ((), (), s32[]{:S(2)}) async-start(), calls=%async_computation.3 | async-start | bytes 2621440 | tf_op jit(solution)/shard_map/reduce_scatter | solution.py:893
  317.3 43.9 %collective-permute-start.17 = (bf16[4,4,256,256]{3,2,1,0:T(8,128)(2,1)S(1)}, bf16[4,4,256,256]{3,2,1,0:T(8,128)(2,1)S(1)}, u32[]{:S(2)}, u32[]{:S(2)}) collective-permute-start(bf16[4,4,256,256]{3,2,1,0:T(8,128)(2,1)S(1)} %copy-done.6), channel_id=1, source_target_pairs={{16,18},{17,19},{18,16},{19,17},{20,22},{21,23},{22,20},{23,21},{2... | collective-permute-start | bytes 6291464 | tf_op jit(solution)/shard_map/ppermute | solution.py:847
  318.1 43.1 %collective-permute-start.13 = (bf16[3,128,1024]{2,1,0:T(8,128)(2,1)}, bf16[3,128,1024]{2,1,0:T(8,128)(2,1)S(1)}, u32[]{:S(2)}, u32[]{:S(2)}) collective-permute-start(bf16[3,128,1024]{2,1,0:T(8,128)(2,1)} %get-tuple-element.75), channel_id=1, source_target_pairs={{16,0},{17,1},{18,2},{19,3},{20,4},{21,5},{22,6},{23,7},{24,8},{25... | collective-permute-start | bytes 2359304 | tf_op jit(solution)/shard_map/ppermute | solution.py:985
  (23 other events, 119.1 us)
Sparse Core Ops, SparseCore 0:
  12.6 134.7 all-gather.2
  272.0 51.9 reduce-scatter.7
  326.4 55.7 reduce-scatter.5
  384.3 57.0 reduce-scatter.3

commit v3 on v2

--- a/solution.py
+++ b/solution.py
@@ -18,6 +18,7 @@
 VMEM = 60 * 1024 * 1024
 ACTIVE = 4
 COST = 8
+LONG = 10**11
 
 
 def mm(left, right):
@@ -162,7 +163,7 @@
         ref[pl.ds(at, F)] = value[i * F : (i + 1) * F]
 
 
-def frames_fwd_body(own, order, s_ref, wa_ref, wb_ref, gain_ref, bias_ref, nin_ref, proj_ref, mixed_ref, hid_ref, nmid_ref, act_ref, slope_ref, out_ref, held, acc, acts, sems):
+def frames_fwd_body(own, order, s_ref, wa_ref, gain_ref, bias_ref, nin_ref, proj_ref, mixed_ref, hid_ref, nmid_ref, act_ref, slope_ref, held, acts, sems):
     g = pl.program_id(0)
     T = pl.num_programs(0) // 2
     R, N = bias_ref.shape[:2]
@@ -193,41 +194,31 @@
     @pl.when(g == T)
     def _():
         nmid_ref[...] = normed(hid_ref[...], gain_ref[1:2])
-        acc[...] = hid_ref[: R * own]
 
     @pl.when(g >= T)
     def _():
-        mine = []
         for j in range(4):
             act, slope = gelu_pair(mm(nmid_ref[...], deep(wa_ref, j)))
             slope_ref[0, j] = slope.astype(BF16)
-            act = act.astype(BF16)
-            acts[jnp.minimum(g - T, 1), j] = act
-            mine.append(act[: R * own])
-        mine = jnp.concatenate(mine, axis=1)
-        for z in range(nz):
-            acc[:, z * BLK : (z + 1) * BLK] += mm(mine, wb_ref[z, 0].reshape(-1, BLK))
+            acts[jnp.minimum(g - T, 1), j] = act.astype(BF16)
 
     store_out(g, T, acts, sems, [act_ref])
 
     @pl.when(g == 2 * T - 1)
     def _():
-        out_ref[...] = acc[...].astype(BF16)
         stored(acts, sems, [act_ref])
 
 
 def frames_fwd(order, s, W, gain, bias, own):
     rows, D = s.shape
     T = W.shape[1]
-    R = bias.shape[0]
     return call(
         functools.partial(frames_fwd_body, own),
         order,
-        (s, W, W, gain, bias),
+        (s, W, gain, bias),
         [
             whole(s.shape),
             weight_spec(W, lambda g: (g % T, g // T)),
-            weight_spec(W, lambda g: (jnp.maximum(g - T, 0), 2)),
             whole(gain.shape),
             whole(bias.shape),
         ],
@@ -239,7 +230,6 @@
             struct((rows, D), BF16),
             struct((4, rows, BLK), BF16),
             struct((T, 4, rows, BLK), BF16),
-            struct((R * own, D), BF16),
         ),
         (
             whole((rows, D)),
@@ -249,12 +239,10 @@
             whole((rows, D)),
             HBM_REF,
             pl.BlockSpec((1, 4, rows, BLK), lambda g, order: (jnp.maximum(g - T, 0) * order[ACTIVE], 0, 0, 0)),
-            whole((R * own, D)),
         ),
         2 * T,
         (
             pltpu.VMEM((rows, BLK), BF16),
-            pltpu.VMEM((R * own, D), F32),
             pltpu.VMEM((2, 4, rows, BLK), BF16),
             pltpu.SemaphoreType.DMA((1,)),
         ),
@@ -263,11 +251,93 @@
     )
 
 
-def frames_bwd_body(own, order, gy_ref, hid_ref, slope_ref, wa_ref, wb_ref, gain_ref, proj_ref, bias_ref, s_ref, gpre_ref, branch_ref, gproj_ref, frame_ref, gg_ref, held, acc, acc_in, ghid, pres, gmix, sems):
+def frames_own_body(own, order, s_ref, wa_ref, wb_ref, gain_ref, bias_ref, out_ref, nin, keys, values, held, hid, nmid):
     g = pl.program_id(0)
     T = pl.num_programs(0) // 2
     R, N = bias_ref.shape[:2]
     nz = wa_ref.shape[0]
+    mine = R * own
+
+    @pl.when(g == 0)
+    def _():
+        nin[...] = normed(s_ref[...], gain_ref[0:1])
+        hid[...] = s_ref[:mine]
+
+    @pl.when(g < T)
+    def _():
+        queries = mm(nin[:mine], deep(wa_ref, 0)).astype(BF16)
+        keys[...] = mm(nin[...], deep(wa_ref, 1)).astype(BF16)
+        values[...] = mm(nin[...], deep(wa_ref, 2)).astype(BF16)
+        masks = head_masks((own, BLK))
+        for r in range(R):
+            q4 = spread(queries[r * own : (r + 1) * own], masks)
+            p = head_weights(q4, pick(keys, r, R, own), bias_ref[r, :own])
+            mixed = gathered(mm(p.astype(BF16), pick(values, r, R, own)), masks)
+            held[r * own : (r + 1) * own] = mixed.astype(BF16)
+        for z in range(nz):
+            hid[:, z * BLK : (z + 1) * BLK] += mm(held[...], wa_ref[z, 0, 3])
+
+    @pl.when(g == T)
+    def _():
+        nmid[...] = normed(hid[...], gain_ref[1:2])
+
+    @pl.when(g >= T)
+    def _():
+        act = [gelu_pair(mm(nmid[...], deep(wa_ref, j)))[0].astype(BF16) for j in range(4)]
+        act = jnp.concatenate(act, axis=1)
+        for z in range(nz):
+            hid[:, z * BLK : (z + 1) * BLK] += mm(act, wb_ref[z, 0].reshape(-1, BLK))
+
+    @pl.when(g == 2 * T - 1)
+    def _():
+        out_ref[...] = hid[...].astype(BF16)
+
+
+def frames_own(order, s, W, gain, bias, own):
+    rows, D = s.shape
+    T = W.shape[1]
+    mine = bias.shape[0] * own
+    return call(
+        functools.partial(frames_own_body, own),
+        order,
+        (s, W, W, gain, bias),
+        [
+            whole(s.shape),
+            weight_spec(W, lambda g: (g % T, g // T)),
+            weight_spec(W, lambda g: (jnp.maximum(g - T, 0), 2)),
+            whole(gain.shape),
+            whole(bias.shape),
+        ],
+        struct((mine, D), BF16),
+        whole((mine, D)),
+        2 * T,
+        (
+            pltpu.VMEM((rows, D), BF16),
+            pltpu.VMEM((rows, BLK), BF16),
+            pltpu.VMEM((rows, BLK), BF16),
+            pltpu.VMEM((mine, BLK), BF16),
+            pltpu.VMEM((mine, D), F32),
+            pltpu.VMEM((mine, D), BF16),
+        ),
+        flops=2 * mine * D * 12 * D,
+        moved=24 * D * D,
+    )
+
+
+def frames_bwd_body(own, order, gy_ref, hid_ref, slope_ref, wa_ref, wb_ref, gain_ref, proj_ref, bias_ref, s_ref, gpre_ref, branch_ref, gproj_ref, frame_ref, gg_ref, held, acc, acc_in, ghid, pres, gmix, sems, hid_at, s_at, bias_at):
+    g = pl.program_id(0)
+    late = [
+        pltpu.make_async_copy(a, b, sems.at[1 + i])
+        for i, (a, b) in enumerate([(hid_ref, hid_at), (s_ref, s_at), (bias_ref, bias_at)])
+    ]
+    T = pl.num_programs(0) // 2
+    R, N = bias_ref.shape[:2]
+    nz = wa_ref.shape[0]
+
+    @pl.when(g == 0)
+    def _():
+        for copy in late:
+            copy.start()
 
     @pl.when(g < T)
     def _():
@@ -285,9 +355,11 @@
 
     @pl.when(g == T - 1)
     def _():
-        back, _ = norm_back(hid_ref[...], gain_ref[1:2], acc[...])
+        for copy in late:
+            copy.wait()
+        back, _ = norm_back(hid_at[...], gain_ref[1:2], acc[...])
         branch_ref[...] = (gy_ref[...].astype(F32) + back).astype(BF16)
-        back_own, gg = norm_back(hid_ref[: R * own], gain_ref[1:2], acc[: R * own])
+        back_own, gg = norm_back(hid_at[: R * own], gain_ref[1:2], acc[: R * own])
         gg_ref[1:2] = gg
         ghid[...] = gy_ref[: R * own].astype(F32) + back_own
 
@@ -299,7 +371,7 @@
         for r in range(R):
             q, k, v = (pick(proj_ref.at[0, i], r, R, own) for i in range(3))
             q4 = spread(q, masks)
-            p = head_weights(q4, k, bias_ref[r])
+            p = head_weights(q4, k, bias_at[r])
             gm4 = spread(pick(gmix, r, R, own), masks)
             ga = mm_t(gm4, v)
             gs = (SCALE * p * (ga - jnp.sum(p * ga, axis=-1, keepdims=True))).astype(BF16)
@@ -319,7 +391,7 @@
 
     @pl.when(g == 2 * T - 1)
     def _():
-        back, gg = norm_back(s_ref[: R * own], gain_ref[0:1], acc_in[...])
+        back, gg = norm_back(s_at[...], gain_ref[0:1], acc_in[...])
         gg_ref[0:1] = gg
         frame_ref[...] = ghid[...] + back
         stored(pres, sems, [gpre_ref])
@@ -335,14 +407,14 @@
         (gy, hid, slope, W, W, gain, proj, bias, s),
         [
             whole(gy.shape),
-            whole(hid.shape),
+            HBM_REF,
             pl.BlockSpec((1, 4, rows, BLK), lambda g, order: (jnp.minimum(g, T - 1) * order[ACTIVE], 0, 0, 0)),
             weight_spec(W, lambda g: (g % T, 1 - g // T)),
             weight_spec(W, lambda g: (jnp.minimum(g, T - 1), 2)),
             whole(gain.shape),
             pl.BlockSpec((1, 3, rows, BLK), lambda g, order: (jnp.maximum(g - T, 0) * order[ACTIVE], 0, 0, 0)),
-            whole(bias.shape),
-            whole(s.shape),
+            HBM_REF,
+            HBM_REF,
         ],
         (
             struct((4, rows, BLK), BF16),
@@ -366,7 +438,10 @@
             pltpu.VMEM((R * own, D), F32),
             pltpu.VMEM((2, 4, rows, BLK), BF16),
             pltpu.VMEM((rows, BLK), BF16),
-            pltpu.SemaphoreType.DMA((1,)),
+            pltpu.SemaphoreType.DMA((4,)),
+            pltpu.VMEM((rows, D), F32),
+            pltpu.VMEM((R * own, D), F32),
+            pltpu.VMEM(bias.shape, F32),
         ),
         flops=2 * rows * D * 14 * D,
         moved=24 * D * D + rows * D * 30,
@@ -784,7 +859,7 @@
 
 def grads(flag, nz, parts, received=None):
     inputs, specs, plan = [], [], []
-    begin = flops = moved = 0
+    begin = 0
     for by_rows, count, ones, zeros in parts:
         for wide, narrow, base, *more in ones + zeros:
             if isinstance(wide, tuple):
@@ -807,8 +882,6 @@
                 )
             )
             inputs += [wide, narrow]
-            flops += rows * nz * BLK * BLK * count
-            moved += 4 * rows * nz * BLK
         plan.append((by_rows, begin, begin + count, len(ones), len(zeros)))
         begin += count
     turns = []
@@ -831,8 +904,7 @@
         block,
         begin,
         turns,
-        flops=2 * flops,
-        moved=moved + nz * begin * BLK * BLK * 4,
+        flops=COST * (LONG if received is not None else 10**9),
     )
 
 
@@ -853,6 +925,14 @@
 
 def after(value, *others):
     return together(value, *others)[0]
+
+
+def pack_body(qkv_ref, out_ref, up_ref, down_ref, flat_ref):
+    flat_ref[0:3] = qkv_ref[...]
+    flat_ref[3] = out_ref[...]
+    for j in range(4):
+        flat_ref[4 + j] = up_ref[:, j * BLK : (j + 1) * BLK]
+    flat_ref[8:12] = down_ref[...]
 
 
 def gather_weights(w_qkv, w_out, w_up, w_down):
@@ -861,10 +941,10 @@
     slices = lax.axis_size("tensor")
     both = ("dp", "tensor")
     if depth == BLK:
-        up_blocks = [w_up[None, :, i : i + BLK] for i in range(0, w_up.shape[1], BLK)]
-        flat = jnp.concatenate(
-            [w_qkv, w_out[None], *up_blocks, w_down.reshape(-1, BLK, BLK)], axis=0
-        )
+        flat = pl.pallas_call(
+            pack_body,
+            out_shape=struct((12, BLK, BLK), BF16),
+        )(w_qkv, w_out, w_up, w_down.reshape(-1, BLK, BLK))
         out = lax.all_gather(flat, both)
         return out.reshape(shards, slices, *flat.shape)
     per = BLK // depth
@@ -933,17 +1013,18 @@
     allowed = (pos[:, None] >= pos[None, :])[None] & (seg[:, :, None] == seg[:, None, :])
     bias = jnp.where(allowed, 0.0, NEG).astype(F32)
 
-    n_in0, proj0, mixed0, hid0, n_mid0, act0, slope0, out0 = frames_fwd(order0, s0, W, gain, bias, F)
+    out0 = frames_own(order0, s0, W, gain, bias, F)
     sent = lax.ppermute(out0, "section", [(0, 1)])
+    s0 = after(s0, out0)
+    n_in0, proj0, mixed0, hid0, n_mid0, act0, slope0 = frames_fwd(order0, s0, W, gain, bias, F)
 
     def swap1(value, bit):
         return swap_in(value, 1, bit)
 
     gact1 = codes_gact(order1, cot, W)
-    late = after(cot, s0)
-    cot_y = swap1(late, 2)
-    cot_s, cot_d = swap1(late, 1), swap1(cot_y, 1)
-    sent = after(sent, cot_s, cot_d)
+    cot_y = swap1(after(cot, out0), 2)
+    cot_s = swap1(after(cot, out0), 1)
+    sent, gact1, cot_y, cot_s, proj0 = together(sent, gact1, cot_y, cot_s, proj0)
     proj1, hid1, ghid1, gg_mid1, own1, act_far, act_other, bundle = codes_fwd(
         order1, codes_t, sent, cot, gact1, W, gain
     )
@@ -960,29 +1041,16 @@
 
     gsent = lax.ppermute(gsent, "section", [(1, 0)])
     act_d = swap1(act_o, 2)
-    out1 = codes_out(order1, hid1, [own1, act_far, bundle, act_other], W, C)
-    gsent, out1 = together(gsent, out1)
-    gfar = swap_in(gsent, 0, 2)
+    cot_d = swap1(after(cot_y, act_o), 1)
 
     M1 = C * M
     gproj1 = gproj1.reshape(-1, M1, BLK)
-    bundle_s = after(bundle_s, gsent)
-    gproj1_s = swap1(after(gproj1_s, gsent), 1).reshape(-1, M1, BLK)
     up_far = grads(
         flag, nz, [(True, 4, [], [((bundle, 16), own1, 8), ((bundle_s, 16), bundle_s, 8)])]
     )
     up_got = swap1(up_far, 2)
-    att_far = grads(
-        flag,
-        nz,
-        [
-            (True, 3, [], [((bundle, 12), gproj1, 3), ((bundle_s, 12), gproj1_s, 3)]),
-            (False, 1, [], [((bundle, 20), own1, 13), ((bundle_s, 20), bundle_s, 25)]),
-        ],
-    )
-    gfar, up_far, att_far = together(gfar, up_far, att_far)
-    att_got = swap1(att_far, 2)
-    glocal = lax.ppermute(after(glocal, gfar), "section", [(1, 0)])
+    gsent, _, act_d, cot_d = together(gsent, up_far, act_d, cot_d)
+    gfar = swap_in(gsent, 0, 2)
     gy0 = jnp.concatenate(
         [gsent, swap_in(gsent, 0, 1), gfar, swap_in(gfar, 0, 1)], axis=0
     )
@@ -1000,10 +1068,24 @@
         ],
     )
     down_part = scatter_blocks(down_total, 0)[1]
-
+    hid0 = after(hid0, down_total)
     gpre0, branch0, gproj0, frame, gg0 = frames_bwd(
-        order0, gy0, hid0, slope0, W, gain, proj0, bias, s0, F
-    )
+        order0, gy0, hid0, slope0, W, gain, proj0, bias, frame_own, F
+    )
+    gproj1, gproj1_s = together(gproj1, gproj1_s, down_total)[:2]
+    gproj1_s = swap1(gproj1_s, 1).reshape(-1, M1, BLK)
+    att_far = grads(
+        flag,
+        nz,
+        [
+            (True, 3, [], [((bundle, 12), gproj1, 3), ((bundle_s, 12), gproj1_s, 3)]),
+            (False, 1, [], [((bundle, 20), own1, 13), ((bundle_s, 20), bundle_s, 25)]),
+        ],
+    )
+    att_got = swap1(att_far, 2)
+    hid1, glocal = together(hid1, glocal, att_far)[:2]
+    glocal = lax.ppermute(glocal, "section", [(1, 0)])
+    out1 = codes_out(order1, hid1, [own1, act_far, bundle, act_other], W, C)
     up_total = grads(
         flag,
         nz,
@@ -1018,7 +1100,7 @@
         up_got,
     )
     up_part = scatter_blocks(up_total, 4)[0]
-    gproj0 = after(gproj0, up_total, glocal)
+    gproj0, out1 = together(gproj0, out1, up_total, glocal)[:2]
     att_total = grads(
         flag,
         nz,

time: 453 us -> 416 us (0.918)
  waiting for transfers between devices: 241 us -> 191 us
  Pallas kernels: 108 us -> 124 us
  local copies, waits for them, and re-layouts: 17.5 us -> 9.02 us
    ppermute x1, waiting for transfers between devices: 41.8 us -> 9.1 us  [on_device(): glocal = lax.ppermute(glocal, 'section', [(1, 0)])]
    ppermute x1, waiting for transfers between devices: 40.4 us -> 21.6 us  [on_device(): gsent = lax.ppermute(gsent, 'section', [(1, 0)])]
    pallas_call x11 -> x12, Pallas kernels: 108 us -> 122 us  [call(): pl.pallas_call(run, out_shape=outs, grid_spec=pltpu.PrefetchScalarGridSpe...]
    unnamed x58 -> x42, local copies, waits for them, and re-layouts: 15.1 us -> 6.61 us
    all_gather x1, waiting for transfers between devices: 105 us -> 110 us  [gather_weights(): out = lax.all_gather(flat, both)]
  transfers between devices with their start and end apart: 23 -> 23, of which waited for: 8 -> 8; matrix products, arithmetic and copies ran while one was open for 2% -> 3% of each run, Pallas kernels for 21% -> 24%
where the time goes in v3:
time: 416 us; the launch traced here: 411 us
  waiting for transfers between devices  191 us (46%)
  Pallas kernels  124 us (30%)
  blocking collectives  34.7 us (8%)
  starting transfers between devices  25.8 us (6%)
  between operations  14.5 us (3%)
  other arithmetic  11.9 us (3%)
  local copies, waits for them, and re-layouts  9.02 us (2%)
    pallas_call x12, Pallas kernels, call(): pl.pallas_call(run, out_shape=outs, grid_spec=pltpu.PrefetchScalarGridSpe...  122 us
    all_gather x1, waiting for transfers between devices, gather_weights(): out = lax.all_gather(flat, both)  110 us
    psum x1, blocking collectives, on_device(): grad_gains = lax.psum(after(gain_part, att_total), ('dp', 'tensor'))  34.7 us
    reduce_scatter x3, waiting for transfers between devices, scatter_blocks(): out = lax.psum_scatter(parts, 'dp', scatter_dimension=0, tiled=False)  28.2 us
    ppermute x1, waiting for transfers between devices, on_device(): gsent = lax.ppermute(gsent, 'section', [(1, 0)])  21.6 us
    ppermute x13, starting transfers between devices, swap_in(): return lax.ppermute(value, ('section', 'tensor'), pairs)  17.7 us
    ppermute x3, waiting for transfers between devices, swap(): return lax.ppermute(value, axis, [(i, i ^ bit) for i in range(count)])  17 us
    ppermute x1, waiting for transfers between devices, on_device(): glocal = lax.ppermute(glocal, 'section', [(1, 0)])  9.1 us
  transfers between devices with their start and end apart: 23, of which 8 were waited for; matrix products, arithmetic and copies ran while one was open for 3% of the time, Pallas kernels for 24%

profile of v3, /device:TPU:0, one launch (start us, length us, event | category | flops | bytes accessed | tf_op | source)
XLA Modules:
  0.0 411.0 jit_solution(6028245357668262833)
XLA Ops:
  7.2 2.7 shard_map.136
  10.2 3.0 collective-permute-start.1
  13.7 16.9 %collective-permute-done.1 = f32[128,1024]{1,0:T(8,128)S(1)} collective-permute-done((f32[128,1024]{1,0:T(8,128)S(1)}, f32[128,1024]{1,0:T(8,128)S(1)}, u32[]{:S(2)}, u32[]{:S(2)}) %collective-permute-start.1) | collective-permute-done | bytes 524320 | tf_op jit(solution)/shard_map/ppermute | solution.py:913
  32.5 2.6 pad_maximum_fusion.refs_0_
  35.1 109.8 %all-gather.3.cloned.1.call-done = bf16[192,256,256]{2,1,0:T(8,128)(2,1)} async-done(((bf16[12,256,256]{2,1,0:T(8,128)(2,1)}), bf16[192,256,256]{2,1,0:T(8,128)(2,1)}) %all-gather.3.cloned.1.call-update) | async-done | bytes 25165840 | tf_op jit(solution)/shard_map/all_gather | solution.py:948
  144.9 17.3 %shard_map.137 = bf16[128,1024]{1,0:T(8,128)(2,1)} custom-call(s32[5]{0:T(128)} %get-tuple-element.129.flags, f32[512,1024]{1,0:T(8,128)} %pad_maximum_fusion.refs_0_, bf16[4,4,12,256,256]{4,3,2,1,0:T(8,128)(2,1)} %bitcast.37, bf16[4,4,12,256,256]{4,3,2,1,0:T(8,128)(2,1)} %bitcast.38, f32[2,1024]{1,0:T(2,128)} %bitcast.69, ...), custom_call_target="tpu_custom_call" | custom-call | flops 402653184 | bytes 3145728 | tf_op jit(solution)/shard_map/pallas_call | solution.py:102
  167.3 3.3 shard_map.138.refs_3_
  170.6 25.3 %shard_map.139 = (bf16[512,1024]{1,0:T(8,128)(2,1)}, bf16[4,3,512,256]{3,2,1,0:T(8,128)(2,1)}, bf16[512,256]{1,0:T(8,128)(2,1)}, f32[512,1024]{1,0:T(8,128)}, bf...) custom-call(s32[5]{0:T(128)} %get-tuple-element.129.flags, ...), custom_call_target="tpu_custom_call" | custom-call | flops 1342177280 | bytes 5111808 | tf_op jit(solution)/shard_map/pallas_call | solution.py:102
  196.6 5.0 %shard_map.140 = (bf16[4,3,384,256]{3,2,1,0:T(8,128)(2,1)}, f32[384,1024]{1,0:T(8,128)}, f32[384,1024]{1,0:T(8,128)}, f32[1,1024]{1,0:T(1,128)}, bf16[14,384,256...) custom-call(s32[5]{0:T(128)} %get-tuple-element.128.flags, ...), custom_call_target="tpu_custom_call" | custom-call | flops 1207959552 | bytes 4063232 | tf_op jit(solution)/shard_map/pallas_call | solution.py:102
  201.6 2.9 collective-permute-start.8
  206.1 4.3 %shard_map.141 = (bf16[2,3,384,256]{3,2,1,0:T(8,128)(2,1)}, bf16[2,3,384,256]{3,2,1,0:T(8,128)(2,1)}, bf16[3,128,1024]{2,1,0:T(8,128)(2,1)}, bf16[128,1024]{1,0:T(8,128)(2,1)}, f32[1,1024]{1,0:T(1,128)}) custom-call(s32[5]{0:T(128)} %get-tuple-element.128.flags, bf16[4,3,384,256]{3,2,1,0:T(8,128)(2,1)} %get-tuple-element.64.refs_0_, ...), custom_call_target="tpu_custom_call" | custom-call | flops 402653184 | bytes 2031616 | tf_op jit(solution)/shard_map/pallas_call | solution.py:102
  213.2 4.2 %shard_map.142 = bf16[4,4,256,256]{3,2,1,0:T(8,128)(2,1)} custom-call(s32[1]{0:T(128)} %bitcast.flags, bf16[26,384,256]{2,1,0:T(8,128)(2,1)} %get-tuple-element.73.refs_0_.refs_4_.refs_3_.refs_2_.refs_8_, bf16[14,384,256]{2,1,0:T(8,128)(2,1)} %get-tuple-element.78.refs_1_.refs_3_.refs_5_.refs_9_, ...), custom_call_target="tpu_custom_call" | custom-call | flops 1000000000 | tf_op jit(solution)/shard_map/pallas_call | solution.py:102
  217.4 21.6 %collective-permute-done.9 = bf16[128,1024]{1,0:T(8,128)(2,1)S(1)} collective-permute-done((bf16[128,1024]{1,0:T(8,128)(2,1)}, bf16[128,1024]{1,0:T(8,128)(2,1)S(1)}, u32[]{:S(2)}, u32[]{:S(2)}) %collective-permute-start.9) | collective-permute-done | bytes 262176 | tf_op jit(solution)/shard_map/ppermute | solution.py:1042
  239.1 2.2 collective-permute-start.13
  245.3 3.6 collective-permute-done.13
  253.3 6.6 %shard_map.143 = bf16[4,4,256,256]{3,2,1,0:T(8,128)(2,1)} custom-call(s32[1]{0:T(128)} %bitcast.flags, bf16[512,1024]{1,0:T(8,128)(2,1)} %copy-done.1, bf16[4,512,256]{2,1,0:T(8,128)(2,1)} %get-tuple-element.84.refs_1_, bf16[384,1024]{1,0:T(8,128)(2,1)} %bitcast.50, bf16[14,384,256]{2,1,0:T(8,128)(2,1)} %get-tuple-element.78.refs_1_.refs_3_.refs_5_.refs_9_, ...), custom_call_target="tpu_custom_call" | custom-call | flops 1000000000 | tf_op jit(solution)/shard_map/pallas_call | solution.py:102
  260.9 32.4 %shard_map.145 = (bf16[4,512,256]{2,1,0:T(8,128)(2,1)}, bf16[512,1024]{1,0:T(8,128)(2,1)}, bf16[3,512,256]{2,1,0:T(8,128)(2,1)}, f32[128,1024]{1,0:T(8,128)}, f32[2,1024]{1,0:T(2,128)}) custom-call(s32[5]{0:T(128)} %get-tuple-element.129.flags, bf16[512,1024]{1,0:T(8,128)(2,1)} %copy-done.1, f32[512,1024]{1,0:T(8,128)} %get-tuple-element.93.refs_1_, ...), custom_call_target="tpu_custom_call" | custom-call | flops 1879048192 | bytes 5111808 | tf_op jit(solution)/shard_map/pallas_call | solution.py:102
  294.3 4.7 %shard_map.144 = bf16[4,4,256,256]{3,2,1,0:T(8,128)(2,1)} custom-call(s32[1]{0:T(128)} %bitcast.flags, bf16[26,384,256]{2,1,0:T(8,128)(2,1)} %get-tuple-element.73.refs_0_.refs_4_.refs_3_.refs_2_.refs_8_, bf16[6,384,256]{2,1,0:T(8,128)(2,1)} %bitcast.60, ...), custom_call_target="tpu_custom_call" | custom-call | flops 1000000000 | tf_op jit(solution)/shard_map/pallas_call | solution.py:102
  301.1 6.4 %shard_map.147 = bf16[4,4,256,256]{3,2,1,0:T(8,128)(2,1)} custom-call(s32[1]{0:T(128)} %bitcast.flags, bf16[512,1024]{1,0:T(8,128)(2,1)} %get-tuple-element.99.refs_0_, bf16[4,512,256]{2,1,0:T(8,128)(2,1)} %get-tuple-element.100.refs_1_, bf16[26,384,256]{2,1,0:T(8,128)(2,1)} %get-tuple-element.73.refs_0_.refs_4_.refs_3_.refs_2_.refs_8_, ...), custom_call_target="tpu_custom_call" | custom-call | flops 99999997952 | tf_op jit(solution)/shard_map/pallas_call | solution.py:102
  307.8 4.5 %shard_map.146 = bf16[3,128,1024]{2,1,0:T(8,128)(2,1)} custom-call(s32[5]{0:T(128)} %get-tuple-element.128.flags, f32[384,1024]{1,0:T(8,128)} %get-tuple-element.98.refs_0_, bf16[14,384,256]{2,1,0:T(8,128)(2,1)} %get-tuple-element.78.refs_1_.refs_3_.refs_5_.refs_9_, bf16[4,384,256]{2,1,0:T(8,128)(2,1)} %get-tuple-element.71.refs_2_, ...), custom_call_target="tpu_custom_call" | custom-call | flops 402653184 | bytes 1736704 | tf_op jit(solution)/shard_map/pallas_call | solution.py:102
  312.4 9.1 %collective-permute-done.16 = bf16[3,128,1024]{2,1,0:T(8,128)(2,1)S(1)} collective-permute-done((bf16[3,128,1024]{2,1,0:T(8,128)(2,1)}, bf16[3,128,1024]{2,1,0:T(8,128)(2,1)S(1)}, u32[]{:S(2)}, u32[]{:S(2)}) %collective-permute-start.16) | collective-permute-done | bytes 786464 | tf_op jit(solution)/shard_map/ppermute | solution.py:1087
  322.9 7.4 %shard_map.148 = bf16[4,4,256,256]{3,2,1,0:T(8,128)(2,1)} custom-call(s32[1]{0:T(128)} %bitcast.flags, bf16[512,1024]{1,0:T(8,128)(2,1)} %get-tuple-element.102.refs_0_, bf16[3,512,256]{2,1,0:T(8,128)(2,1)} %get-tuple-element.103.refs_1_, bf16[26,384,256]{2,1,0:T(8,128)(2,1)} %get-tuple-element.73.refs_0_.refs_4_.refs_3_.refs_2_.refs_8_, ...), custom_call_target="tpu_custom_call" | custom-call | flops 99999997952 | tf_op jit(solution)/shard_map/pallas_call | solution.py:102
  332.9 34.7 %psum.7 = f32[1,2,1024]{2,1,0:T(2,128)} all-reduce(f32[1,2,1024]{2,1,0:T(2,128)S(1)} %bitcast.75), channel_id=1, replica_groups=mesh['section'=2,'dp'=4,'tensor'=4] {'dp','tensor'}, use_global_device_ids=true, to_apply=%region_6.7 | all-reduce | flops 2048 | bytes 16384 | tf_op jit(solution)/shard_map/psum | solution.py:1125
  372.5 28.2 %reduce-scatter.4.cloned.1.call-done = bf16[1,4,256,256]{3,2,1,0:T(8,128)(2,1)} async-done(((bf16[4,4,256,256]{3,2,1,0:T(8,128)(2,1)}), bf16[1,4,256,256]{3,2,1,0:T(8,128)(2,1)}) %reduce-scatter.4.cloned.1.call-update) | async-done | bytes 524304 | tf_op jit(solution)/shard_map/reduce_scatter | solution.py:973
  (103 shorter events, 37.7 us)
Async XLA Ops:
  7.2 137.7 %all-gather.3.cloned.1.call-start = ((), (), s32[]{:S(2)}) async-start(), calls=%async_computation.6 | async-start | bytes 26738688 | tf_op jit(solution)/shard_map/all_gather | solution.py:948
  10.0 357.6 %reduce-scatter.8.cloned.1.call-start = ((), (), s32[]{:S(2)}) async-start(), calls=%async_computation.5 | async-start | bytes 2621440 | tf_op jit(solution)/shard_map/reduce_scatter | solution.py:973
  10.2 20.4 %collective-permute-start.1 = (f32[128,1024]{1,0:T(8,128)S(1)}, f32[128,1024]{1,0:T(8,128)S(1)}, u32[]{:S(2)}, u32[]{:S(2)}) collective-permute-start(f32[128,1024]{1,0:T(8,128)S(1)} %bitcast.53), channel_id=1, source_target_pairs={{0,2},{1,3},{2,0},{3,1},{4,6},{5,7},{6,4},{7,5},{8,10},{9,11},{10,... | collective-permute-start | bytes 1572872 | tf_op jit(solution)/shard_map/ppermute | solution.py:913
  13.2 19.1 %collective-permute-start = (f32[128,1024]{1,0:T(8,128)S(1)}, f32[128,1024]{1,0:T(8,128)}, u32[]{:S(2)}, u32[]{:S(2)}) collective-permute-start(f32[128,1024]{1,0:T(8,128)S(1)} %bitcast.54), channel_id=1, source_target_pairs={{0,1},{1,0},{2,3},{3,2},{4,5},{5,4},{6,7},{7,6},{8,9},{9,8},{10,11... | collective-permute-start | bytes 1572872 | tf_op jit(solution)/shard_map/ppermute | solution.py:913
  13.6 149.3 %copy-start = (bf16[3,2,64,1024]{3,2,1,0:T(8,128)(2,1)}, bf16[3,2,64,1024]{3,2,1,0:T(8,128)(2,1)S(1)}, u32[]{:S(2)}) copy-start(bf16[3,2,64,1024]{3,2,1,0:T(8,128)(2,1)S(1)} %copy.29) | copy-start | bytes 2359300
  30.6 1.9 collective-permute-start.2
  162.2 33.7 %collective-permute-start.5 = (bf16[384,1024]{1,0:T(8,128)(2,1)S(1)}, bf16[384,1024]{1,0:T(8,128)(2,1)S(1)}, u32[]{:S(2)}, u32[]{:S(2)}) collective-permute-start(bf16[384,1024]{1,0:T(8,128)(2,1)S(1)} %bitcast.46), channel_id=1, source_target_pairs={{16,17},{17,16},{18,19},{19,18},{20,21},{21,20},{22,23},{23,22},{2... | collective-permute-start | bytes 2359304 | tf_op jit(solution)/shard_map/ppermute | solution.py:919
  163.0 33.0 %collective-permute-start.4 = (bf16[384,1024]{1,0:T(8,128)(2,1)S(1)}, bf16[384,1024]{1,0:T(8,128)(2,1)}, u32[]{:S(2)}, u32[]{:S(2)}) collective-permute-start(bf16[384,1024]{1,0:T(8,128)(2,1)S(1)} %bitcast.47), channel_id=1, source_target_pairs={{16,18},{17,19},{18,16},{19,17},{20,22},{21,23},{22,20},{23,21},{2... | collective-permute-start | bytes 2359304 | tf_op jit(solution)/shard_map/ppermute | solution.py:919
  164.5 31.4 %collective-permute-start.3 = (bf16[128,1024]{1,0:T(8,128)(2,1)}, bf16[128,1024]{1,0:T(8,128)(2,1)S(1)}, u32[]{:S(2)}, u32[]{:S(2)}) collective-permute-start(bf16[128,1024]{1,0:T(8,128)(2,1)} %shard_map.137), channel_id=1, source_target_pairs={{0,16},{1,17},{2,18},{3,19},{4,20},{5,21},{6,22},{7,23},{8,24},{9,... | collective-permute-start | bytes 786440 | tf_op jit(solution)/shard_map/ppermute | solution.py:1017
  201.6 8.8 %collective-permute-start.8 = (bf16[26,384,256]{2,1,0:T(8,128)(2,1)}, bf16[26,384,256]{2,1,0:T(8,128)(2,1)}, u32[]{:S(2)}, u32[]{:S(2)}) collective-permute-start(bf16[26,384,256]{2,1,0:T(8,128)(2,1)} %get-tuple-element.73.refs_0_.refs_4_.refs_3_.refs_2_.refs_8_), channel_id=1, source_target_pairs={{16,17},{17,16},{18,19},{19,18},{20,21},{21,20},{22,23},{23,22},{2... | collective-permute-start | bytes 15335432 | tf_op jit(solution)/shard_map/ppermute | solution.py:919
  204.5 5.9 %collective-permute-start.6 = (bf16[4,384,256]{2,1,0:T(8,128)(2,1)}, bf16[4,384,256]{2,1,0:T(8,128)(2,1)S(1)}, u32[]{:S(2)}, u32[]{:S(2)}) collective-permute-start(bf16[4,384,256]{2,1,0:T(8,128)(2,1)} %get-tuple-element.71.refs_2_), channel_id=1, source_target_pairs={{16,18},{17,19},{18,16},{19,17},{20,22},{21,23},{22,20},{23,21},{2... | collective-permute-start | bytes 2359304 | tf_op jit(solution)/shard_map/ppermute | solution.py:919
  205.2 5.2 %collective-permute-start.7 = (bf16[4,384,256]{2,1,0:T(8,128)(2,1)}, bf16[4,384,256]{2,1,0:T(8,128)(2,1)S(1)}, u32[]{:S(2)}, u32[]{:S(2)}) collective-permute-start(bf16[4,384,256]{2,1,0:T(8,128)(2,1)} %get-tuple-element.72.refs_4_), channel_id=1, source_target_pairs={{16,17},{17,16},{18,19},{19,18},{20,21},{21,20},{22,23},{23,22},{2... | collective-permute-start | bytes 2359304 | tf_op jit(solution)/shard_map/ppermute | solution.py:919
  210.5 28.6 %collective-permute-start.11 = (bf16[384,1024]{1,0:T(8,128)(2,1)}, bf16[384,1024]{1,0:T(8,128)(2,1)S(1)}, u32[]{:S(2)}, u32[]{:S(2)}) collective-permute-start(bf16[384,1024]{1,0:T(8,128)(2,1)} %collective-permute-done.4.refs_6_), channel_id=1, source_target_pairs={{16,17},{17,16},{18,19},{19,18},{20,21},{21,20},{22,23},{23,22},{2... | collective-permute-start | bytes 2359304 | tf_op jit(solution)/shard_map/ppermute | solution.py:919
  211.2 27.9 %collective-permute-start.10 = (bf16[4,384,256]{2,1,0:T(8,128)(2,1)S(1)}, bf16[4,384,256]{2,1,0:T(8,128)(2,1)S(1)}, u32[]{:S(2)}, u32[]{:S(2)}) collective-permute-start(bf16[4,384,256]{2,1,0:T(8,128)(2,1)S(1)} %collective-permute-done.7), channel_id=1, source_target_pairs={{16,18},{17,19},{18,16},{19,17},{20,22},{21,23},{22,20},{23,21},{2... | collective-permute-start | bytes 2359304 | tf_op jit(solution)/shard_map/ppermute | solution.py:919
  211.9 27.2 %collective-permute-start.9 = (bf16[128,1024]{1,0:T(8,128)(2,1)}, bf16[128,1024]{1,0:T(8,128)(2,1)S(1)}, u32[]{:S(2)}, u32[]{:S(2)}) collective-permute-start(bf16[128,1024]{1,0:T(8,128)(2,1)} %get-tuple-element.77), channel_id=1, source_target_pairs={{16,0},{17,1},{18,2},{19,3},{20,4},{21,5},{22,6},{23,7},{24,8},{25... | collective-permute-start | bytes 786440 | tf_op jit(solution)/shard_map/ppermute | solution.py:1042
  239.1 9.8 %collective-permute-start.13 = (bf16[128,1024]{1,0:T(8,128)(2,1)S(1)}, bf16[128,1024]{1,0:T(8,128)(2,1)S(1)}, u32[]{:S(2)}, u32[]{:S(2)}) collective-permute-start(bf16[128,1024]{1,0:T(8,128)(2,1)S(1)} %collective-permute-done.9), channel_id=1, source_target_pairs={{0,2},{1,3},{2,0},{3,1},{4,6},{5,7},{6,4},{7,5},{8,10},{9,11},{10,... | collective-permute-start | bytes 786440 | tf_op jit(solution)/shard_map/ppermute | solution.py:919
  241.3 59.8 %collective-permute-start.17 = (bf16[4,4,256,256]{3,2,1,0:T(8,128)(2,1)}, bf16[4,4,256,256]{3,2,1,0:T(8,128)(2,1)}, u32[]{:S(2)}, u32[]{:S(2)}) collective-permute-start(bf16[4,4,256,256]{3,2,1,0:T(8,128)(2,1)} %shard_map.142), channel_id=1, source_target_pairs={{16,18},{17,19},{18,16},{19,17},{20,22},{21,23},{22,20},{23,21},{2... | collective-permute-start | bytes 6291464 | tf_op jit(solution)/shard_map/ppermute | solution.py:919
  243.3 7.5 %collective-permute-start.12 = (bf16[128,1024]{1,0:T(8,128)(2,1)S(1)}, bf16[128,1024]{1,0:T(8,128)(2,1)S(1)}, u32[]{:S(2)}, u32[]{:S(2)}) collective-permute-start(bf16[128,1024]{1,0:T(8,128)(2,1)S(1)} %collective-permute-done.9), channel_id=1, source_target_pairs={{0,1},{1,0},{2,3},{3,2},{4,5},{5,4},{6,7},{7,6},{8,9},{9,8},{10,11... | collective-permute-start | bytes 786440 | tf_op jit(solution)/shard_map/ppermute | solution.py:919
  248.9 3.4 collective-permute-start.14
  259.9 33.4 %collective-permute-start.15 = (bf16[2,3,384,256]{3,2,1,0:T(8,128)(2,1)}, bf16[2,3,384,256]{3,2,1,0:T(8,128)(2,1)S(1)}, u32[]{:S(2)}, u32[]{:S(2)}) collective-permute-start(bf16[2,3,384,256]{3,2,1,0:T(8,128)(2,1)} %get-tuple-element.90), channel_id=1, source_target_pairs={{16,17},{17,16},{18,19},{19,18},{20,21},{21,20},{22,23},{23,22},{2... | collective-permute-start | bytes 3538952 | tf_op jit(solution)/shard_map/ppermute | solution.py:919
  260.6 109.1 %reduce-scatter.6.cloned.1.call-start = ((), (), s32[]{:S(2)}) async-start(), calls=%async_computation.4 | async-start | bytes 2621440 | tf_op jit(solution)/shard_map/reduce_scatter | solution.py:973
  299.0 22.5 %collective-permute-start.18 = (bf16[4,4,256,256]{3,2,1,0:T(8,128)(2,1)}, bf16[4,4,256,256]{3,2,1,0:T(8,128)(2,1)S(1)}, u32[]{:S(2)}, u32[]{:S(2)}) collective-permute-start(bf16[4,4,256,256]{3,2,1,0:T(8,128)(2,1)} %shard_map.144), channel_id=1, source_target_pairs={{16,18},{17,19},{18,16},{19,17},{20,22},{21,23},{22,20},{23,21},{2... | collective-permute-start | bytes 6291464 | tf_op jit(solution)/shard_map/ppermute | solution.py:919
  299.8 21.7 %collective-permute-start.16 = (bf16[3,128,1024]{2,1,0:T(8,128)(2,1)}, bf16[3,128,1024]{2,1,0:T(8,128)(2,1)S(1)}, u32[]{:S(2)}, u32[]{:S(2)}) collective-permute-start(bf16[3,128,1024]{2,1,0:T(8,128)(2,1)} %get-tuple-element.91), channel_id=1, source_target_pairs={{16,0},{17,1},{18,2},{19,3},{20,4},{21,5},{22,6},{23,7},{24,8},{25... | collective-permute-start | bytes 2359304 | tf_op jit(solution)/shard_map/ppermute | solution.py:1087
  307.5 93.1 %reduce-scatter.4.cloned.1.call-start = ((), (), s32[]{:S(2)}) async-start(), calls=%async_computation.3 | async-start | bytes 2621440 | tf_op jit(solution)/shard_map/reduce_scatter | solution.py:973
  (18 other events, 85.9 us)
Sparse Core Ops, SparseCore 0:
  10.1 134.7 all-gather.2
  260.7 48.8 reduce-scatter.7
  312.1 43.5 reduce-scatter.5
  357.8 42.8 reduce-scatter.3

commit v4 on v3

--- a/solution.py
+++ b/solution.py
@@ -163,7 +163,7 @@
         ref[pl.ds(at, F)] = value[i * F : (i + 1) * F]
 
 
-def frames_fwd_body(own, order, s_ref, wa_ref, gain_ref, bias_ref, nin_ref, proj_ref, mixed_ref, hid_ref, nmid_ref, act_ref, slope_ref, held, acts, sems):
+def frames_fwd_body(own, order, s_ref, nin_ref, wa_ref, gain_ref, bias_ref, proj_ref, mixed_ref, hid_ref, nmid_ref, act_ref, slope_ref, held, acts, sems):
     g = pl.program_id(0)
     T = pl.num_programs(0) // 2
     R, N = bias_ref.shape[:2]
@@ -171,9 +171,7 @@
 
     @pl.when(g == 0)
     def _():
-        s = s_ref[...]
-        nin_ref[...] = normed(s, gain_ref[0:1])
-        hid_ref[...] = s
+        hid_ref[...] = s_ref[...]
 
     @pl.when(g < T)
     def _():
@@ -209,21 +207,21 @@
         stored(acts, sems, [act_ref])
 
 
-def frames_fwd(order, s, W, gain, bias, own):
+def frames_fwd(order, s, nin, W, gain, bias, own):
     rows, D = s.shape
     T = W.shape[1]
     return call(
         functools.partial(frames_fwd_body, own),
         order,
-        (s, W, gain, bias),
+        (s, nin, W, gain, bias),
         [
             whole(s.shape),
+            whole(nin.shape),
             weight_spec(W, lambda g: (g % T, g // T)),
             whole(gain.shape),
             whole(bias.shape),
         ],
         (
-            struct((rows, D), BF16),
             struct((T, 3, rows, BLK), BF16),
             struct((rows, BLK), BF16),
             struct((rows, D), F32),
@@ -232,7 +230,6 @@
             struct((T, 4, rows, BLK), BF16),
         ),
         (
-            whole((rows, D)),
             pl.BlockSpec((1, 3, rows, BLK), lambda g, order: (jnp.minimum(g, T - 1) * order[ACTIVE], 0, 0, 0)),
             whole((rows, BLK)),
             whole((rows, D)),
@@ -251,7 +248,7 @@
     )
 
 
-def frames_own_body(own, order, s_ref, wa_ref, wb_ref, gain_ref, bias_ref, out_ref, nin, keys, values, held, hid, nmid):
+def frames_own_body(own, order, s_ref, nin, wa_ref, wb_ref, gain_ref, bias_ref, out_ref, keys, values, held, hid, nmid):
     g = pl.program_id(0)
     T = pl.num_programs(0) // 2
     R, N = bias_ref.shape[:2]
@@ -260,8 +257,7 @@
 
     @pl.when(g == 0)
     def _():
-        nin[...] = normed(s_ref[...], gain_ref[0:1])
-        hid[...] = s_ref[:mine]
+        hid[...] = s_ref[...]
 
     @pl.when(g < T)
     def _():
@@ -293,16 +289,17 @@
         out_ref[...] = hid[...].astype(BF16)
 
 
-def frames_own(order, s, W, gain, bias, own):
-    rows, D = s.shape
+def frames_own(order, s, nin, W, gain, bias, own):
+    rows, D = nin.shape
     T = W.shape[1]
     mine = bias.shape[0] * own
     return call(
         functools.partial(frames_own_body, own),
         order,
-        (s, W, W, gain, bias),
+        (s, nin, W, W, gain, bias),
         [
             whole(s.shape),
+            whole(nin.shape),
             weight_spec(W, lambda g: (g % T, g // T)),
             weight_spec(W, lambda g: (jnp.maximum(g - T, 0), 2)),
             whole(gain.shape),
@@ -312,7 +309,6 @@
         whole((mine, D)),
         2 * T,
         (
-            pltpu.VMEM((rows, D), BF16),
             pltpu.VMEM((rows, BLK), BF16),
             pltpu.VMEM((rows, BLK), BF16),
             pltpu.VMEM((mine, BLK), BF16),
@@ -923,6 +919,21 @@
     return lax.optimization_barrier(values)
 
 
+def mark_body(flag_ref, *refs):
+    refs[-1][0] = flag_ref[0]
+
+
+def mark(flag, *values):
+    scalar = pl.BlockSpec(memory_space=pltpu.SMEM)
+    return pl.pallas_call(
+        mark_body,
+        out_shape=struct((1,), jnp.int32),
+        in_specs=[scalar] + [HBM_REF] * len(values),
+        out_specs=scalar,
+        cost_estimate=pl.CostEstimate(flops=10**9, bytes_accessed=0, transcendentals=0),
+    )(flag, *values)
+
+
 def after(value, *others):
     return together(value, *others)[0]
 
@@ -933,6 +944,20 @@
     for j in range(4):
         flat_ref[4 + j] = up_ref[:, j * BLK : (j + 1) * BLK]
     flat_ref[8:12] = down_ref[...]
+
+
+def widen_body(parts_ref, rows_ref, cols_ref):
+    split = rows_ref.shape[0]
+    rows_ref[...] = parts_ref[:split].astype(F32)
+    cols_ref[...] = parts_ref[split:].astype(F32)
+
+
+def widen(parts, split):
+    rest = (parts.shape[0] - split,) + parts.shape[1:]
+    return pl.pallas_call(
+        widen_body,
+        out_shape=(struct((split,) + parts.shape[1:], F32), struct(rest, F32)),
+    )(parts)
 
 
 def gather_weights(w_qkv, w_out, w_up, w_down):
@@ -971,7 +996,7 @@
     per = shards // nz
     if per == 1:
         out = lax.psum_scatter(parts, "dp", scatter_dimension=0, tiled=False)
-        return out[:split], out[split:]
+        return widen(out, split) if 0 < split < count else (out[:split], out[split:])
     depth = BLK // per
     rows = parts[:, :split].reshape(nz, split, per, depth, BLK)
     rows = rows.transpose(0, 2, 1, 3, 4).reshape(shards, -1, BLK)
@@ -1013,10 +1038,11 @@
     allowed = (pos[:, None] >= pos[None, :])[None] & (seg[:, :, None] == seg[:, None, :])
     bias = jnp.where(allowed, 0.0, NEG).astype(F32)
 
-    out0 = frames_own(order0, s0, W, gain, bias, F)
+    n_in0 = normed(s0, gain[0:1])
+    out0 = frames_own(order0, frame_own, n_in0, W, gain, bias, F)
     sent = lax.ppermute(out0, "section", [(0, 1)])
     s0 = after(s0, out0)
-    n_in0, proj0, mixed0, hid0, n_mid0, act0, slope0 = frames_fwd(order0, s0, W, gain, bias, F)
+    proj0, mixed0, hid0, n_mid0, act0, slope0 = frames_fwd(order0, s0, n_in0, W, gain, bias, F)
 
     def swap1(value, bit):
         return swap_in(value, 1, bit)
@@ -1029,19 +1055,17 @@
         order1, codes_t, sent, cot, gact1, W, gain
     )
     act_y = swap1(act_far, 2)
-    act_o = swap1(act_other, 1)
-    bundle_s = swap1(bundle, 1)
+    bundle_s, cot_d = swap1(bundle, 1), swap1(after(cot_y, bundle), 1)
     gproj1, gproj1_s, glocal, gsent, gg_in1 = codes_back(
         order1, proj1, W, codes_t, sent, ghid1, gain
     )
 
-    gproj1, gproj1_s, glocal, gsent, gg_in1, act_y, act_o, bundle_s = together(
-        gproj1, gproj1_s, glocal, gsent, gg_in1, act_y, act_o, bundle_s
+    gproj1, gproj1_s, glocal, gsent, gg_in1, bundle_s, cot_d = together(
+        gproj1, gproj1_s, glocal, gsent, gg_in1, bundle_s, cot_d
     )
 
     gsent = lax.ppermute(gsent, "section", [(1, 0)])
-    act_d = swap1(act_o, 2)
-    cot_d = swap1(after(cot_y, act_o), 1)
+    act_d = swap1(act_other, 3)
 
     M1 = C * M
     gproj1 = gproj1.reshape(-1, M1, BLK)
@@ -1049,14 +1073,14 @@
         flag, nz, [(True, 4, [], [((bundle, 16), own1, 8), ((bundle_s, 16), bundle_s, 8)])]
     )
     up_got = swap1(up_far, 2)
-    gsent, _, act_d, cot_d = together(gsent, up_far, act_d, cot_d)
+    gsent, later = together(gsent, mark(flag, up_far, act_y, act_d))
     gfar = swap_in(gsent, 0, 2)
     gy0 = jnp.concatenate(
         [gsent, swap_in(gsent, 0, 1), gfar, swap_in(gfar, 0, 1)], axis=0
     )
 
     down_total = grads(
-        flag,
+        later,
         nz,
         [
             (
@@ -1083,9 +1107,8 @@
         ],
     )
     att_got = swap1(att_far, 2)
-    hid1, glocal = together(hid1, glocal, att_far)[:2]
+    glocal = after(glocal, att_far)
     glocal = lax.ppermute(glocal, "section", [(1, 0)])
-    out1 = codes_out(order1, hid1, [own1, act_far, bundle, act_other], W, C)
     up_total = grads(
         flag,
         nz,
@@ -1100,6 +1123,8 @@
         up_got,
     )
     up_part = scatter_blocks(up_total, 4)[0]
+    hid1 = after(hid1, up_total)
+    out1 = codes_out(order1, hid1, [own1, act_far, bundle, act_other], W, C)
     gproj0, out1 = together(gproj0, out1, up_total, glocal)[:2]
     att_total = grads(
         flag,

time: 416 us -> 410 us (0.986)
  waiting for transfers between devices: 191 us -> 182 us
    ppermute x1, waiting for transfers between devices: 21.6 us -> 14.6 us  [on_device(): gsent = lax.ppermute(gsent, 'section', [(1, 0)])]
    ppermute x13 -> x12, starting transfers between devices: 17.7 us -> 20.6 us  [swap_in(): return lax.ppermute(value, ('section', 'tensor'), pairs)]
  transfers between devices with their start and end apart: 23 -> 22, of which waited for: 8 -> 8; matrix products, arithmetic and copies ran while one was open for 3% -> 3% of each run, Pallas kernels for 24% -> 25%
where the time goes in v4:
time: 410 us; the launch traced here: 405 us
  waiting for transfers between devices  182 us (44%)
  Pallas kernels  127 us (31%)
  blocking collectives  35.5 us (9%)
  starting transfers between devices  28.6 us (7%)
  between operations  14.5 us (4%)
  local copies, waits for them, and re-layouts  9.66 us (2%)
  other arithmetic  8.54 us (2%)
    pallas_call x12, Pallas kernels, call(): pl.pallas_call(run, out_shape=outs, grid_spec=pltpu.PrefetchScalarGridSpe...  122 us
    all_gather x1, waiting for transfers between devices, gather_weights(): out = lax.all_gather(flat, both)  110 us
    psum x1, blocking collectives, on_device(): grad_gains = lax.psum(after(gain_part, att_total), ('dp', 'tensor'))  35.5 us
    reduce_scatter x3, waiting for transfers between devices, scatter_blocks(): out = lax.psum_scatter(parts, 'dp', scatter_dimension=0, tiled=False)  28.2 us
    ppermute x12, starting transfers between devices, swap_in(): return lax.ppermute(value, ('section', 'tensor'), pairs)  20.6 us
    ppermute x3, waiting for transfers between devices, swap(): return lax.ppermute(value, axis, [(i, i ^ bit) for i in range(count)])  15.9 us
    ppermute x1, waiting for transfers between devices, on_device(): gsent = lax.ppermute(gsent, 'section', [(1, 0)])  14.6 us
    ppermute x1, waiting for transfers between devices, on_device(): glocal = lax.ppermute(glocal, 'section', [(1, 0)])  9.12 us
  transfers between devices with their start and end apart: 22, of which 8 were waited for; matrix products, arithmetic and copies ran while one was open for 3% of the time, Pallas kernels for 25%

profile of v4, /device:TPU:0, one launch (start us, length us, event | category | flops | bytes accessed | tf_op | source)
XLA Modules:
  0.0 405.2 jit_solution(3466671125012845712)
XLA Ops:
  7.2 2.7 shard_map.136
  10.2 3.0 collective-permute-start.1
  14.8 15.8 %collective-permute-done.1 = f32[128,1024]{1,0:T(8,128)S(1)} collective-permute-done((f32[128,1024]{1,0:T(8,128)S(1)}, f32[128,1024]{1,0:T(8,128)S(1)}, u32[]{:S(2)}, u32[]{:S(2)}) %collective-permute-start.1) | collective-permute-done | bytes 524320 | tf_op jit(solution)/shard_map/ppermute | solution.py:909
  35.3 109.6 %all-gather.3.cloned.1.call-done = bf16[192,256,256]{2,1,0:T(8,128)(2,1)} async-done(((bf16[12,256,256]{2,1,0:T(8,128)(2,1)}), bf16[192,256,256]{2,1,0:T(8,128)(2,1)}) %all-gather.3.cloned.1.call-update) | async-done | bytes 25165840 | tf_op jit(solution)/shard_map/all_gather | solution.py:973
  144.9 16.9 %shard_map.137 = bf16[128,1024]{1,0:T(8,128)(2,1)} custom-call(s32[5]{0:T(128)} %get-tuple-element.129.flags, f32[128,1024]{1,0:T(8,128)} %bitcast.48, bf16[512,1024]{1,0:T(8,128)(2,1)} %multiply_convert_fusion.refs_1_.refs_0_, bf16[4,4,12,256,256]{4,3,2,1,0:T(8,128)(2,1)} %bitcast.35, bf16[4,4,12,256,256]{4,3,2,1,0:T(8,128)(2,1)} %bitcast.36, ...), custom_call_target="tpu_custom_call" | custom-call | flops 402653184 | bytes 3145728 | tf_op jit(solution)/shard_map/pallas_call | solution.py:102
  166.9 3.3 shard_map.138.refs_3_
  170.2 25.0 %shard_map.139 = (bf16[4,3,512,256]{3,2,1,0:T(8,128)(2,1)}, bf16[512,256]{1,0:T(8,128)(2,1)}, f32[512,1024]{1,0:T(8,128)}, bf16[512,1024]{1,0:T(8,128)(2,1)}, bf...) custom-call(s32[5]{0:T(128)} %get-tuple-element.129.flags, f32[512,1024]{1,0:T(8,128)} %get-tuple-element.58.refs_0_, ...), custom_call_target="tpu_custom_call" | custom-call | flops 1342177280 | bytes 5111808 | tf_op jit(solution)/shard_map/pallas_call | solution.py:102
  195.9 5.1 %shard_map.140 = (bf16[4,3,384,256]{3,2,1,0:T(8,128)(2,1)}, f32[384,1024]{1,0:T(8,128)}, f32[384,1024]{1,0:T(8,128)}, f32[1,1024]{1,0:T(1,128)}, bf16[14,384,256...) custom-call(s32[5]{0:T(128)} %get-tuple-element.128.flags, ...), custom_call_target="tpu_custom_call" | custom-call | flops 1207959552 | bytes 4063232 | tf_op jit(solution)/shard_map/pallas_call | solution.py:102
  201.0 2.9 collective-permute-start.6
  207.0 4.3 %shard_map.141 = (bf16[2,3,384,256]{3,2,1,0:T(8,128)(2,1)}, bf16[2,3,384,256]{3,2,1,0:T(8,128)(2,1)}, bf16[3,128,1024]{2,1,0:T(8,128)(2,1)}, bf16[128,1024]{1,0:T(8,128)(2,1)}, f32[1,1024]{1,0:T(1,128)}) custom-call(s32[5]{0:T(128)} %get-tuple-element.128.flags, bf16[4,3,384,256]{3,2,1,0:T(8,128)(2,1)} %get-tuple-element.62.refs_0_, ...), custom_call_target="tpu_custom_call" | custom-call | flops 402653184 | bytes 2031616 | tf_op jit(solution)/shard_map/pallas_call | solution.py:102
  212.6 4.3 %shard_map.142.refs_0_ = bf16[4,4,256,256]{3,2,1,0:T(8,128)(2,1)} custom-call(s32[1]{0:T(128)} %bitcast.flags.flag_ref, bf16[26,384,256]{2,1,0:T(8,128)(2,1)} %get-tuple-element.69.refs_0_.refs_4_.refs_2_.refs_3_.refs_8_, bf16[14,384,256]{2,1,0:T(8,128)(2,1)} %get-tuple-element.76.refs_1_.refs_3_.refs_5_.refs_9_, ...), custom_call_target="tpu_custom_call" | custom-call | flops 1000000000 | tf_op jit(solution)/shard_map/pallas_call | solution.py:102
  218.4 14.6 %collective-permute-done.8 = bf16[128,1024]{1,0:T(8,128)(2,1)S(1)} collective-permute-done((bf16[128,1024]{1,0:T(8,128)(2,1)}, bf16[128,1024]{1,0:T(8,128)(2,1)S(1)}, u32[]{:S(2)}, u32[]{:S(2)}) %collective-permute-start.8) | collective-permute-done | bytes 262176 | tf_op jit(solution)/shard_map/ppermute | solution.py:1067
  233.0 3.7 collective-permute-start.12
  240.7 2.6 collective-permute-done.12
  247.7 7.2 %shard_map.144 = bf16[4,4,256,256]{3,2,1,0:T(8,128)(2,1)} custom-call(s32[1]{0:T(128)} %shard_map.143.flags, bf16[512,1024]{1,0:T(8,128)(2,1)} %copy-done.2, bf16[4,512,256]{2,1,0:T(8,128)(2,1)} %get-tuple-element.82.refs_1_, bf16[384,1024]{1,0:T(8,128)(2,1)} %bitcast.54, bf16[14,384,256]{2,1,0:T(8,128)(2,1)} %get-tuple-element.76.refs_1_.refs_3_.refs_5_.refs_9_, ...), custom_call_target="tpu_custom_call" | custom-call | flops 1000000000 | tf_op jit(solution)/shard_map/pallas_call | solution.py:102
  256.0 32.3 %shard_map.146 = (bf16[4,512,256]{2,1,0:T(8,128)(2,1)}, bf16[512,1024]{1,0:T(8,128)(2,1)}, bf16[3,512,256]{2,1,0:T(8,128)(2,1)}, f32[128,1024]{1,0:T(8,128)}, f32[2,1024]{1,0:T(2,128)}) custom-call(s32[5]{0:T(128)} %get-tuple-element.129.flags, bf16[512,1024]{1,0:T(8,128)(2,1)} %copy-done.2, f32[512,1024]{1,0:T(8,128)} %get-tuple-element.89.refs_1_, ...), custom_call_target="tpu_custom_call" | custom-call | flops 1879048192 | bytes 5111808 | tf_op jit(solution)/shard_map/pallas_call | solution.py:102
  289.3 4.7 %shard_map.145 = bf16[4,4,256,256]{3,2,1,0:T(8,128)(2,1)} custom-call(s32[1]{0:T(128)} %bitcast.flags.flag_ref, bf16[26,384,256]{2,1,0:T(8,128)(2,1)} %get-tuple-element.69.refs_0_.refs_4_.refs_2_.refs_3_.refs_8_, bf16[6,384,256]{2,1,0:T(8,128)(2,1)} %bitcast.60, ...), custom_call_target="tpu_custom_call" | custom-call | flops 1000000000 | tf_op jit(solution)/shard_map/pallas_call | solution.py:102
  297.3 6.4 %shard_map.147 = bf16[4,4,256,256]{3,2,1,0:T(8,128)(2,1)} custom-call(s32[1]{0:T(128)} %bitcast.flags.flag_ref, bf16[512,1024]{1,0:T(8,128)(2,1)} %get-tuple-element.95.refs_0_, bf16[4,512,256]{2,1,0:T(8,128)(2,1)} %get-tuple-element.96.refs_1_, bf16[26,384,256]{2,1,0:T(8,128)(2,1)} %get-tuple-element.69.refs_0_.refs_4_.refs_2_.refs_3_.refs_8_, ...), custom_call_target="tpu_custom_call" | custom-call | flops 99999997952 | tf_op jit(solution)/shard_map/pallas_call | solution.py:102
  304.1 4.5 %shard_map.148 = bf16[3,128,1024]{2,1,0:T(8,128)(2,1)} custom-call(s32[5]{0:T(128)} %get-tuple-element.128.flags, f32[384,1024]{1,0:T(8,128)} %get-tuple-element.97.refs_0_, bf16[14,384,256]{2,1,0:T(8,128)(2,1)} %get-tuple-element.76.refs_1_.refs_3_.refs_5_.refs_9_, bf16[4,384,256]{2,1,0:T(8,128)(2,1)} %get-tuple-element.78.refs_2_, ...), custom_call_target="tpu_custom_call" | custom-call | flops 402653184 | bytes 1736704 | tf_op jit(solution)/shard_map/pallas_call | solution.py:102
  308.6 9.1 %collective-permute-done.15 = bf16[3,128,1024]{2,1,0:T(8,128)(2,1)S(1)} collective-permute-done((bf16[3,128,1024]{2,1,0:T(8,128)(2,1)}, bf16[3,128,1024]{2,1,0:T(8,128)(2,1)S(1)}, u32[]{:S(2)}, u32[]{:S(2)}) %collective-permute-start.15) | collective-permute-done | bytes 786464 | tf_op jit(solution)/shard_map/ppermute | solution.py:1111
  317.7 7.5 %shard_map.149 = bf16[4,4,256,256]{3,2,1,0:T(8,128)(2,1)} custom-call(s32[1]{0:T(128)} %bitcast.flags.flag_ref, bf16[512,1024]{1,0:T(8,128)(2,1)} %multiply_convert_fusion.refs_1_.refs_0_, bf16[3,512,256]{2,1,0:T(8,128)(2,1)} %get-tuple-element.99.refs_1_, bf16[26,384,256]{2,1,0:T(8,128)(2,1)} %get-tuple-element.69.refs_0_.refs_4_.refs_2_.refs_3_.refs_8_, ...), custom_call_target="tpu_custom_call" | custom-call | flops 99999997952 | tf_op jit(solution)/shard_map/pallas_call | solution.py:102
  327.8 35.5 %psum.7 = f32[1,2,1024]{2,1,0:T(2,128)} all-reduce(f32[1,2,1024]{2,1,0:T(2,128)S(1)} %bitcast.77), channel_id=1, replica_groups=mesh['section'=2,'dp'=4,'tensor'=4] {'dp','tensor'}, use_global_device_ids=true, to_apply=%region_7.8 | all-reduce | flops 2048 | bytes 16384 | tf_op jit(solution)/shard_map/psum | solution.py:1150
  363.3 2.1 bitcast_convert_fusion
  368.1 28.2 %reduce-scatter.4.cloned.1.call-done = bf16[1,4,256,256]{3,2,1,0:T(8,128)(2,1)} async-done(((bf16[4,4,256,256]{3,2,1,0:T(8,128)(2,1)}), bf16[1,4,256,256]{3,2,1,0:T(8,128)(2,1)}) %reduce-scatter.4.cloned.1.call-update) | async-done | bytes 524304 | tf_op jit(solution)/shard_map/reduce_scatter | solution.py:998
  (101 shorter events, 39.3 us)
Async XLA Ops:
  7.2 137.7 %all-gather.3.cloned.1.call-start = ((), (), s32[]{:S(2)}) async-start(), calls=%async_computation.6 | async-start | bytes 26738688 | tf_op jit(solution)/shard_map/all_gather | solution.py:973
  10.0 353.3 %reduce-scatter.8.cloned.1.call-start = ((), (), s32[]{:S(2)}) async-start(), calls=%async_computation.5 | async-start | bytes 2621440 | tf_op jit(solution)/shard_map/reduce_scatter | solution.py:998
  10.1 23.9 %copy-start = (f32[2,64,1024]{2,1,0:T(8,128)}, f32[2,64,1024]{2,1,0:T(8,128)S(1)}, u32[]{:S(2)}) copy-start(f32[2,64,1024]{2,1,0:T(8,128)S(1)} %convert_reduce_fusion) | copy-start | bytes 1572868
  10.2 20.4 %collective-permute-start.1 = (f32[128,1024]{1,0:T(8,128)S(1)}, f32[128,1024]{1,0:T(8,128)S(1)}, u32[]{:S(2)}, u32[]{:S(2)}) collective-permute-start(f32[128,1024]{1,0:T(8,128)S(1)} %bitcast.44), channel_id=1, source_target_pairs={{0,2},{1,3},{2,0},{3,1},{4,6},{5,7},{6,4},{7,5},{8,10},{9,11},{10,... | collective-permute-start | bytes 1572872 | tf_op jit(solution)/shard_map/ppermute | solution.py:909
  13.2 19.2 %collective-permute-start = (f32[128,1024]{1,0:T(8,128)S(1)}, f32[128,1024]{1,0:T(8,128)S(1)}, u32[]{:S(2)}, u32[]{:S(2)}) collective-permute-start(f32[128,1024]{1,0:T(8,128)S(1)} %bitcast.45), channel_id=1, source_target_pairs={{0,1},{1,0},{2,3},{3,2},{4,5},{5,4},{6,7},{7,6},{8,9},{9,8},{10,11... | collective-permute-start | bytes 1572872 | tf_op jit(solution)/shard_map/ppermute | solution.py:909
  14.7 147.8 %copy-start.1 = (bf16[3,2,64,1024]{3,2,1,0:T(8,128)(2,1)}, bf16[3,2,64,1024]{3,2,1,0:T(8,128)(2,1)S(1)}, u32[]{:S(2)}) copy-start(bf16[3,2,64,1024]{3,2,1,0:T(8,128)(2,1)S(1)} %copy.29) | copy-start | bytes 2359300
  30.6 1.9 collective-permute-start.2
  161.8 33.4 %collective-permute-start.5 = (bf16[384,1024]{1,0:T(8,128)(2,1)S(1)}, bf16[384,1024]{1,0:T(8,128)(2,1)S(1)}, u32[]{:S(2)}, u32[]{:S(2)}) collective-permute-start(bf16[384,1024]{1,0:T(8,128)(2,1)S(1)} %bitcast.50), channel_id=1, source_target_pairs={{16,17},{17,16},{18,19},{19,18},{20,21},{21,20},{22,23},{23,22},{2... | collective-permute-start | bytes 2359304 | tf_op jit(solution)/shard_map/ppermute | solution.py:915
  162.5 32.7 %collective-permute-start.4 = (bf16[384,1024]{1,0:T(8,128)(2,1)S(1)}, bf16[384,1024]{1,0:T(8,128)(2,1)}, u32[]{:S(2)}, u32[]{:S(2)}) collective-permute-start(bf16[384,1024]{1,0:T(8,128)(2,1)S(1)} %bitcast.51), channel_id=1, source_target_pairs={{16,18},{17,19},{18,16},{19,17},{20,22},{21,23},{22,20},{23,21},{2... | collective-permute-start | bytes 2359304 | tf_op jit(solution)/shard_map/ppermute | solution.py:915
  164.1 31.1 %collective-permute-start.3 = (bf16[128,1024]{1,0:T(8,128)(2,1)}, bf16[128,1024]{1,0:T(8,128)(2,1)S(1)}, u32[]{:S(2)}, u32[]{:S(2)}) collective-permute-start(bf16[128,1024]{1,0:T(8,128)(2,1)} %shard_map.137), channel_id=1, source_target_pairs={{0,16},{1,17},{2,18},{3,19},{4,20},{5,21},{6,22},{7,23},{8,24},{9,... | collective-permute-start | bytes 786440 | tf_op jit(solution)/shard_map/ppermute | solution.py:1043
  201.0 10.3 %collective-permute-start.6 = (bf16[26,384,256]{2,1,0:T(8,128)(2,1)}, bf16[26,384,256]{2,1,0:T(8,128)(2,1)}, u32[]{:S(2)}, u32[]{:S(2)}) collective-permute-start(bf16[26,384,256]{2,1,0:T(8,128)(2,1)} %get-tuple-element.69.refs_0_.refs_4_.refs_2_.refs_3_.refs_8_), channel_id=1, source_target_pairs={{16,17},{17,16},{18,19},{19,18},{20,21},{21,20},{22,23},{23,22},{2... | collective-permute-start | bytes 15335432 | tf_op jit(solution)/shard_map/ppermute | solution.py:915
  203.9 7.4 %collective-permute-start.7 = (bf16[384,1024]{1,0:T(8,128)(2,1)}, bf16[384,1024]{1,0:T(8,128)(2,1)S(1)}, u32[]{:S(2)}, u32[]{:S(2)}) collective-permute-start(bf16[384,1024]{1,0:T(8,128)(2,1)} %collective-permute-done.4.refs_6_), channel_id=1, source_target_pairs={{16,17},{17,16},{18,19},{19,18},{20,21},{21,20},{22,23},{23,22},{2... | collective-permute-start | bytes 2359304 | tf_op jit(solution)/shard_map/ppermute | solution.py:915
  204.6 12.4 %collective-permute-start.9 = (bf16[4,384,256]{2,1,0:T(8,128)(2,1)}, bf16[4,384,256]{2,1,0:T(8,128)(2,1)S(1)}, u32[]{:S(2)}, u32[]{:S(2)}) collective-permute-start(bf16[4,384,256]{2,1,0:T(8,128)(2,1)} %get-tuple-element.78.refs_2_), channel_id=1, source_target_pairs={{16,18},{17,19},{18,16},{19,17},{20,22},{21,23},{22,20},{23,21},{2... | collective-permute-start | bytes 2359304 | tf_op jit(solution)/shard_map/ppermute | solution.py:915
  205.3 11.7 %collective-permute-start.10 = (bf16[4,384,256]{2,1,0:T(8,128)(2,1)}, bf16[4,384,256]{2,1,0:T(8,128)(2,1)}, u32[]{:S(2)}, u32[]{:S(2)}) collective-permute-start(bf16[4,384,256]{2,1,0:T(8,128)(2,1)} %get-tuple-element.79.refs_4_), channel_id=1, source_target_pairs={{16,19},{17,18},{18,17},{19,16},{20,23},{21,22},{22,21},{23,20},{2... | collective-permute-start | bytes 2359304 | tf_op jit(solution)/shard_map/ppermute | solution.py:915
  211.3 21.7 %collective-permute-start.8 = (bf16[128,1024]{1,0:T(8,128)(2,1)}, bf16[128,1024]{1,0:T(8,128)(2,1)S(1)}, u32[]{:S(2)}, u32[]{:S(2)}) collective-permute-start(bf16[128,1024]{1,0:T(8,128)(2,1)} %get-tuple-element.75), channel_id=1, source_target_pairs={{16,0},{17,1},{18,2},{19,3},{20,4},{21,5},{22,6},{23,7},{24,8},{25... | collective-permute-start | bytes 786440 | tf_op jit(solution)/shard_map/ppermute | solution.py:1067
  233.0 10.3 %collective-permute-start.12 = (bf16[128,1024]{1,0:T(8,128)(2,1)S(1)}, bf16[128,1024]{1,0:T(8,128)(2,1)S(1)}, u32[]{:S(2)}, u32[]{:S(2)}) collective-permute-start(bf16[128,1024]{1,0:T(8,128)(2,1)S(1)} %collective-permute-done.8), channel_id=1, source_target_pairs={{0,2},{1,3},{2,0},{3,1},{4,6},{5,7},{6,4},{7,5},{8,10},{9,11},{10,... | collective-permute-start | bytes 786440 | tf_op jit(solution)/shard_map/ppermute | solution.py:915
  236.7 60.6 %collective-permute-start.16 = (bf16[4,4,256,256]{3,2,1,0:T(8,128)(2,1)S(1)}, bf16[4,4,256,256]{3,2,1,0:T(8,128)(2,1)}, u32[]{:S(2)}, u32[]{:S(2)}) collective-permute-start(bf16[4,4,256,256]{3,2,1,0:T(8,128)(2,1)S(1)} %copy-done.5), channel_id=1, source_target_pairs={{16,18},{17,19},{18,16},{19,17},{20,22},{21,23},{22,20},{23,21},{2... | collective-permute-start | bytes 6291464 | tf_op jit(solution)/shard_map/ppermute | solution.py:915
  238.8 6.5 %collective-permute-start.11 = (bf16[128,1024]{1,0:T(8,128)(2,1)S(1)}, bf16[128,1024]{1,0:T(8,128)(2,1)S(1)}, u32[]{:S(2)}, u32[]{:S(2)}) collective-permute-start(bf16[128,1024]{1,0:T(8,128)(2,1)S(1)} %collective-permute-done.8), channel_id=1, source_target_pairs={{0,1},{1,0},{2,3},{3,2},{4,5},{5,4},{6,7},{7,6},{8,9},{9,8},{10,11... | collective-permute-start | bytes 786440 | tf_op jit(solution)/shard_map/ppermute | solution.py:915
  243.3 3.4 collective-permute-start.13
  255.0 33.3 %collective-permute-start.14 = (bf16[2,3,384,256]{3,2,1,0:T(8,128)(2,1)}, bf16[2,3,384,256]{3,2,1,0:T(8,128)(2,1)S(1)}, u32[]{:S(2)}, u32[]{:S(2)}) collective-permute-start(bf16[2,3,384,256]{3,2,1,0:T(8,128)(2,1)} %get-tuple-element.86), channel_id=1, source_target_pairs={{16,17},{17,16},{18,19},{19,18},{20,21},{21,20},{22,23},{23,22},{2... | collective-permute-start | bytes 3538952 | tf_op jit(solution)/shard_map/ppermute | solution.py:915
  255.7 109.6 %reduce-scatter.6.cloned.1.call-start = ((), (), s32[]{:S(2)}) async-start(), calls=%async_computation.4 | async-start | bytes 2621440 | tf_op jit(solution)/shard_map/reduce_scatter | solution.py:998
  294.1 23.6 %collective-permute-start.17 = (bf16[4,4,256,256]{3,2,1,0:T(8,128)(2,1)}, bf16[4,4,256,256]{3,2,1,0:T(8,128)(2,1)}, u32[]{:S(2)}, u32[]{:S(2)}) collective-permute-start(bf16[4,4,256,256]{3,2,1,0:T(8,128)(2,1)} %shard_map.145), channel_id=1, source_target_pairs={{16,18},{17,19},{18,16},{19,17},{20,22},{21,23},{22,20},{23,21},{2... | collective-permute-start | bytes 6291464 | tf_op jit(solution)/shard_map/ppermute | solution.py:915
  296.0 21.7 %collective-permute-start.15 = (bf16[3,128,1024]{2,1,0:T(8,128)(2,1)}, bf16[3,128,1024]{2,1,0:T(8,128)(2,1)S(1)}, u32[]{:S(2)}, u32[]{:S(2)}) collective-permute-start(bf16[3,128,1024]{2,1,0:T(8,128)(2,1)} %get-tuple-element.87), channel_id=1, source_target_pairs={{16,0},{17,1},{18,2},{19,3},{20,4},{21,5},{22,6},{23,7},{24,8},{25... | collective-permute-start | bytes 2359304 | tf_op jit(solution)/shard_map/ppermute | solution.py:1111
  303.8 92.5 %reduce-scatter.4.cloned.1.call-start = ((), (), s32[]{:S(2)}) async-start(), calls=%async_computation.3 | async-start | bytes 2621440 | tf_op jit(solution)/shard_map/reduce_scatter | solution.py:998
  (16 other events, 46.2 us)
Sparse Core Ops, SparseCore 0:
  10.1 134.7 all-gather.2
  255.8 48.9 reduce-scatter.7
  307.3 44.0 reduce-scatter.5
  353.5 42.8 reduce-scatter.3

commit v5 on v4

--- a/solution.py
+++ b/solution.py
@@ -1027,10 +1027,10 @@
     cot = cotangent.transpose(2, 0, 1, 3).reshape(C * M, D)
 
     frame_own = jnp.sum(codes_t.astype(F32), axis=0)
-    far = swap(frame_own, "tensor", 2)
-    s0 = jnp.concatenate(
-        [frame_own, swap(frame_own, "tensor", 1), far, swap(far, "tensor", 1)], axis=0
-    )
+    near = frame_own.astype(BF16)
+    far = swap(near, "tensor", 2)
+    others = [swap(near, "tensor", 1), far, swap(far, "tensor", 1)]
+    s0 = jnp.concatenate([frame_own, *[part.astype(F32) for part in others]], axis=0)
     spot = t ^ lax.iota(jnp.int32, T)
     pos = (spot[:, None] * F + lax.iota(jnp.int32, F)[None]).reshape(N)
     ends = jnp.cumsum(doc_lengths, axis=1)
@@ -1060,8 +1060,8 @@
         order1, proj1, W, codes_t, sent, ghid1, gain
     )
 
-    gproj1, gproj1_s, glocal, gsent, gg_in1, bundle_s, cot_d = together(
-        gproj1, gproj1_s, glocal, gsent, gg_in1, bundle_s, cot_d
+    gproj1, gproj1_s, glocal, gsent, gg_in1, bundle_s = together(
+        gproj1, gproj1_s, glocal, gsent, gg_in1, bundle_s
     )
 
     gsent = lax.ppermute(gsent, "section", [(1, 0)])

time: 410 us -> 403 us (0.983)
  waiting for transfers between devices: 182 us -> 175 us
    ppermute x3, waiting for transfers between devices: 15.9 us -> 5.76 us  [swap(): return lax.ppermute(value, axis, [(i, i ^ bit) for i in range(count)])]
    all_gather x1, waiting for transfers between devices: 110 us -> 116 us  [gather_weights(): out = lax.all_gather(flat, both)]
  transfers between devices with their start and end apart: 22 -> 22, of which waited for: 8 -> 7; matrix products, arithmetic and copies ran while one was open for 3% -> 3% of each run, Pallas kernels for 25% -> 25%
where the time goes in v5:
time: 403 us; the launch traced here: 399 us
  waiting for transfers between devices  175 us (43%)
  Pallas kernels  127 us (32%)
  blocking collectives  34.8 us (9%)
  starting transfers between devices  28.9 us (7%)
  between operations  14.5 us (4%)
  other arithmetic  9.76 us (2%)
  local copies, waits for them, and re-layouts  8.54 us (2%)
    pallas_call x12, Pallas kernels, call(): pl.pallas_call(run, out_shape=outs, grid_spec=pltpu.PrefetchScalarGridSpe...  122 us
    all_gather x1, waiting for transfers between devices, gather_weights(): out = lax.all_gather(flat, both)  116 us
    psum x1, blocking collectives, on_device(): grad_gains = lax.psum(after(gain_part, att_total), ('dp', 'tensor'))  34.8 us
    reduce_scatter x3, waiting for transfers between devices, scatter_blocks(): out = lax.psum_scatter(parts, 'dp', scatter_dimension=0, tiled=False)  28.8 us
    ppermute x12, starting transfers between devices, swap_in(): return lax.ppermute(value, ('section', 'tensor'), pairs)  20.8 us
    ppermute x1, waiting for transfers between devices, on_device(): gsent = lax.ppermute(gsent, 'section', [(1, 0)])  11.4 us
    ppermute x1, waiting for transfers between devices, on_device(): glocal = lax.ppermute(glocal, 'section', [(1, 0)])  9.09 us
  transfers between devices with their start and end apart: 22, of which 7 were waited for; matrix products, arithmetic and copies ran while one was open for 3% of the time, Pallas kernels for 25%

profile of v5, /device:TPU:0, one launch (start us, length us, event | category | flops | bytes accessed | tf_op | source)
XLA Modules:
  0.0 398.7 jit_solution(12963009537942641309)
XLA Ops:
  7.2 2.7 shard_map.136
  10.2 3.0 collective-permute-start.1
  13.8 5.8 %collective-permute-done.1 = bf16[128,1024]{1,0:T(8,128)(2,1)S(1)} collective-permute-done((bf16[128,1024]{1,0:T(8,128)(2,1)S(1)}, bf16[128,1024]{1,0:T(8,128)(2,1)S(1)}, u32[]{:S(2)}, u32[]{:S(2)}) %collective-permute-start.1) | collective-permute-done | bytes 262176 | tf_op jit(solution)/shard_map/ppermute | solution.py:909
  25.3 116.1 %all-gather.3.cloned.1.call-done = bf16[192,256,256]{2,1,0:T(8,128)(2,1)} async-done(((bf16[12,256,256]{2,1,0:T(8,128)(2,1)}), bf16[192,256,256]{2,1,0:T(8,128)(2,1)}) %all-gather.3.cloned.1.call-update) | async-done | bytes 25165840 | tf_op jit(solution)/shard_map/all_gather | solution.py:973
  141.4 16.9 %shard_map.137 = bf16[128,1024]{1,0:T(8,128)(2,1)} custom-call(s32[5]{0:T(128)} %get-tuple-element.127.flags, f32[128,1024]{1,0:T(8,128)} %bitcast.47, bf16[512,1024]{1,0:T(8,128)(2,1)} %multiply_convert_fusion.refs_1_.refs_0_, bf16[4,4,12,256,256]{4,3,2,1,0:T(8,128)(2,1)} %bitcast.36, bf16[4,4,12,256,256]{4,3,2,1,0:T(8,128)(2,1)} %bitcast.37, ...), custom_call_target="tpu_custom_call" | custom-call | flops 402653184 | bytes 3145728 | tf_op jit(solution)/shard_map/pallas_call | solution.py:102
  163.4 3.3 shard_map.138.refs_3_
  166.7 25.0 %shard_map.139 = (bf16[4,3,512,256]{3,2,1,0:T(8,128)(2,1)}, bf16[512,256]{1,0:T(8,128)(2,1)}, f32[512,1024]{1,0:T(8,128)}, bf16[512,1024]{1,0:T(8,128)(2,1)}, bf...) custom-call(s32[5]{0:T(128)} %get-tuple-element.127.flags, f32[512,1024]{1,0:T(8,128)} %get-tuple-element.57.refs_0_, ...), custom_call_target="tpu_custom_call" | custom-call | flops 1342177280 | bytes 5111808 | tf_op jit(solution)/shard_map/pallas_call | solution.py:102
  192.4 5.1 %shard_map.140 = (bf16[4,3,384,256]{3,2,1,0:T(8,128)(2,1)}, f32[384,1024]{1,0:T(8,128)}, f32[384,1024]{1,0:T(8,128)}, f32[1,1024]{1,0:T(1,128)}, bf16[14,384,256...) custom-call(s32[5]{0:T(128)} %get-tuple-element.126.flags, ...), custom_call_target="tpu_custom_call" | custom-call | flops 1207959552 | bytes 4063232 | tf_op jit(solution)/shard_map/pallas_call | solution.py:102
  197.5 2.9 collective-permute-start.6
  202.8 4.3 %shard_map.141 = (bf16[2,3,384,256]{3,2,1,0:T(8,128)(2,1)}, bf16[2,3,384,256]{3,2,1,0:T(8,128)(2,1)}, bf16[3,128,1024]{2,1,0:T(8,128)(2,1)}, bf16[128,1024]{1,0:T(8,128)(2,1)}, f32[1,1024]{1,0:T(1,128)}) custom-call(s32[5]{0:T(128)} %get-tuple-element.126.flags, bf16[4,3,384,256]{3,2,1,0:T(8,128)(2,1)} %get-tuple-element.61.refs_0_, ...), custom_call_target="tpu_custom_call" | custom-call | flops 402653184 | bytes 2031616 | tf_op jit(solution)/shard_map/pallas_call | solution.py:102
  210.0 4.3 %shard_map.142.refs_0_ = bf16[4,4,256,256]{3,2,1,0:T(8,128)(2,1)} custom-call(s32[1]{0:T(128)} %bitcast.flags.flag_ref, bf16[26,384,256]{2,1,0:T(8,128)(2,1)} %get-tuple-element.68.refs_0_.refs_4_.refs_2_.refs_3_.refs_8_, bf16[14,384,256]{2,1,0:T(8,128)(2,1)} %get-tuple-element.73.refs_1_.refs_3_.refs_5_.refs_9_, ...), custom_call_target="tpu_custom_call" | custom-call | flops 1000000000 | tf_op jit(solution)/shard_map/pallas_call | solution.py:102
  215.7 11.4 %collective-permute-done.7 = bf16[128,1024]{1,0:T(8,128)(2,1)S(1)} collective-permute-done((bf16[128,1024]{1,0:T(8,128)(2,1)}, bf16[128,1024]{1,0:T(8,128)(2,1)S(1)}, u32[]{:S(2)}, u32[]{:S(2)}) %collective-permute-start.7) | collective-permute-done | bytes 262176 | tf_op jit(solution)/shard_map/ppermute | solution.py:1067
  227.1 3.1 collective-permute-start.11
  234.1 2.8 collective-permute-done.11
  241.4 7.2 %shard_map.144 = bf16[4,4,256,256]{3,2,1,0:T(8,128)(2,1)} custom-call(s32[1]{0:T(128)} %shard_map.143.flags, bf16[512,1024]{1,0:T(8,128)(2,1)} %copy-done.2, bf16[4,512,256]{2,1,0:T(8,128)(2,1)} %get-tuple-element.79.refs_1_, bf16[384,1024]{1,0:T(8,128)(2,1)} %bitcast.53, bf16[14,384,256]{2,1,0:T(8,128)(2,1)} %get-tuple-element.73.refs_1_.refs_3_.refs_5_.refs_9_, ...), custom_call_target="tpu_custom_call" | custom-call | flops 1000000000 | tf_op jit(solution)/shard_map/pallas_call | solution.py:102
  249.6 32.3 %shard_map.146 = (bf16[4,512,256]{2,1,0:T(8,128)(2,1)}, bf16[512,1024]{1,0:T(8,128)(2,1)}, bf16[3,512,256]{2,1,0:T(8,128)(2,1)}, f32[128,1024]{1,0:T(8,128)}, f32[2,1024]{1,0:T(2,128)}) custom-call(s32[5]{0:T(128)} %get-tuple-element.127.flags, bf16[512,1024]{1,0:T(8,128)(2,1)} %copy-done.2, f32[512,1024]{1,0:T(8,128)} %get-tuple-element.87.refs_1_, ...), custom_call_target="tpu_custom_call" | custom-call | flops 1879048192 | bytes 5111808 | tf_op jit(solution)/shard_map/pallas_call | solution.py:102
  283.0 4.7 %shard_map.145 = bf16[4,4,256,256]{3,2,1,0:T(8,128)(2,1)} custom-call(s32[1]{0:T(128)} %bitcast.flags.flag_ref, bf16[26,384,256]{2,1,0:T(8,128)(2,1)} %get-tuple-element.68.refs_0_.refs_4_.refs_2_.refs_3_.refs_8_, bf16[6,384,256]{2,1,0:T(8,128)(2,1)} %bitcast.59, ...), custom_call_target="tpu_custom_call" | custom-call | flops 1000000000 | tf_op jit(solution)/shard_map/pallas_call | solution.py:102
  291.0 6.4 %shard_map.147 = bf16[4,4,256,256]{3,2,1,0:T(8,128)(2,1)} custom-call(s32[1]{0:T(128)} %bitcast.flags.flag_ref, bf16[512,1024]{1,0:T(8,128)(2,1)} %get-tuple-element.93.refs_0_, bf16[4,512,256]{2,1,0:T(8,128)(2,1)} %get-tuple-element.94.refs_1_, bf16[26,384,256]{2,1,0:T(8,128)(2,1)} %get-tuple-element.68.refs_0_.refs_4_.refs_2_.refs_3_.refs_8_, ...), custom_call_target="tpu_custom_call" | custom-call | flops 99999997952 | tf_op jit(solution)/shard_map/pallas_call | solution.py:102
  297.7 4.5 %shard_map.148 = bf16[3,128,1024]{2,1,0:T(8,128)(2,1)} custom-call(s32[5]{0:T(128)} %get-tuple-element.126.flags, f32[384,1024]{1,0:T(8,128)} %get-tuple-element.95.refs_0_, bf16[14,384,256]{2,1,0:T(8,128)(2,1)} %get-tuple-element.73.refs_1_.refs_3_.refs_5_.refs_9_, bf16[4,384,256]{2,1,0:T(8,128)(2,1)} %get-tuple-element.75.refs_2_, ...), custom_call_target="tpu_custom_call" | custom-call | flops 402653184 | bytes 1736704 | tf_op jit(solution)/shard_map/pallas_call | solution.py:102
  302.2 9.1 %collective-permute-done.15 = bf16[3,128,1024]{2,1,0:T(8,128)(2,1)S(1)} collective-permute-done((bf16[3,128,1024]{2,1,0:T(8,128)(2,1)}, bf16[3,128,1024]{2,1,0:T(8,128)(2,1)S(1)}, u32[]{:S(2)}, u32[]{:S(2)}) %collective-permute-start.15) | collective-permute-done | bytes 786464 | tf_op jit(solution)/shard_map/ppermute | solution.py:1111
  311.3 7.5 %shard_map.149 = bf16[4,4,256,256]{3,2,1,0:T(8,128)(2,1)} custom-call(s32[1]{0:T(128)} %bitcast.flags.flag_ref, bf16[512,1024]{1,0:T(8,128)(2,1)} %multiply_convert_fusion.refs_1_.refs_0_, bf16[3,512,256]{2,1,0:T(8,128)(2,1)} %get-tuple-element.97.refs_1_, bf16[26,384,256]{2,1,0:T(8,128)(2,1)} %get-tuple-element.68.refs_0_.refs_4_.refs_2_.refs_3_.refs_8_, ...), custom_call_target="tpu_custom_call" | custom-call | flops 99999997952 | tf_op jit(solution)/shard_map/pallas_call | solution.py:102
  321.4 34.8 %psum.7 = f32[1,2,1024]{2,1,0:T(2,128)} all-reduce(f32[1,2,1024]{2,1,0:T(2,128)S(1)} %bitcast.76), channel_id=1, replica_groups=mesh['section'=2,'dp'=4,'tensor'=4] {'dp','tensor'}, use_global_device_ids=true, to_apply=%region_7.8 | all-reduce | flops 2048 | bytes 16384 | tf_op jit(solution)/shard_map/psum | solution.py:1150
  356.2 2.1 bitcast_convert_fusion
  361.1 28.8 %reduce-scatter.4.cloned.1.call-done = bf16[1,4,256,256]{3,2,1,0:T(8,128)(2,1)} async-done(((bf16[4,4,256,256]{3,2,1,0:T(8,128)(2,1)}), bf16[1,4,256,256]{3,2,1,0:T(8,128)(2,1)}) %reduce-scatter.4.cloned.1.call-update) | async-done | bytes 524304 | tf_op jit(solution)/shard_map/reduce_scatter | solution.py:998
  (105 shorter events, 40.1 us)
Async XLA Ops:
  7.2 134.2 %all-gather.3.cloned.1.call-start = ((), (), s32[]{:S(2)}) async-start(), calls=%async_computation.6 | async-start | bytes 26738688 | tf_op jit(solution)/shard_map/all_gather | solution.py:973
  10.0 346.3 %reduce-scatter.8.cloned.1.call-start = ((), (), s32[]{:S(2)}) async-start(), calls=%async_computation.5 | async-start | bytes 2621440 | tf_op jit(solution)/shard_map/reduce_scatter | solution.py:998
  10.2 9.3 %collective-permute-start.1 = (bf16[128,1024]{1,0:T(8,128)(2,1)S(1)}, bf16[128,1024]{1,0:T(8,128)(2,1)S(1)}, u32[]{:S(2)}, u32[]{:S(2)}) collective-permute-start(bf16[128,1024]{1,0:T(8,128)(2,1)S(1)} %bitcast_convert_fusion.1), channel_id=1, source_target_pairs={{0,2},{1,3},{2,0},{3,1},{4,6},{5,7},{6,4},{7,5},{8,10},{9,11},{10,... | collective-permute-start | bytes 786440 | tf_op jit(solution)/shard_map/ppermute | solution.py:909
  13.2 8.2 %collective-permute-start = (bf16[128,1024]{1,0:T(8,128)(2,1)S(1)}, bf16[128,1024]{1,0:T(8,128)(2,1)}, u32[]{:S(2)}, u32[]{:S(2)}) collective-permute-start(bf16[128,1024]{1,0:T(8,128)(2,1)S(1)} %bitcast_convert_fusion.1), channel_id=1, source_target_pairs={{0,1},{1,0},{2,3},{3,2},{4,5},{5,4},{6,7},{7,6},{8,9},{9,8},{10,11... | collective-permute-start | bytes 786440 | tf_op jit(solution)/shard_map/ppermute | solution.py:909
  19.5 2.9 collective-permute-start.2
  20.3 138.7 %copy-start.1 = (bf16[3,2,64,1024]{3,2,1,0:T(8,128)(2,1)}, bf16[3,2,64,1024]{3,2,1,0:T(8,128)(2,1)S(1)}, u32[]{:S(2)}) copy-start(bf16[3,2,64,1024]{3,2,1,0:T(8,128)(2,1)S(1)} %copy.29) | copy-start | bytes 2359300
  158.3 33.4 %collective-permute-start.5 = (bf16[384,1024]{1,0:T(8,128)(2,1)S(1)}, bf16[384,1024]{1,0:T(8,128)(2,1)S(1)}, u32[]{:S(2)}, u32[]{:S(2)}) collective-permute-start(bf16[384,1024]{1,0:T(8,128)(2,1)S(1)} %bitcast.49), channel_id=1, source_target_pairs={{16,17},{17,16},{18,19},{19,18},{20,21},{21,20},{22,23},{23,22},{2... | collective-permute-start | bytes 2359304 | tf_op jit(solution)/shard_map/ppermute | solution.py:915
  159.0 32.7 %collective-permute-start.4 = (bf16[384,1024]{1,0:T(8,128)(2,1)S(1)}, bf16[384,1024]{1,0:T(8,128)(2,1)}, u32[]{:S(2)}, u32[]{:S(2)}) collective-permute-start(bf16[384,1024]{1,0:T(8,128)(2,1)S(1)} %bitcast.50), channel_id=1, source_target_pairs={{16,18},{17,19},{18,16},{19,17},{20,22},{21,23},{22,20},{23,21},{2... | collective-permute-start | bytes 2359304 | tf_op jit(solution)/shard_map/ppermute | solution.py:915
  160.6 31.1 %collective-permute-start.3 = (bf16[128,1024]{1,0:T(8,128)(2,1)}, bf16[128,1024]{1,0:T(8,128)(2,1)S(1)}, u32[]{:S(2)}, u32[]{:S(2)}) collective-permute-start(bf16[128,1024]{1,0:T(8,128)(2,1)} %shard_map.137), channel_id=1, source_target_pairs={{0,16},{1,17},{2,18},{3,19},{4,20},{5,21},{6,22},{7,23},{8,24},{9,... | collective-permute-start | bytes 786440 | tf_op jit(solution)/shard_map/ppermute | solution.py:1043
  197.5 9.6 %collective-permute-start.6 = (bf16[26,384,256]{2,1,0:T(8,128)(2,1)}, bf16[26,384,256]{2,1,0:T(8,128)(2,1)}, u32[]{:S(2)}, u32[]{:S(2)}) collective-permute-start(bf16[26,384,256]{2,1,0:T(8,128)(2,1)} %get-tuple-element.68.refs_0_.refs_4_.refs_2_.refs_3_.refs_8_), channel_id=1, source_target_pairs={{16,17},{17,16},{18,19},{19,18},{20,21},{21,20},{22,23},{23,22},{2... | collective-permute-start | bytes 15335432 | tf_op jit(solution)/shard_map/ppermute | solution.py:915
  200.4 13.9 %collective-permute-start.8 = (bf16[4,384,256]{2,1,0:T(8,128)(2,1)}, bf16[4,384,256]{2,1,0:T(8,128)(2,1)S(1)}, u32[]{:S(2)}, u32[]{:S(2)}) collective-permute-start(bf16[4,384,256]{2,1,0:T(8,128)(2,1)} %get-tuple-element.75.refs_2_), channel_id=1, source_target_pairs={{16,18},{17,19},{18,16},{19,17},{20,22},{21,23},{22,20},{23,21},{2... | collective-permute-start | bytes 2359304 | tf_op jit(solution)/shard_map/ppermute | solution.py:915
  201.1 13.2 %collective-permute-start.9 = (bf16[4,384,256]{2,1,0:T(8,128)(2,1)}, bf16[4,384,256]{2,1,0:T(8,128)(2,1)}, u32[]{:S(2)}, u32[]{:S(2)}) collective-permute-start(bf16[4,384,256]{2,1,0:T(8,128)(2,1)} %get-tuple-element.76.refs_4_), channel_id=1, source_target_pairs={{16,19},{17,18},{18,17},{19,16},{20,23},{21,22},{22,21},{23,20},{2... | collective-permute-start | bytes 2359304 | tf_op jit(solution)/shard_map/ppermute | solution.py:915
  207.1 19.9 %collective-permute-start.7 = (bf16[128,1024]{1,0:T(8,128)(2,1)}, bf16[128,1024]{1,0:T(8,128)(2,1)S(1)}, u32[]{:S(2)}, u32[]{:S(2)}) collective-permute-start(bf16[128,1024]{1,0:T(8,128)(2,1)} %get-tuple-element.72), channel_id=1, source_target_pairs={{16,0},{17,1},{18,2},{19,3},{20,4},{21,5},{22,6},{23,7},{24,8},{25... | collective-permute-start | bytes 786440 | tf_op jit(solution)/shard_map/ppermute | solution.py:1067
  208.4 32.0 %collective-permute-start.13 = (bf16[384,1024]{1,0:T(8,128)(2,1)}, bf16[384,1024]{1,0:T(8,128)(2,1)}, u32[]{:S(2)}, u32[]{:S(2)}) collective-permute-start(bf16[384,1024]{1,0:T(8,128)(2,1)} %collective-permute-done.4.refs_6_), channel_id=1, source_target_pairs={{16,17},{17,16},{18,19},{19,18},{20,21},{21,20},{22,23},{23,22},{2... | collective-permute-start | bytes 2359304 | tf_op jit(solution)/shard_map/ppermute | solution.py:915
  214.3 15.9 %copy-start.5 = (bf16[4,4,256,256]{3,2,1,0:T(8,128)(2,1)S(1)}, bf16[4,4,256,256]{3,2,1,0:T(8,128)(2,1)}, u32[]{:S(2)}) copy-start(bf16[4,4,256,256]{3,2,1,0:T(8,128)(2,1)} %shard_map.142.refs_0_) | copy-start | bytes 6291460
  227.1 9.9 %collective-permute-start.11 = (bf16[128,1024]{1,0:T(8,128)(2,1)S(1)}, bf16[128,1024]{1,0:T(8,128)(2,1)S(1)}, u32[]{:S(2)}, u32[]{:S(2)}) collective-permute-start(bf16[128,1024]{1,0:T(8,128)(2,1)S(1)} %collective-permute-done.7), channel_id=1, source_target_pairs={{0,2},{1,3},{2,0},{3,1},{4,6},{5,7},{6,4},{7,5},{8,10},{9,11},{10,... | collective-permute-start | bytes 786440 | tf_op jit(solution)/shard_map/ppermute | solution.py:915
  230.2 60.8 %collective-permute-start.16 = (bf16[4,4,256,256]{3,2,1,0:T(8,128)(2,1)S(1)}, bf16[4,4,256,256]{3,2,1,0:T(8,128)(2,1)}, u32[]{:S(2)}, u32[]{:S(2)}) collective-permute-start(bf16[4,4,256,256]{3,2,1,0:T(8,128)(2,1)S(1)} %copy-done.5), channel_id=1, source_target_pairs={{16,18},{17,19},{18,16},{19,17},{20,22},{21,23},{22,20},{23,21},{2... | collective-permute-start | bytes 6291464 | tf_op jit(solution)/shard_map/ppermute | solution.py:915
  232.2 6.7 %collective-permute-start.10 = (bf16[128,1024]{1,0:T(8,128)(2,1)S(1)}, bf16[128,1024]{1,0:T(8,128)(2,1)S(1)}, u32[]{:S(2)}, u32[]{:S(2)}) collective-permute-start(bf16[128,1024]{1,0:T(8,128)(2,1)S(1)} %collective-permute-done.7), channel_id=1, source_target_pairs={{0,1},{1,0},{2,3},{3,2},{4,5},{5,4},{6,7},{7,6},{8,9},{9,8},{10,11... | collective-permute-start | bytes 786440 | tf_op jit(solution)/shard_map/ppermute | solution.py:915
  236.9 3.4 collective-permute-start.12
  248.6 33.4 %collective-permute-start.14 = (bf16[2,3,384,256]{3,2,1,0:T(8,128)(2,1)}, bf16[2,3,384,256]{3,2,1,0:T(8,128)(2,1)S(1)}, u32[]{:S(2)}, u32[]{:S(2)}) collective-permute-start(bf16[2,3,384,256]{3,2,1,0:T(8,128)(2,1)} %get-tuple-element.84), channel_id=1, source_target_pairs={{16,17},{17,16},{18,19},{19,18},{20,21},{21,20},{22,23},{23,22},{2... | collective-permute-start | bytes 3538952 | tf_op jit(solution)/shard_map/ppermute | solution.py:915
  249.4 108.9 %reduce-scatter.6.cloned.1.call-start = ((), (), s32[]{:S(2)}) async-start(), calls=%async_computation.4 | async-start | bytes 2621440 | tf_op jit(solution)/shard_map/reduce_scatter | solution.py:998
  287.7 23.6 %collective-permute-start.17 = (bf16[4,4,256,256]{3,2,1,0:T(8,128)(2,1)}, bf16[4,4,256,256]{3,2,1,0:T(8,128)(2,1)}, u32[]{:S(2)}, u32[]{:S(2)}) collective-permute-start(bf16[4,4,256,256]{3,2,1,0:T(8,128)(2,1)} %shard_map.145), channel_id=1, source_target_pairs={{16,18},{17,19},{18,16},{19,17},{20,22},{21,23},{22,20},{23,21},{2... | collective-permute-start | bytes 6291464 | tf_op jit(solution)/shard_map/ppermute | solution.py:915
  289.7 21.7 %collective-permute-start.15 = (bf16[3,128,1024]{2,1,0:T(8,128)(2,1)}, bf16[3,128,1024]{2,1,0:T(8,128)(2,1)S(1)}, u32[]{:S(2)}, u32[]{:S(2)}) collective-permute-start(bf16[3,128,1024]{2,1,0:T(8,128)(2,1)} %get-tuple-element.85), channel_id=1, source_target_pairs={{16,0},{17,1},{18,2},{19,3},{20,4},{21,5},{22,6},{23,7},{24,8},{25... | collective-permute-start | bytes 2359304 | tf_op jit(solution)/shard_map/ppermute | solution.py:1111
  297.4 92.5 %reduce-scatter.4.cloned.1.call-start = ((), (), s32[]{:S(2)}) async-start(), calls=%async_computation.3 | async-start | bytes 2621440 | tf_op jit(solution)/shard_map/reduce_scatter | solution.py:998
  (16 other events, 49.3 us)
Sparse Core Ops, SparseCore 0:
  10.1 131.2 all-gather.2
  249.5 49.3 reduce-scatter.7
  301.3 43.6 reduce-scatter.5
  347.1 42.7 reduce-scatter.3
